TPU v7x, 32 devices: a whole 2x2x4 slice. The times are simulated.
32 devices in a mesh: row: 16 (over z, y, core), col: 2 (over x).
Axes of the slice: x: 2, y: 2, z: 4, core: 2. Of those that a mesh axis runs over, the one named last changes fastest.
Arguments:
- inputs: bfloat16 [8192, 2048], P('row', 'col'), may hold values from -32 to 32, as said below
- segment_ids: int32 [16, 512], P('row'), may hold values from 0 to 3, never falling along the last dimension, each value on 1 to 256 neighbouring positions
- routes: int32 [8192, 6], P('row'), may hold values from 0 to 63, all different within a row; in each aligned block of 512 rows (0 to 511, 512 to 1023, ...) at most 64 rows name the same one
- norm_gain: float32 [2048], P('col'), may hold values from 0.5 to 1.5
- query_weight: bfloat16 [2048, 3072], P('row', 'col'), may hold values from -0.125 to 0.125
- latent_weight: bfloat16 [2048, 576], P('row'), may hold values from -0.125 to 0.125
- latent_gain: float32 [512], replicated, may hold values from 0.5 to 1.5
- expand_weight: bfloat16 [512, 4096], P('row', 'col'), may hold values from -0.25 to 0.25
- output_weight: bfloat16 [2048, 2048], P('col', 'row'), may hold values from -0.75 to 0.75
- ffn_gain: float32 [2048], P('col'), may hold values from 0.5 to 1.5
- router_weight: bfloat16 [2048, 64], P('row'), may hold values from -0.0625 to 0.0625
- expert_gate: bfloat16 [64, 1408, 2048], P('row', 'col'), may hold values from -0.125 to 0.125
- expert_up: bfloat16 [64, 1408, 2048], P('row', 'col'), may hold values from -0.125 to 0.125
- expert_down: bfloat16 [64, 1408, 2048], P('row', 'col'), may hold values from -6 to 6
- shared_gate: bfloat16 [2048, 2816], P('row', 'col'), may hold values from -0.125 to 0.125
- shared_up: bfloat16 [2048, 2816], P('row', 'col'), may hold values from -0.125 to 0.125
- shared_down: bfloat16 [2816, 2048], P('col', 'row'), may hold values from -0.109375 to 0.109375
- out_grad: bfloat16 [8192, 2048], P('row', 'col'), may hold values from -6 to 6
Outputs:
- output: bfloat16 [8192, 2048], P('row', 'col')
- input_grad: float32 [8192, 2048], P('row', 'col')
- norm_gain_grad: float32 [2048], P('col')
- query_weight_grad: float32 [2048, 3072], P('row', 'col')
- latent_weight_grad: float32 [2048, 576], P('row')
- latent_gain_grad: float32 [512], replicated
- expand_weight_grad: float32 [512, 4096], P('row', 'col')
- output_weight_grad: float32 [2048, 2048], P('col', 'row')
- ffn_gain_grad: float32 [2048], P('col')
- router_weight_grad: float32 [2048, 64], P('row')
- expert_gate_grad: float32 [64, 1408, 2048], P('row', 'col')
- expert_up_grad: float32 [64, 1408, 2048], P('row', 'col')
- expert_down_grad: float32 [64, 1408, 2048], P('row', 'col')
- shared_gate_grad: float32 [2048, 2816], P('row', 'col')
- shared_up_grad: float32 [2048, 2816], P('row', 'col')
- shared_down_grad: float32 [2816, 2048], P('col', 'row')
Inputs may be any that keep to these rules, and one draw needn't show every extreme that they name: `inputs`: A scale that varies by token times a scale that varies by feature times a bounded random factor. `segment_ids`: ids never fall along a sequence; every document has at most half of 512 tokens, one exactly that many. `routes`: A token's 6 experts differ. In each aligned block of 512 rows (the rows of one device) no expert is named by more than 64 rows, a bound that some block reaches.
All inputs are finite; a program needn't handle non-finite values.
Results may differ from a plain program's by a relative error of at most 0.03.
Values may be sent and summed in bfloat16 or wider, within the bound.
No kernel may reach another device: no remote copies, remote signals or barrier semaphores. Data moves between devices by JAX's collectives and lax.ppermute only.
A program may use at most 448 MiB of HBM per device.

v0:
```python
import jax
import jax.numpy as jnp
from jax import lax
from jax.sharding import PartitionSpec as P

D = 2048
NOPE = 128
ROPE = 64
RANK = 512
VDIM = 128
TOPK = 6
EXP_DEV = 4


epsilon = 1e-06
theta = 10000.0


def rotation(count, width):
    half = width // 2
    places = jnp.arange(count, dtype=jnp.float32)
    rates = theta ** (-jnp.arange(half, dtype=jnp.float32) * 2.0 / width)
    angles = places[:, None] * rates[None, :]
    return (jnp.cos(angles), jnp.sin(angles))


def rotate(values, cosine, sine):
    half = values.shape[-1] // 2
    first = values[..., :half]
    second = values[..., half:]
    return jnp.concatenate(
        [first * cosine - second * sine, second * cosine + first * sine], axis=-1
    )


def unrotate(grads, cosine, sine):
    half = grads.shape[-1] // 2
    first = grads[..., :half]
    second = grads[..., half:]
    return jnp.concatenate(
        [first * cosine + second * sine, second * cosine - first * sine], axis=-1
    )


def silu_slope(pre, sigmoid_value):
    return sigmoid_value * (1.0 + pre * (1.0 - sigmoid_value))


def col_total(values):
    return lax.psum(values, "col")


def spread(values):
    return lax.all_gather(values, "col", axis=1, tiled=True)


def mix_sums(values):
    return lax.psum_scatter(
        values.astype(jnp.bfloat16), "col", scatter_dimension=1, tiled=True
    ).astype(jnp.float32)


def send_rows(rows):
    return lax.all_to_all(rows, "row", split_axis=1, concat_axis=1, tiled=True)


def return_rows(rows):
    return lax.all_to_all(rows, "row", split_axis=1, concat_axis=1, tiled=True)


def rms_scale(rows):
    total = col_total(jnp.sum(rows * rows, axis=1))
    return lax.rsqrt(total / D + epsilon)[:, None]


def norm_backward(grads, unit, scale, gain):
    weighted = grads * gain
    average = col_total(jnp.sum(weighted * unit, axis=1)) / D
    return scale * (weighted - unit * average[:, None])


def on_device(
    inputs,
    segment_ids,
    routes,
    norm_gain,
    query_weight,
    latent_weight,
    latent_gain,
    expand_weight,
    output_weight,
    ffn_gain,
    router_weight,
    expert_gate,
    expert_up,
    expert_down,
    shared_gate,
    shared_up,
    shared_down,
    out_grad,
):
    bf16 = jnp.bfloat16
    f32 = jnp.float32
    rows_count = inputs.shape[0]
    width_share = inputs.shape[1]
    row_devices = lax.axis_size("row")
    col_devices = lax.axis_size("col")
    col_place = lax.axis_index("col")
    local_heads = query_weight.shape[1] // (NOPE + ROPE)
    expert_count = EXP_DEV * row_devices
    capacity = 4 * rows_count * TOPK // (3 * expert_count)
    score_scale = (NOPE + ROPE) ** (-0.5)
    block_rows = min(512, rows_count)
    segment_row = segment_ids[0]
    places = jnp.arange(rows_count, dtype=jnp.int32)
    (
        query_full,
        latent_full,
        expand_full,
        output_full,
        router_full,
        shared_gate_full,
        shared_up_full,
        shared_down_full,
    ) = (
        lax.all_gather(query_weight, "row", axis=0, tiled=True),
        lax.all_gather(latent_weight, "row", axis=0, tiled=True),
        lax.all_gather(expand_weight, "row", axis=0, tiled=True),
        lax.all_gather(output_weight, "row", axis=1, tiled=True),
        lax.all_gather(router_weight, "row", axis=0, tiled=True),
        lax.all_gather(shared_gate, "row", axis=0, tiled=True),
        lax.all_gather(shared_up, "row", axis=0, tiled=True),
        lax.all_gather(shared_down, "row", axis=1, tiled=True),
    )
    source = inputs.astype(f32)
    scale_one = rms_scale(source)
    unit_one = source * scale_one
    normed_one = spread((unit_one * norm_gain).astype(bf16))
    query = jnp.dot(normed_one, query_full, preferred_element_type=f32).reshape(
        rows_count, local_heads, NOPE + ROPE
    )
    latent = jnp.dot(normed_one, latent_full, preferred_element_type=f32).astype(bf16)
    cosine, sine = rotation(rows_count, ROPE)
    head_cos = cosine[:, None, :]
    head_sin = sine[:, None, :]
    compressed = latent[:, :RANK].astype(f32)
    latent_scale = lax.rsqrt(jnp.mean(compressed * compressed, axis=1, keepdims=True) + epsilon)
    latent_unit = compressed * latent_scale
    latent_normed = (latent_unit * latent_gain).astype(bf16)
    key_rope = rotate(latent[:, RANK:].astype(f32), cosine, sine).astype(bf16)
    expanded = jnp.dot(latent_normed, expand_full, preferred_element_type=f32).reshape(
        rows_count, local_heads, NOPE + VDIM
    )
    key_nope = expanded[..., :NOPE].astype(bf16)
    values_all = expanded[..., NOPE:].astype(bf16)
    query_nope = query[..., :NOPE].astype(bf16)
    query_rope = rotate(query[..., NOPE:], head_cos, head_sin).astype(bf16)

    def block_scores(start):
        ending = start + block_rows
        raw = jnp.einsum("qhd,khd->hqk", query_nope, key_nope, preferred_element_type=f32)
        raw = raw + jnp.einsum("qhd,kd->hqk", query_rope, key_rope, preferred_element_type=f32)
        allowed = (segment_row[start:ending, None] == segment_row[None, :]) & (
            places[None, :] <= places[:, None]
        )
        return jnp.where(allowed[None], raw * score_scale, -1e30)

    start = 0
    scores = block_scores(start)
    top = jnp.max(scores, axis=2, keepdims=True)
    exponent = jnp.exp(scores - top)
    total = jnp.sum(exponent, axis=2, keepdims=True)
    weights = exponent / total
    log_blocks = top + jnp.log(total)
    mixed_blocks = jnp.einsum(
        "hqk,khd->qhd", weights.astype(bf16), values_all, preferred_element_type=f32
    ).astype(bf16)
    mixed = mixed_blocks.reshape(rows_count, local_heads * VDIM)
    attended = mix_sums(jnp.dot(mixed, output_full, preferred_element_type=f32))
    middle = source + attended
    scale_two = rms_scale(middle)
    unit_two = middle * scale_two
    normed_two_share = (unit_two * ffn_gain).astype(bf16)
    normed_two = spread(normed_two_share)
    logits = jnp.dot(normed_two, router_full, preferred_element_type=f32)
    log_total = jax.nn.logsumexp(logits, axis=1, keepdims=True)
    chosen = routes[:, :, None] == jnp.arange(expert_count, dtype=jnp.int32)[None, None, :]
    picked = jnp.sum(jnp.where(chosen, logits[:, None, :], 0.0), axis=2)
    gates = jnp.exp(picked - log_total)
    upstream = out_grad.astype(f32)
    upstream_full = spread(out_grad)
    shared_gate_pre = jnp.dot(normed_two, shared_gate_full, preferred_element_type=f32)
    shared_up_pre = jnp.dot(normed_two, shared_up_full, preferred_element_type=f32)
    shared_hidden = (jax.nn.silu(shared_gate_pre) * shared_up_pre).astype(bf16)
    shared_part = jnp.dot(shared_hidden, shared_down_full, preferred_element_type=f32)
    flat_routes = routes.reshape(-1)
    hits = (flat_routes[:, None] == jnp.arange(expert_count, dtype=jnp.int32)[None, :]).astype(
        jnp.int32
    )
    ranks = jnp.sum((jnp.cumsum(hits, axis=0) - 1) * hits, axis=1)
    owners = jnp.arange(rows_count * TOPK, dtype=jnp.int32) // TOPK
    share_slots = capacity // col_devices
    slot_count = row_devices * share_slots
    buffer_size = EXP_DEV * slot_count
    inside = ranks // share_slots == col_place
    slot_place = jnp.where(
        inside,
        flat_routes % EXP_DEV * slot_count
        + flat_routes // EXP_DEV * share_slots
        + ranks
        - col_place * share_slots,
        buffer_size,
    )
    token_of_slot = (
        jnp.full((buffer_size + 1,), rows_count, jnp.int32).at[slot_place].set(owners)[:buffer_size]
    )
    gate_of_slot = (
        jnp.zeros((buffer_size + 1,), f32).at[slot_place].set(gates.reshape(-1))[:buffer_size]
    )
    position = slot_place.reshape(rows_count, TOPK)
    gate_stack, up_stack, down_stack = (
        lax.all_gather(expert_gate, "col", axis=1, tiled=True),
        lax.all_gather(expert_up, "col", axis=1, tiled=True),
        lax.all_gather(expert_down, "col", axis=1, tiled=True),
    )
    padded_rows = jnp.concatenate([normed_two, jnp.zeros((1, D), bf16)], axis=0)
    outgoing = padded_rows[token_of_slot].reshape(EXP_DEV, slot_count, D)
    arrived = send_rows(outgoing)
    gate_pre = jnp.einsum("jnd,jfd->jnf", arrived, gate_stack, preferred_element_type=f32)
    up_pre = jnp.einsum("jnd,jfd->jnf", arrived, up_stack, preferred_element_type=f32)
    hidden = (jax.nn.silu(gate_pre) * up_pre).astype(bf16)
    expert_result = jnp.einsum(
        "jnf,jfd->jnd", hidden, down_stack, preferred_element_type=f32
    ).astype(bf16)
    returned = return_rows(expert_result).reshape(buffer_size, D)
    returned = jnp.concatenate([returned, jnp.zeros((1, D), bf16)], axis=0)
    slot_values = returned[position].astype(f32)
    combined = mix_sums(jnp.sum(gates[:, :, None] * slot_values, axis=1) + shared_part)
    upstream_wide = upstream_full.astype(f32)
    gate_partial = jnp.sum(upstream_wide[:, None, :] * slot_values, axis=2)
    output = (middle + combined).astype(bf16)
    gate_grads = lax.psum(gate_partial, "col")
    chances = jnp.exp(logits - log_total)
    weighted_gates = gate_grads * gates
    logit_grads = (
        jnp.sum(jnp.where(chosen, weighted_gates[:, :, None], 0.0), axis=1)
        - chances * jnp.sum(weighted_gates, axis=1, keepdims=True)
    ).astype(bf16)
    router_rows = lax.dynamic_slice_in_dim(router_full, col_place * width_share, width_share, 0)
    router_back = jnp.einsum("te,de->td", logit_grads, router_rows, preferred_element_type=f32)
    router_grad_part = jnp.einsum("td,te->de", normed_two, logit_grads, preferred_element_type=f32)
    shared_hidden_back = jnp.einsum(
        "td,fd->tf", upstream_full, shared_down_full, preferred_element_type=f32
    )
    shared_sigmoid = jax.nn.sigmoid(shared_gate_pre)
    shared_gate_back = (
        shared_hidden_back * shared_up_pre * silu_slope(shared_gate_pre, shared_sigmoid)
    ).astype(bf16)
    shared_up_back = (shared_hidden_back * (shared_gate_pre * shared_sigmoid)).astype(bf16)
    shared_input_back = jnp.einsum(
        "tf,df->td", shared_gate_back, shared_gate_full, preferred_element_type=f32
    ) + jnp.einsum("tf,df->td", shared_up_back, shared_up_full, preferred_element_type=f32)
    shared_gate_part = jnp.einsum(
        "td,tf->df", normed_two, shared_gate_back, preferred_element_type=f32
    )
    shared_up_part = jnp.einsum("td,tf->df", normed_two, shared_up_back, preferred_element_type=f32)
    shared_down_part = jnp.einsum(
        "tf,td->fd", shared_hidden, upstream_full, preferred_element_type=f32
    )
    padded_upstream = jnp.concatenate([upstream_wide, jnp.zeros((1, D), f32)], axis=0)
    slot_grads = (
        (gate_of_slot[:, None] * padded_upstream[token_of_slot])
        .astype(bf16)
        .reshape(EXP_DEV, slot_count, D)
    )
    arrived_grads = send_rows(slot_grads)
    hidden_back = jnp.einsum("jnd,jfd->jnf", arrived_grads, down_stack, preferred_element_type=f32)
    gate_sigmoid = jax.nn.sigmoid(gate_pre)
    gate_back = (hidden_back * up_pre * silu_slope(gate_pre, gate_sigmoid)).astype(bf16)
    up_back = (hidden_back * (gate_pre * gate_sigmoid)).astype(bf16)
    row_back = jnp.einsum(
        "jnf,jfd->jnd", gate_back, gate_stack, preferred_element_type=f32
    ) + jnp.einsum("jnf,jfd->jnd", up_back, up_stack, preferred_element_type=f32)
    returned_grads = return_rows(row_back.astype(bf16)).reshape(buffer_size, D)
    returned_grads = jnp.concatenate([returned_grads, jnp.zeros((1, D), bf16)], axis=0)
    routed_back = jnp.sum(returned_grads[position].astype(f32), axis=1)
    normed_two_back = mix_sums(routed_back + shared_input_back) + router_back
    gate_pieces = []
    up_pieces = []
    down_pieces = []
    for expert in range(EXP_DEV):
        gate_piece, up_piece, down_piece = (
            lax.psum_scatter(
                jnp.einsum(
                    "nf,nd->fd", gate_back[expert], arrived[expert], preferred_element_type=f32
                ).astype(jnp.bfloat16),
                "col",
                scatter_dimension=0,
                tiled=True,
            ).astype(jnp.float32),
            lax.psum_scatter(
                jnp.einsum(
                    "nf,nd->fd", up_back[expert], arrived[expert], preferred_element_type=f32
                ).astype(jnp.bfloat16),
                "col",
                scatter_dimension=0,
                tiled=True,
            ).astype(jnp.float32),
            lax.psum_scatter(
                jnp.einsum(
                    "nf,nd->fd", hidden[expert], arrived_grads[expert], preferred_element_type=f32
                ).astype(jnp.bfloat16),
                "col",
                scatter_dimension=0,
                tiled=True,
            ).astype(jnp.float32),
        )
        gate_pieces.append(gate_piece)
        up_pieces.append(up_piece)
        down_pieces.append(down_piece)
    expert_gate_grad = jnp.stack(gate_pieces, axis=0)
    expert_up_grad = jnp.stack(up_pieces, axis=0)
    expert_down_grad = jnp.stack(down_pieces, axis=0)
    ffn_gain_part = jnp.sum(normed_two_back * unit_two, axis=0)
    middle_back = upstream + norm_backward(normed_two_back, unit_two, scale_two, ffn_gain)
    attended_back = spread(middle_back.astype(bf16))
    mixed_back = (
        jnp.einsum("td,vd->tv", attended_back, output_full, preferred_element_type=f32)
        .astype(bf16)
        .reshape(rows_count, local_heads, VDIM)
    )
    output_grad_part = jnp.einsum("tv,td->vd", mixed, attended_back, preferred_element_type=f32)
    start = 0
    ending = start + block_rows
    scores = block_scores(start)
    weights = jnp.exp(scores - log_blocks)
    weight_back = jnp.einsum("qhd,khd->hqk", mixed_back, values_all, preferred_element_type=f32)
    center = jnp.sum(weight_back * weights, axis=2, keepdims=True)
    raw_back = (weights * (weight_back - center) * score_scale).astype(bf16)
    query_nope_back = jnp.einsum("hqk,khd->qhd", raw_back, key_nope, preferred_element_type=f32)
    query_rope_back = jnp.einsum("hqk,kd->qhd", raw_back, key_rope, preferred_element_type=f32)
    key_nope_back = jnp.einsum("hqk,qhd->khd", raw_back, query_nope, preferred_element_type=f32)
    key_rope_back = jnp.einsum("hqk,qhd->kd", raw_back, query_rope, preferred_element_type=f32)
    values_back = jnp.einsum(
        "hqk,qhd->khd", weights.astype(bf16), mixed_back, preferred_element_type=f32
    )
    query_back = jnp.concatenate(
        [query_nope_back, unrotate(query_rope_back, head_cos, head_sin)], axis=2
    )
    query_back = query_back.astype(bf16).reshape(rows_count, local_heads * (NOPE + ROPE))
    expanded_back = (
        jnp.concatenate([key_nope_back, values_back], axis=2)
        .astype(bf16)
        .reshape(rows_count, local_heads * (NOPE + VDIM))
    )
    latent_normed_back = jnp.einsum(
        "tc,rc->tr", expanded_back, expand_full, preferred_element_type=f32
    )
    expand_grad_part = jnp.einsum(
        "tr,tc->rc", latent_normed, expanded_back, preferred_element_type=f32
    )
    latent_gain_part = jnp.sum(latent_normed_back * latent_unit, axis=0)
    latent_weighted = latent_normed_back * latent_gain
    compressed_back = latent_scale * (
        latent_weighted
        - latent_unit * jnp.mean(latent_weighted * latent_unit, axis=1, keepdims=True)
    )
    rope_back = unrotate(key_rope_back, cosine, sine)
    latent_back, latent_gain_col = (
        lax.psum(
            jnp.concatenate([compressed_back, rope_back], axis=1).astype(jnp.bfloat16), "col"
        ).astype(jnp.float32),
        lax.psum(latent_gain_part.astype(jnp.bfloat16), "col").astype(jnp.float32),
    )
    latent_back = latent_back.astype(bf16)
    latent_grad_part = jnp.einsum("td,tc->dc", normed_one, latent_back, preferred_element_type=f32)
    query_grad_part = jnp.einsum("td,tc->dc", normed_one, query_back, preferred_element_type=f32)
    latent_rows = lax.dynamic_slice_in_dim(latent_full, col_place * width_share, width_share, 0)
    input_part = jnp.einsum("tc,dc->td", query_back, query_full, preferred_element_type=f32)
    normed_one_back = mix_sums(input_part) + jnp.einsum(
        "tc,dc->td", latent_back, latent_rows, preferred_element_type=f32
    )
    norm_gain_part = jnp.sum(normed_one_back * unit_one, axis=0)
    input_grad = middle_back + norm_backward(normed_one_back, unit_one, scale_one, norm_gain)
    norm_gain_grad, ffn_gain_grad, latent_gain_grad = lax.psum(
        (norm_gain_part, ffn_gain_part, latent_gain_col), "row"
    )
    (
        query_grad,
        latent_grad,
        expand_grad,
        output_grad,
        router_grad,
        shared_gate_grad,
        shared_up_grad,
        shared_down_grad,
    ) = (
        lax.psum_scatter(
            query_grad_part.astype(jnp.bfloat16), "row", scatter_dimension=0, tiled=True
        ).astype(jnp.float32),
        lax.psum_scatter(
            latent_grad_part.astype(jnp.bfloat16), "row", scatter_dimension=0, tiled=True
        ).astype(jnp.float32),
        lax.psum_scatter(
            expand_grad_part.astype(jnp.bfloat16), "row", scatter_dimension=0, tiled=True
        ).astype(jnp.float32),
        lax.psum_scatter(
            output_grad_part.astype(jnp.bfloat16), "row", scatter_dimension=1, tiled=True
        ).astype(jnp.float32),
        lax.psum_scatter(
            router_grad_part.astype(jnp.bfloat16), "row", scatter_dimension=0, tiled=True
        ).astype(jnp.float32),
        lax.psum_scatter(
            shared_gate_part.astype(jnp.bfloat16), "row", scatter_dimension=0, tiled=True
        ).astype(jnp.float32),
        lax.psum_scatter(
            shared_up_part.astype(jnp.bfloat16), "row", scatter_dimension=0, tiled=True
        ).astype(jnp.float32),
        lax.psum_scatter(
            shared_down_part.astype(jnp.bfloat16), "row", scatter_dimension=1, tiled=True
        ).astype(jnp.float32),
    )
    return (
        output,
        input_grad,
        norm_gain_grad,
        query_grad,
        latent_grad,
        latent_gain_grad,
        expand_grad,
        output_grad,
        ffn_gain_grad,
        router_grad,
        expert_gate_grad,
        expert_up_grad,
        expert_down_grad,
        shared_gate_grad,
        shared_up_grad,
        shared_down_grad,
    )


def solution(mesh):
    in_specs = (
        P("row", "col"),
        P("row", None),
        P("row", None),
        P("col"),
        P("row", "col"),
        P("row", None),
        P(),
        P("row", "col"),
        P("col", "row"),
        P("col"),
        P("row", None),
        P("row", "col", None),
        P("row", "col", None),
        P("row", "col", None),
        P("row", "col"),
        P("row", "col"),
        P("col", "row"),
        P("row", "col"),
    )
    out_specs = (
        P("row", "col"),
        P("row", "col"),
        P("col"),
        P("row", "col"),
        P("row", None),
        P(),
        P("row", "col"),
        P("col", "row"),
        P("col"),
        P("row", None),
        P("row", "col", None),
        P("row", "col", None),
        P("row", "col", None),
        P("row", "col"),
        P("row", "col"),
        P("col", "row"),
    )
    return jax.shard_map(
        on_device, mesh=mesh, in_specs=in_specs, out_specs=out_specs, check_vma=False
    )
```

profile of v0, /device:TPU:0, one launch (start us, length us, event | category | flops | bytes accessed | tf_op | source)
XLA Modules:
  0.0 3629.5 jit_solution(2246811430044839044)
XLA Ops:
  21.4 31.4 all-gather.15.cloned.1.call-done
  52.8 44.9 %all-gather.17.cloned.1.call-done = bf16[2048,576]{0,1:T(8,128)(2,1)} async-done(((bf16[128,576]{0,1:T(8,128)(2,1)}), bf16[2048,576]{0,1:T(8,128)(2,1)}) %all-gather.17.cloned.1.call-update) | async-done | bytes 2359312 | tf_op jit(solution)/shard_map/all_gather | solution.py:127
  101.5 38.4 %all-gather.19.cloned.1.call-done = bf16[512,2048]{1,0:T(8,128)(2,1)} async-done(((bf16[32,2048]{1,0:T(8,128)(2,1)}), bf16[512,2048]{1,0:T(8,128)(2,1)}) %all-gather.19.cloned.1.call-update) | async-done | bytes 2097168 | tf_op jit(solution)/shard_map/all_gather | solution.py:128
  146.0 56.8 %all-gather.21.cloned.1.call-done = bf16[2048,1536]{1,0:T(8,128)(2,1)} async-done(((bf16[128,1536]{1,0:T(8,128)(2,1)}), bf16[2048,1536]{1,0:T(8,128)(2,1)}) %all-gather.21.cloned.1.call-update) | async-done | bytes 6291472 | tf_op jit(solution)/shard_map/all_gather | solution.py:126
  218.0 38.6 %all-gather.23.cloned.1.call-done = bf16[1024,2048]{1,0:T(8,128)(2,1)} async-done(((bf16[1024,128]{1,0:T(8,128)(2,1)}), bf16[1024,2048]{1,0:T(8,128)(2,1)}) %all-gather.23.cloned.1.call-update) | async-done | bytes 4194320 | tf_op jit(solution)/shard_map/all_gather | solution.py:129
  369.1 165.9 %all_gather.51 = bf16[2048,64]{0,1:T(8,128)(2,1)S(1)} all-gather(bf16[128,64]{0,1:T(8,128)(2,1)S(1)} %copy-done.63), channel_id=1, replica_groups=mesh['row'=16,'col'=2] {'row'}, dimensions={0}, use_global_device_ids=true | all-gather | bytes 278528 | tf_op jit(solution)/shard_map/all_gather | solution.py:130
  669.3 244.6 %all-gather.29.cloned.1.call-done = bf16[4,1408,2048]{2,1,0:T(8,128)(2,1)} async-done(((bf16[4,704,2048]{2,1,0:T(8,128)(2,1)}), bf16[4,1408,2048]{2,1,0:T(8,128)(2,1)}) %all-gather.29.cloned.1.call-update) | async-done | bytes 23068688 | tf_op jit(solution)/shard_map/all_gather | solution.py:223
  940.8 244.9 %all-gather.31.cloned.1.call-done = bf16[4,1408,2048]{2,1,0:T(8,128)(2,1)} async-done(((bf16[4,704,2048]{2,1,0:T(8,128)(2,1)}), bf16[4,1408,2048]{2,1,0:T(8,128)(2,1)}) %all-gather.31.cloned.1.call-update) | async-done | bytes 23068688 | tf_op jit(solution)/shard_map/all_gather | solution.py:224
  1185.7 51.2 %multiply_convert_fusion = (bf16[4,512,1408]{2,1,0:T(8,128)(2,1)}, bf16[4,512,1408]{2,1,0:T(8,128)(2,1)}, bf16[4,512,1408]{2,1,0:T(8,128)(2,1)}) fusion(f32[4,512,1408]{2,1,0:T(8,128)} %fusion.131, f32[4,512,1408]{2,1,0:T(8,128)} %fusion.129, bf16[4,1408,2048]{2,1,0:T(8,128)(2,1)} %all-gather.31.cloned.1.call-done, bf16[4,512,2048]{2,0,1:T(4,128)(2,1)} %all-to-all-done.2), kind=kOutput, calls=%fused_computation.15 | convolution fusion | flops 11854413824 | bytes 71827456 | tf_op jit(solution)/shard_map/jnd,jfd->jnf/dot_general | solution.py:277
  1337.3 151.3 %all-to-all-done.3 = bf16[4,512,2048]{2,0,1:T(4,128)(2,1)} async-done(((bf16[4,512,2048]{2,0,1:T(4,128)(2,1)}), bf16[4,512,2048]{2,0,1:T(4,128)(2,1)}, u32[]{:S(2)}, u32[]{:S(2)}) %all-to-all-start.3) | async-done | bytes 8388640 | tf_op jit(solution)/shard_map/all_to_all | solution.py:68
  1488.6 36.5 %all-to-all-start.1 = ((bf16[4,512,2048]{2,0,1:T(4,128)(2,1)}), bf16[4,512,2048]{2,0,1:T(4,128)(2,1)}, u32[]{:S(2)}, u32[]{:S(2)}) async-start(bf16[4,512,2048]{2,0,1:T(4,128)(2,1)} %copy.260), calls=%async_computation.2 | async-start | bytes 16777216 | tf_op jit(solution)/shard_map/all_to_all | solution.py:68
  1542.5 158.0 %all-gather.37.cloned.1.call-done = bf16[1408,2048]{1,0:T(8,128)(2,1)} async-done(((bf16[1408,128]{1,0:T(8,128)(2,1)}), bf16[1408,2048]{1,0:T(8,128)(2,1)}) %all-gather.37.cloned.1.call-update) | async-done | bytes 5767184 | tf_op jit(solution)/shard_map/all_gather | solution.py:133
  1938.3 38.4 %all-gather.41.cloned.1.call-done = bf16[512,2048]{1,0:T(8,128)(2,1)} async-done(((bf16[512,1024]{1,0:T(8,128)(2,1)}), bf16[512,2048]{1,0:T(8,128)(2,1)}) %all-gather.41.cloned.1.call-update) | async-done | bytes 2097168 | tf_op jit(solution)/shard_map/all_gather | solution.py:54
  2256.7 56.0 %reduce-scatter.71.cloned.1.call-done = bf16[128,1408]{1,0:T(8,128)(2,1)} async-done(((bf16[2048,1408]{1,0:T(8,128)(2,1)}), bf16[128,1408]{1,0:T(8,128)(2,1)}) %reduce-scatter.71.cloned.1.call-update) | async-done | bytes 360464 | tf_op jit(solution)/shard_map/reduce_scatter | solution.py:416
  2314.6 71.6 %reduce-scatter.51.cloned.1.call-done = bf16[704,2048]{1,0:T(8,128)(2,1)} async-done(((bf16[1408,2048]{1,0:T(8,128)(2,1)}), bf16[704,2048]{1,0:T(8,128)(2,1)}) %reduce-scatter.51.cloned.1.call-update) | async-done | bytes 2883600 | tf_op jit(solution)/shard_map/reduce_scatter | solution.py:293
  2386.2 73.7 %reduce-scatter.49.cloned.1.call-done = bf16[704,2048]{1,0:T(8,128)(2,1)} async-done(((bf16[1408,2048]{1,0:T(8,128)(2,1)}), bf16[704,2048]{1,0:T(8,128)(2,1)}) %reduce-scatter.49.cloned.1.call-update) | async-done | bytes 2883600 | tf_op jit(solution)/shard_map/reduce_scatter | solution.py:293
  2459.9 73.8 %reduce-scatter.47.cloned.1.call-done = bf16[704,2048]{1,0:T(8,128)(2,1)} async-done(((bf16[1408,2048]{1,0:T(8,128)(2,1)}), bf16[704,2048]{1,0:T(8,128)(2,1)}) %reduce-scatter.47.cloned.1.call-update) | async-done | bytes 2883600 | tf_op jit(solution)/shard_map/reduce_scatter | solution.py:293
  2533.8 73.5 %reduce-scatter.45.cloned.1.call-done = bf16[704,2048]{1,0:T(8,128)(2,1)} async-done(((bf16[1408,2048]{1,0:T(8,128)(2,1)}), bf16[704,2048]{1,0:T(8,128)(2,1)}) %reduce-scatter.45.cloned.1.call-update) | async-done | bytes 2883600 | tf_op jit(solution)/shard_map/reduce_scatter | solution.py:293
  2620.4 60.7 %reduce-scatter.59.cloned.1.call-done = bf16[704,2048]{1,0:T(8,128)(2,1)} async-done(((bf16[1408,2048]{1,0:T(8,128)(2,1)}), bf16[704,2048]{1,0:T(8,128)(2,1)}) %reduce-scatter.59.cloned.1.call-update) | async-done | bytes 2883600 | tf_op jit(solution)/shard_map/reduce_scatter | solution.py:301
  2681.1 73.5 %reduce-scatter.57.cloned.1.call-done = bf16[704,2048]{1,0:T(8,128)(2,1)} async-done(((bf16[1408,2048]{1,0:T(8,128)(2,1)}), bf16[704,2048]{1,0:T(8,128)(2,1)}) %reduce-scatter.57.cloned.1.call-update) | async-done | bytes 2883600 | tf_op jit(solution)/shard_map/reduce_scatter | solution.py:301
  2754.7 73.7 %reduce-scatter.55.cloned.1.call-done = bf16[704,2048]{1,0:T(8,128)(2,1)} async-done(((bf16[1408,2048]{1,0:T(8,128)(2,1)}), bf16[704,2048]{1,0:T(8,128)(2,1)}) %reduce-scatter.55.cloned.1.call-update) | async-done | bytes 2883600 | tf_op jit(solution)/shard_map/reduce_scatter | solution.py:301
  2828.4 73.7 %reduce-scatter.53.cloned.1.call-done = bf16[704,2048]{1,0:T(8,128)(2,1)} async-done(((bf16[1408,2048]{1,0:T(8,128)(2,1)}), bf16[704,2048]{1,0:T(8,128)(2,1)}) %reduce-scatter.53.cloned.1.call-update) | async-done | bytes 2883600 | tf_op jit(solution)/shard_map/reduce_scatter | solution.py:301
  2915.2 60.7 %reduce-scatter.67.cloned.1.call-done = bf16[704,2048]{1,0:T(8,128)(2,1)} async-done(((bf16[1408,2048]{1,0:T(8,128)(2,1)}), bf16[704,2048]{1,0:T(8,128)(2,1)}) %reduce-scatter.67.cloned.1.call-update) | async-done | bytes 2883600 | tf_op jit(solution)/shard_map/reduce_scatter | solution.py:309
  2975.9 73.5 %reduce-scatter.65.cloned.1.call-done = bf16[704,2048]{1,0:T(8,128)(2,1)} async-done(((bf16[1408,2048]{1,0:T(8,128)(2,1)}), bf16[704,2048]{1,0:T(8,128)(2,1)}) %reduce-scatter.65.cloned.1.call-update) | async-done | bytes 2883600 | tf_op jit(solution)/shard_map/reduce_scatter | solution.py:309
  3049.4 73.8 %reduce-scatter.63.cloned.1.call-done = bf16[704,2048]{1,0:T(8,128)(2,1)} async-done(((bf16[1408,2048]{1,0:T(8,128)(2,1)}), bf16[704,2048]{1,0:T(8,128)(2,1)}) %reduce-scatter.63.cloned.1.call-update) | async-done | bytes 2883600 | tf_op jit(solution)/shard_map/reduce_scatter | solution.py:309
  3123.3 73.7 %reduce-scatter.61.cloned.1.call-done = bf16[704,2048]{1,0:T(8,128)(2,1)} async-done(((bf16[1408,2048]{1,0:T(8,128)(2,1)}), bf16[704,2048]{1,0:T(8,128)(2,1)}) %reduce-scatter.61.cloned.1.call-update) | async-done | bytes 2883600 | tf_op jit(solution)/shard_map/reduce_scatter | solution.py:309
  3210.1 47.0 %reduce-scatter.77.cloned.1.call-done = bf16[128,64]{1,0:T(8,128)(2,1)} async-done(((bf16[2048,64]{1,0:T(8,128)(2,1)}), bf16[128,64]{1,0:T(8,128)(2,1)}) %reduce-scatter.77.cloned.1.call-update) | async-done | bytes 16400
  3263.5 58.0 %reduce-scatter.43.cloned.1.call-done = bf16[32,2048]{1,0:T(8,128)(2,1)} async-done(((bf16[512,2048]{1,0:T(8,128)(2,1)}), bf16[32,2048]{1,0:T(8,128)(2,1)}) %reduce-scatter.43.cloned.1.call-update) | async-done | bytes 131088 | tf_op jit(solution)/shard_map/reduce_scatter | solution.py:404
  3323.2 65.5 %reduce-scatter.73.cloned.1.call-done = bf16[128,576]{1,0:T(8,128)(2,1)} async-done(((bf16[2048,576]{1,0:T(8,128)(2,1)}), bf16[128,576]{1,0:T(8,128)(2,1)}) %reduce-scatter.73.cloned.1.call-update) | async-done | bytes 147472
  3431.1 60.0 %all-reduce.4 = (f32[1024]{0:T(1024)}, f32[512]{0:T(512)}, f32[1024]{0:T(1024)}) all-reduce(f32[1024]{0:T(1024)S(1)} %get-tuple-element.20, bf16[512]{0:T(512)(128)(2,1)S(1)} %psum.77, f32[1024]{0:T(1024)S(1)} %copy-done.66), channel_id=1, replica_groups=mesh['row'=16,'col'=2] {'row'}, use_global_device_ids=true, to_apply=%region_33.34 | all-reduce | flops 2560 | bytes 19456 | tf_op jit(solution)/shard_map/psum | solution.py:385
  3495.7 36.8 %reduce-scatter.75.cloned.1.call-done = bf16[128,1024]{1,0:T(8,128)(2,1)} async-done(((bf16[2048,1024]{1,0:T(8,128)(2,1)}), bf16[128,1024]{1,0:T(8,128)(2,1)}) %reduce-scatter.75.cloned.1.call-update) | async-done | bytes 262160
  3534.4 86.1 %reduce-scatter.41.cloned.1.call-done = bf16[128,1536]{1,0:T(8,128)(2,1)} async-done(((bf16[2048,1536]{1,0:T(8,128)(2,1)}), bf16[128,1536]{1,0:T(8,128)(2,1)}) %reduce-scatter.41.cloned.1.call-update) | async-done | bytes 393232 | tf_op jit(solution)/shard_map/reduce_scatter | solution.py:398
  (408 shorter events, 1047.0 us)
Async XLA Ops:
  19.8 236.8 %all-gather.23.cloned.1.call-start = ((), (), s32[]{:S(2)}) async-start(), calls=%async_computation.32 | async-start | bytes 4456448 | tf_op jit(solution)/shard_map/all_gather | solution.py:129
  20.3 272.4 %reduce-scatter.33.cloned.1.call-start = ((), (), s32[]{:S(2)}) async-start(), calls=%async_computation.33 | async-start | bytes 3145728 | tf_op jit(solution)/shard_map/reduce_scatter | solution.py:58
  302.5 232.5 %all-gather.39.cloned.1.call-start = ((), (), s32[]{:S(2)}) async-start(), calls=%async_computation.42 | async-start | bytes 3145728 | tf_op jit(solution)/shard_map/all_gather | solution.py:54
  303.2 339.1 %all-gather.27.cloned.1.call-start = ((), (), s32[]{:S(2)}) async-start(), calls=%async_computation.35 | async-start | bytes 34603008 | tf_op jit(solution)/shard_map/all_gather | solution.py:222
  304.0 609.9 %all-gather.29.cloned.1.call-start = ((), (), s32[]{:S(2)}) async-start(), calls=%async_computation.36 | async-start | bytes 34603008 | tf_op jit(solution)/shard_map/all_gather | solution.py:223
  368.4 817.3 %all-gather.31.cloned.1.call-start = ((), (), s32[]{:S(2)}) async-start(), calls=%async_computation.37 | async-start | bytes 34603008 | tf_op jit(solution)/shard_map/all_gather | solution.py:224
  593.0 592.7 %all-to-all-start.2 = ((bf16[4,512,2048]{2,0,1:T(4,128)(2,1)}), bf16[4,512,2048]{2,0,1:T(4,128)(2,1)}, u32[]{:S(2)}, u32[]{:S(2)}) async-start(bf16[4,512,2048]{2,0,1:T(4,128)(2,1)} %fusion.1), calls=%async_computation.4 | async-start | bytes 16777216 | tf_op jit(solution)/shard_map/all_to_all | solution.py:64
  623.9 903.1 %all-gather.33.cloned.1.call-start = ((), (), s32[]{:S(2)}) async-start(), calls=%async_computation.38 | async-start | bytes 6127616 | tf_op jit(solution)/shard_map/all_gather | solution.py:131
  1303.1 231.6 %all-gather.35.cloned.1.call-start = ((), (), s32[]{:S(2)}) async-start(), calls=%async_computation.39 | async-start | bytes 6127616 | tf_op jit(solution)/shard_map/all_gather | solution.py:132
  1488.6 330.8 %all-to-all-start.1 = ((bf16[4,512,2048]{2,0,1:T(4,128)(2,1)}), bf16[4,512,2048]{2,0,1:T(4,128)(2,1)}, u32[]{:S(2)}, u32[]{:S(2)}) async-start(bf16[4,512,2048]{2,0,1:T(4,128)(2,1)} %copy.260), calls=%async_computation.2 | async-start | bytes 16777216 | tf_op jit(solution)/shard_map/all_to_all | solution.py:68
  1525.6 400.2 %reduce-scatter.37.cloned.1.call-start = ((), (), s32[]{:S(2)}) async-start(), calls=%async_computation.43 | async-start | bytes 3145728 | tf_op jit(solution)/shard_map/reduce_scatter | solution.py:58
  1938.2 243.3 %all-reduce.7.cloned.1.call-start = ((), (), s32[]{:S(2)}) async-start(), calls=%async_computation.46 | async-start | bytes 1179648 | tf_op jit(solution)/shard_map/psum | solution.py:370
  2049.6 263.1 %reduce-scatter.71.cloned.1.call-start = ((), (), s32[]{:S(2)}) async-start(), calls=%async_computation.62 | async-start | bytes 6127616 | tf_op jit(solution)/shard_map/reduce_scatter | solution.py:416
  2056.4 329.8 %reduce-scatter.51.cloned.1.call-start = ((), (), s32[]{:S(2)}) async-start(), calls=%async_computation.52 | async-start | bytes 8650752 | tf_op jit(solution)/shard_map/reduce_scatter | solution.py:293
  2075.9 384.0 %reduce-scatter.49.cloned.1.call-start = ((), (), s32[]{:S(2)}) async-start(), calls=%async_computation.51 | async-start | bytes 8650752 | tf_op jit(solution)/shard_map/reduce_scatter | solution.py:293
  2084.3 449.4 %reduce-scatter.47.cloned.1.call-start = ((), (), s32[]{:S(2)}) async-start(), calls=%async_computation.50 | async-start | bytes 8650752 | tf_op jit(solution)/shard_map/reduce_scatter | solution.py:293
  2092.3 515.0 %reduce-scatter.45.cloned.1.call-start = ((), (), s32[]{:S(2)}) async-start(), calls=%async_computation.49 | async-start | bytes 8650752 | tf_op jit(solution)/shard_map/reduce_scatter | solution.py:293
  2100.1 581.1 %reduce-scatter.59.cloned.1.call-start = ((), (), s32[]{:S(2)}) async-start(), calls=%async_computation.56 | async-start | bytes 8650752 | tf_op jit(solution)/shard_map/reduce_scatter | solution.py:301
  2107.8 646.9 %reduce-scatter.57.cloned.1.call-start = ((), (), s32[]{:S(2)}) async-start(), calls=%async_computation.55 | async-start | bytes 8650752 | tf_op jit(solution)/shard_map/reduce_scatter | solution.py:301
  2115.8 712.6 %reduce-scatter.55.cloned.1.call-start = ((), (), s32[]{:S(2)}) async-start(), calls=%async_computation.54 | async-start | bytes 8650752 | tf_op jit(solution)/shard_map/reduce_scatter | solution.py:301
  2123.5 778.5 %reduce-scatter.53.cloned.1.call-start = ((), (), s32[]{:S(2)}) async-start(), calls=%async_computation.53 | async-start | bytes 8650752 | tf_op jit(solution)/shard_map/reduce_scatter | solution.py:301
  2131.3 844.7 %reduce-scatter.67.cloned.1.call-start = ((), (), s32[]{:S(2)}) async-start(), calls=%async_computation.60 | async-start | bytes 8650752 | tf_op jit(solution)/shard_map/reduce_scatter | solution.py:309
  2150.7 898.8 %reduce-scatter.65.cloned.1.call-start = ((), (), s32[]{:S(2)}) async-start(), calls=%async_computation.59 | async-start | bytes 8650752 | tf_op jit(solution)/shard_map/reduce_scatter | solution.py:309
  2158.6 964.7 %reduce-scatter.63.cloned.1.call-start = ((), (), s32[]{:S(2)}) async-start(), calls=%async_computation.58 | async-start | bytes 8650752 | tf_op jit(solution)/shard_map/reduce_scatter | solution.py:309
  2167.0 1030.0 %reduce-scatter.61.cloned.1.call-start = ((), (), s32[]{:S(2)}) async-start(), calls=%async_computation.57 | async-start | bytes 8650752 | tf_op jit(solution)/shard_map/reduce_scatter | solution.py:309
  2174.8 1082.4 %reduce-scatter.77.cloned.1.call-start = ((), (), s32[]{:S(2)}) async-start(), calls=%async_computation.65 | async-start | bytes 557056
  2177.1 1144.4 %reduce-scatter.43.cloned.1.call-start = ((), (), s32[]{:S(2)}) async-start(), calls=%async_computation.48 | async-start | bytes 2228224 | tf_op jit(solution)/shard_map/reduce_scatter | solution.py:404
  2181.4 1207.2 %reduce-scatter.73.cloned.1.call-start = ((), (), s32[]{:S(2)}) async-start(), calls=%async_computation.63 | async-start | bytes 2785280
  2187.3 1234.4 %reduce-scatter.39.cloned.1.call-start = ((), (), s32[]{:S(2)}) async-start(), calls=%async_computation.45 | async-start | bytes 3145728 | tf_op jit(solution)/shard_map/reduce_scatter | solution.py:58
  2223.2 1267.9 %reduce-scatter.35.cloned.1.call-start = ((), (), s32[]{:S(2)}) async-start(), calls=%async_computation.41 | async-start | bytes 3145728 | tf_op jit(solution)/shard_map/reduce_scatter | solution.py:58
  2232.5 1300.0 %reduce-scatter.75.cloned.1.call-start = ((), (), s32[]{:S(2)}) async-start(), calls=%async_computation.64 | async-start | bytes 4456448
  2245.3 1375.2 %reduce-scatter.41.cloned.1.call-start = ((), (), s32[]{:S(2)}) async-start(), calls=%async_computation.47 | async-start | bytes 6684672 | tf_op jit(solution)/shard_map/reduce_scatter | solution.py:398
  (87 other events, 5065.8 us)
Sparse Core Ops, SparseCore 0:
  54.9 42.6 all-gather.16
  99.8 40.1 all-gather.18
  142.1 60.6 all-gather.20
  204.8 51.8 all-gather.22
  372.1 270.0 all-gather.26
  643.8 270.0 all-gather.28
  915.5 270.0 all-gather.30
  1188.0 59.0 all-gather.32
  1306.5 161.6 all-gather.34
  1528.0 172.5 all-gather.36
  1817.0 38.9 reduce-scatter.36
  1938.3 38.3 all-gather.40
  2060.9 81.5 reduce-scatter.78
  2146.9 80.7 reduce-scatter.68
  2231.9 80.7 reduce-scatter.70
  2315.7 70.4 reduce-scatter.50
  2388.5 71.3 reduce-scatter.48
  2462.4 71.3 reduce-scatter.46
  2535.9 71.3 reduce-scatter.44
  2609.7 71.3 reduce-scatter.58
  2683.3 71.3 reduce-scatter.56
  2756.9 71.3 reduce-scatter.54
  2830.7 71.3 reduce-scatter.52
  2904.5 71.3 reduce-scatter.66
  2978.1 71.3 reduce-scatter.64
  3051.9 71.3 reduce-scatter.62
  3125.6 71.3 reduce-scatter.60
  3201.4 55.7 reduce-scatter.76
  3260.9 60.6 reduce-scatter.42
  3325.8 62.8 reduce-scatter.72
  3460.0 72.4 reduce-scatter.74
  3536.3 84.1 reduce-scatter.40
  (7 shorter events, 223.4 us)
where the time goes:
time: 3640 us; the launch traced here: 3630 us
  waiting for transfers between devices  2340 us (64%)
  matrix products  478 us (13%)
  local copies, waits for them, and re-layouts  296 us (8%)
  blocking collectives  262 us (7%)
  other arithmetic  156 us (4%)
  starting transfers between devices  82.8 us (2%)
    reduce_scatter x4, waiting for transfers between devices, on_device(): lax.psum_scatter(jnp.einsum('nf,nd->fd', gate_back[expert], arrived[exper...  293 us
    reduce_scatter x4, waiting for transfers between devices, on_device(): lax.psum_scatter(jnp.einsum('nf,nd->fd', hidden[expert], arrived_grads[ex...  282 us
    reduce_scatter x4, waiting for transfers between devices, on_device(): lax.psum_scatter(jnp.einsum('nf,nd->fd', up_back[expert], arrived[expert]...  282 us
    all_gather x1, waiting for transfers between devices, on_device(): lax.all_gather(expert_down, 'col', axis=1, tiled=True)  245 us
    all_gather x1, waiting for transfers between devices, on_device(): lax.all_gather(expert_up, 'col', axis=1, tiled=True)  245 us
    all_gather x1, blocking collectives, on_device(): lax.all_gather(router_weight, 'row', axis=0, tiled=True)  166 us
    all_gather x1, waiting for transfers between devices, on_device(): lax.all_gather(shared_down, 'row', axis=1, tiled=True)  158 us
    unnamed x43, waiting for transfers between devices  156 us
  transfers between devices with their start and end apart: 43, of which 31 were waited for; matrix products, arithmetic and copies ran while one was open for 23% of the time, Pallas kernels for 0%

commit v1 on v0

--- a/solution.py
+++ b/solution.py
@@ -1,6 +1,8 @@
 import jax
 import jax.numpy as jnp
 from jax import lax
+from jax.experimental import pallas as pl
+from jax.experimental.pallas import tpu as pltpu
 from jax.sharding import PartitionSpec as P
 
 D = 2048
@@ -79,7 +81,812 @@
     return scale * (weighted - unit * average[:, None])
 
 
+PLANES = 4
+COMMON = 192
+UNIQUE = 160
+SENT = COMMON + UNIQUE
+SHARED_PAD = 128
+
+
+def swap_cols(values):
+    return lax.ppermute(values, "col", [(0, 1), (1, 0)])
+
+
+def swap_rows(values, bit):
+    return lax.ppermute(values, "row", [(i, i ^ bit) for i in range(16)])
+
+
+def turn_planes(values):
+    return lax.ppermute(values, "row", [(i, (i + 4) % 16) for i in range(16)])
+
+
+def join_cols(values, first):
+    other = swap_cols(values)
+    return jnp.where(
+        first,
+        jnp.concatenate([values, other], axis=1),
+        jnp.concatenate([other, values], axis=1),
+    )
+
+
+def own_columns(values, first):
+    half = values.shape[-1] // 2
+    return jnp.where(first, values[..., :half], values[..., half:])
+
+
+def other_columns(values, first):
+    half = values.shape[-1] // 2
+    return jnp.where(first, values[..., half:], values[..., :half])
+
+
+def sent_rows(values, first):
+    return jnp.concatenate(
+        [values[:COMMON], jnp.where(first, values[COMMON:SENT], values[SENT:])], axis=0
+    )
+
+
+def local_tokens(values, axis, first):
+    common = lax.slice_in_dim(values, 0, COMMON, axis=axis)
+    one = lax.slice_in_dim(values, COMMON, SENT, axis=axis)
+    two = lax.slice_in_dim(values, SENT, SENT + UNIQUE, axis=axis)
+    return jnp.concatenate(
+        [common, jnp.where(first, one, two), jnp.where(first, two, one)], axis=axis
+    )
+
+
+def spread_rows(rows):
+    planes = []
+    current = rows
+    for plane in range(PLANES):
+        if plane > 0:
+            current = turn_planes(current)
+        across = swap_rows(current, 2)
+        held = [
+            (current, swap_cols(current[COMMON:])),
+            (across, swap_cols(across[COMMON:])),
+        ]
+        family = []
+        for sent, unique in held:
+            family.append((sent, unique))
+            family.append((swap_rows(sent, 1), swap_rows(unique, 1)))
+        planes.append(family)
+    return planes
+
+
+def collect_rows(planes):
+    moving = None
+    for plane in (1, 2, 3, 0):
+        sibling, mine = planes[plane]
+        total = mine + swap_rows(sibling, 1)
+        unique = swap_cols(total[:, SENT:])
+        total = jnp.concatenate([total[:, :COMMON], total[:, COMMON:SENT] + unique], axis=1)
+        total = total[0] + swap_rows(total[1], 2)
+        if moving is not None:
+            total = total + turn_planes(moving)
+        moving = total
+    return moving
+
+
+def merge_rows(own, received, first):
+    own = own.astype(jnp.float32)
+    received = received.astype(jnp.float32)
+    common = own[:COMMON] + received[:COMMON]
+    mine = own[COMMON:]
+    theirs = received[COMMON:]
+    return jnp.concatenate(
+        [common, jnp.where(first, mine, theirs), jnp.where(first, theirs, mine)], axis=0
+    )
+
+
+FAMILIES = 4
+VMEM_BYTES = 60 * 1024 * 1024
+
+
+def kernel_params(**extra):
+    return pltpu.CompilerParams(vmem_limit_bytes=VMEM_BYTES, **extra)
+
+
+def dot_last(left, right):
+    return lax.dot_general(
+        left, right, (((1,), (1,)), ((), ())), preferred_element_type=jnp.float32
+    )
+
+
+def dot_first(left, right):
+    return lax.dot_general(
+        left, right, (((0,), (0,)), ((), ())), preferred_element_type=jnp.float32
+    )
+
+
+def dot_plain(left, right):
+    return jnp.dot(left, right, preferred_element_type=jnp.float32)
+
+
+def slot_matches(codes_ref, capacity):
+    tokens = codes_ref.shape[-1]
+    ranks = lax.broadcasted_iota(jnp.int32, (capacity, tokens), 0)
+    return [codes_ref[0, j : j + 1, :] == ranks for j in range(EXP_DEV)]
+
+
+def as_picks(matches):
+    one = [jnp.where(m, 1.0, 0.0).astype(jnp.bfloat16) for m in matches]
+    return jnp.concatenate(one, axis=0)
+
+
+def start_rows(pieces, held, sems):
+    for f in range(FAMILIES):
+        pltpu.make_async_copy(pieces[2 * f], held.at[f, pl.ds(0, SENT)], sems.at[f, 0]).start()
+        pltpu.make_async_copy(
+            pieces[2 * f + 1], held.at[f, pl.ds(SENT, UNIQUE)], sems.at[f, 1]
+        ).start()
+
+
+def wait_rows(pieces, held, sems, f):
+    pltpu.make_async_copy(pieces[0], held.at[f, pl.ds(0, SENT)], sems.at[f, 0]).wait()
+    pltpu.make_async_copy(pieces[1], held.at[f, pl.ds(SENT, UNIQUE)], sems.at[f, 1]).wait()
+
+
+def pick_grads(plane, codes, last, capacity):
+    pieces = [piece for family in plane for piece in family]
+    tokens = SENT + UNIQUE
+    width = last.shape[1]
+    pad = last.shape[0]
+
+    def body(*refs):
+        rows_in = refs[:8]
+        codes_ref, last_ref, slots_ref, hidden_ref, held, sems = refs[8:]
+        f = pl.program_id(0)
+
+        @pl.when(f == 0)
+        def _():
+            start_rows(rows_in, held, sems)
+
+        wait_rows(rows_in, held, sems, f)
+        rows = held[f]
+        picks = as_picks(slot_matches(codes_ref, capacity))
+        taken = dot_plain(picks, rows).astype(jnp.bfloat16)
+        slots_ref[...] = taken.reshape(EXP_DEV, capacity, width)
+        hidden_ref[0] = dot_last(rows, last_ref[...])
+
+    return pl.pallas_call(
+        body,
+        grid=(FAMILIES,),
+        in_specs=[pl.BlockSpec(memory_space=pl.ANY)] * 8
+        + [
+            pl.BlockSpec((1, 8, tokens), lambda f: (f, 0, 0)),
+            pl.BlockSpec((pad, width), lambda f: (0, 0)),
+        ],
+        out_specs=[
+            pl.BlockSpec((EXP_DEV, capacity, width), lambda f: (0, f, 0)),
+            pl.BlockSpec((1, tokens, pad), lambda f: (f, 0, 0)),
+        ],
+        out_shape=[
+            jax.ShapeDtypeStruct((EXP_DEV, FAMILIES * capacity, width), jnp.bfloat16),
+            jax.ShapeDtypeStruct((FAMILIES, tokens, pad), jnp.float32),
+        ],
+        scratch_shapes=[
+            pltpu.VMEM((FAMILIES, tokens, width), jnp.bfloat16),
+            pltpu.SemaphoreType.DMA((FAMILIES, 2)),
+        ],
+        compiler_params=kernel_params(),
+        cost_estimate=pl.CostEstimate(
+            flops=FAMILIES * 2 * tokens * width * (EXP_DEV * capacity + 2 * pad),
+            bytes_accessed=FAMILIES * tokens * width * 4,
+            transcendentals=0,
+        ),
+    )(*pieces, codes, last)
+
+
+def pick_rows(plane, grad_plane, codes, router, pair, hidden_grads, capacity):
+    pieces = [piece for family in plane for piece in family]
+    grad_pieces = [piece for family in grad_plane for piece in family]
+    tokens = SENT + UNIQUE
+    width = pair.shape[1]
+    pad = pair.shape[0] // 2
+
+    def body(*refs):
+        rows_in = refs[:8]
+        grads_in = refs[8:16]
+        (codes_ref, router_ref, pair_ref, hidden_grads_ref) = refs[16:20]
+        (slots_ref, gates_ref, hidden_ref, back_ref, grad_ref) = refs[20:25]
+        held, held_grads, sems, grad_sems = refs[25:]
+        f = pl.program_id(0)
+
+        @pl.when(f == 0)
+        def _():
+            start_rows(rows_in, held, sems)
+            start_rows(grads_in, held_grads, grad_sems)
+            grad_ref[...] = jnp.zeros_like(grad_ref)
+
+        wait_rows(rows_in, held, sems, f)
+        rows = held[f]
+        matches = slot_matches(codes_ref, capacity)
+        taken = dot_plain(as_picks(matches), rows).astype(jnp.bfloat16)
+        slots_ref[...] = taken.reshape(EXP_DEV, capacity, width)
+        logits = dot_last(router_ref[...], rows)
+        top = jnp.max(logits, axis=0, keepdims=True)
+        total = jnp.log(jnp.sum(jnp.exp(logits - top), axis=0, keepdims=True)) + top
+        for j in range(EXP_DEV):
+            chance = jnp.exp(logits[j : j + 1] - total)
+            gate = jnp.sum(jnp.where(matches[j], chance, 0.0), axis=1, keepdims=True)
+            gates_ref[j] = jnp.broadcast_to(gate, (capacity, 128))
+        pre = dot_last(rows, pair_ref[...])
+        gate_pre = pre[:, :pad]
+        up_pre = pre[:, pad:]
+        hidden_back = hidden_grads_ref[0]
+        sigmoid_value = jax.nn.sigmoid(gate_pre)
+        silu_value = gate_pre * sigmoid_value
+        hidden = (silu_value * up_pre).astype(jnp.bfloat16)
+        slope = sigmoid_value * (1.0 + gate_pre * (1.0 - sigmoid_value))
+        gate_back = (hidden_back * up_pre * slope).astype(jnp.bfloat16)
+        up_back = (hidden_back * silu_value).astype(jnp.bfloat16)
+        back = jnp.concatenate([gate_back, up_back], axis=1)
+        hidden_ref[0] = hidden
+        back_ref[0] = back
+        grad_ref[: 2 * pad] += dot_first(back, rows)
+        wait_rows(grads_in, held_grads, grad_sems, f)
+        grad_ref[2 * pad :] += dot_first(hidden, held_grads[f])
+
+    return pl.pallas_call(
+        body,
+        grid=(FAMILIES,),
+        in_specs=[pl.BlockSpec(memory_space=pl.ANY)] * 16
+        + [
+            pl.BlockSpec((1, 8, tokens), lambda f: (f, 0, 0)),
+            pl.BlockSpec(router.shape, lambda f: (0, 0)),
+            pl.BlockSpec(pair.shape, lambda f: (0, 0)),
+            pl.BlockSpec((1, tokens, pad), lambda f: (f, 0, 0)),
+        ],
+        out_specs=[
+            pl.BlockSpec((EXP_DEV, capacity, width), lambda f: (0, f, 0)),
+            pl.BlockSpec((EXP_DEV, capacity, 128), lambda f: (0, f, 0)),
+            pl.BlockSpec((1, tokens, pad), lambda f: (f, 0, 0)),
+            pl.BlockSpec((1, tokens, 2 * pad), lambda f: (f, 0, 0)),
+            pl.BlockSpec((3 * pad, width), lambda f: (0, 0)),
+        ],
+        out_shape=[
+            jax.ShapeDtypeStruct((EXP_DEV, FAMILIES * capacity, width), jnp.bfloat16),
+            jax.ShapeDtypeStruct((EXP_DEV, FAMILIES * capacity, 128), jnp.float32),
+            jax.ShapeDtypeStruct((FAMILIES, tokens, pad), jnp.bfloat16),
+            jax.ShapeDtypeStruct((FAMILIES, tokens, 2 * pad), jnp.bfloat16),
+            jax.ShapeDtypeStruct((3 * pad, width), jnp.float32),
+        ],
+        scratch_shapes=[
+            pltpu.VMEM((FAMILIES, tokens, width), jnp.bfloat16),
+            pltpu.VMEM((FAMILIES, tokens, width), jnp.bfloat16),
+            pltpu.SemaphoreType.DMA((FAMILIES, 2)),
+            pltpu.SemaphoreType.DMA((FAMILIES, 2)),
+        ],
+        compiler_params=kernel_params(),
+        cost_estimate=pl.CostEstimate(
+            flops=FAMILIES * 2 * tokens * width * (EXP_DEV * capacity + 7 * pad),
+            bytes_accessed=FAMILIES * tokens * width * 6,
+            transcendentals=FAMILIES * tokens * 4 * pad,
+        ),
+    )(*pieces, *grad_pieces, codes, router, pair, hidden_grads)
+
+
+def run_experts(slot_rows, slot_grads, gates, expert_gate, expert_up, expert_down):
+    count, slots, width = slot_rows.shape
+    units = expert_gate.shape[1]
+
+    def body(
+        rows_ref,
+        grads_ref,
+        gates_ref,
+        gate_ref,
+        up_ref,
+        down_ref,
+        sum_ref,
+        back_ref,
+        hidden_ref,
+        gate_back_ref,
+        up_back_ref,
+        gate_grad_ref,
+    ):
+        rows = rows_ref[0]
+        gates_here = gates_ref[0][:, :1]
+        gate_pre = dot_last(rows, gate_ref[0])
+        up_pre = dot_last(rows, up_ref[0])
+        down_back = dot_last(grads_ref[0], down_ref[0])
+        sigmoid_value = jax.nn.sigmoid(gate_pre)
+        silu_value = gate_pre * sigmoid_value
+        hidden = silu_value * up_pre
+        gate_grad = jnp.sum(hidden * down_back, axis=1, keepdims=True)
+        gate_grad_ref[0] = jnp.broadcast_to(gate_grad, (slots, 128))
+        hidden_back = down_back * gates_here
+        slope = sigmoid_value * (1.0 + gate_pre * (1.0 - sigmoid_value))
+        gate_back = (hidden_back * up_pre * slope).astype(jnp.bfloat16)
+        up_back = (hidden_back * silu_value).astype(jnp.bfloat16)
+        scaled = (hidden * gates_here).astype(jnp.bfloat16)
+        hidden_ref[0] = scaled
+        gate_back_ref[0] = gate_back
+        up_back_ref[0] = up_back
+        back = dot_plain(gate_back, gate_ref[0]) + dot_plain(up_back, up_ref[0])
+        back_ref[0] = back.astype(jnp.bfloat16)
+        sum_ref[0] = dot_plain(scaled, down_ref[0]).astype(jnp.bfloat16)
+
+    wide = pl.BlockSpec((1, slots, width), lambda j: (j, 0, 0))
+    narrow = pl.BlockSpec((1, slots, 128), lambda j: (j, 0, 0))
+    inner = pl.BlockSpec((1, slots, units), lambda j: (j, 0, 0))
+    matrix = pl.BlockSpec((1, units, width), lambda j: (j, 0, 0))
+    return pl.pallas_call(
+        body,
+        grid=(count,),
+        in_specs=[wide, wide, narrow, matrix, matrix, matrix],
+        out_specs=[wide, wide, inner, inner, inner, narrow],
+        out_shape=[
+            jax.ShapeDtypeStruct((count, slots, width), jnp.bfloat16),
+            jax.ShapeDtypeStruct((count, slots, width), jnp.bfloat16),
+            jax.ShapeDtypeStruct((count, slots, units), jnp.bfloat16),
+            jax.ShapeDtypeStruct((count, slots, units), jnp.bfloat16),
+            jax.ShapeDtypeStruct((count, slots, units), jnp.bfloat16),
+            jax.ShapeDtypeStruct((count, slots, 128), jnp.float32),
+        ],
+        compiler_params=kernel_params(),
+        cost_estimate=pl.CostEstimate(
+            flops=12 * count * slots * units * width,
+            bytes_accessed=count * width * (6 * units + 8 * slots),
+            transcendentals=count * slots * units,
+        ),
+    )(slot_rows, slot_grads, gates, expert_gate, expert_up, expert_down)
+
+
+def sum_tokens(values, codes, shared, matrix, gate_grads, capacity):
+    tokens = codes.shape[2]
+    width = values.shape[2]
+    inner = matrix.shape[0]
+    with_gates = gate_grads is not None
+
+    def family(i):
+        return 2 * (i % 2) + 1 - i // 2
+
+    def body(*refs):
+        values_ref, codes_ref, shared_ref, matrix_ref = refs[:4]
+        sibling_ref, mine_ref = refs[4 + with_gates : 6 + with_gates]
+        i = pl.program_id(0)
+        matches = slot_matches(codes_ref, capacity)
+        rows = values_ref[...].reshape(EXP_DEV * capacity, width)
+        total = dot_first(as_picks(matches), rows)
+        total = total + dot_plain(shared_ref[0], matrix_ref[...])
+        total = total.astype(jnp.bfloat16)
+
+        @pl.when(i < 2)
+        def _():
+            sibling_ref[0] = total
+
+        @pl.when(i >= 2)
+        def _():
+            mine_ref[0] = total
+
+        if with_gates:
+            gate_grads_ref, dense_ref = refs[4], refs[7]
+            dense = [
+                jnp.sum(
+                    jnp.where(matches[j], gate_grads_ref[j][:, :1], 0.0), axis=0, keepdims=True
+                )
+                for j in range(EXP_DEV)
+            ]
+            dense_ref[0] = jnp.concatenate(dense + [jnp.zeros((4, tokens), jnp.float32)], axis=0)
+
+    in_specs = [
+        pl.BlockSpec((EXP_DEV, capacity, width), lambda i: (0, family(i), 0)),
+        pl.BlockSpec((1, 8, tokens), lambda i: (family(i), 0, 0)),
+        pl.BlockSpec((1, tokens, inner), lambda i: (family(i), 0, 0)),
+        pl.BlockSpec((inner, width), lambda i: (0, 0)),
+    ]
+    out_specs = [
+        pl.BlockSpec((1, tokens, width), lambda i: (jnp.minimum(i, 1), 0, 0)),
+        pl.BlockSpec((1, tokens, width), lambda i: (jnp.maximum(i - 2, 0), 0, 0)),
+    ]
+    out_shape = [jax.ShapeDtypeStruct((2, tokens, width), jnp.bfloat16)] * 2
+    operands = [values, codes, shared, matrix]
+    if with_gates:
+        in_specs.append(pl.BlockSpec((EXP_DEV, capacity, 128), lambda i: (0, family(i), 0)))
+        out_specs.append(pl.BlockSpec((1, 8, tokens), lambda i: (family(i), 0, 0)))
+        out_shape.append(jax.ShapeDtypeStruct((FAMILIES, 8, tokens), jnp.float32))
+        operands.append(gate_grads)
+    return pl.pallas_call(
+        body,
+        grid=(FAMILIES,),
+        in_specs=in_specs,
+        out_specs=out_specs,
+        out_shape=out_shape,
+        compiler_params=kernel_params(),
+        cost_estimate=pl.CostEstimate(
+            flops=FAMILIES * 2 * tokens * width * (EXP_DEV * capacity + inner),
+            bytes_accessed=FAMILIES * width * (4 * tokens + 2 * EXP_DEV * capacity),
+            transcendentals=0,
+        ),
+    )(*operands)
+
+
+def expert_weight_grads(rows, grads, gate_backs, up_backs, hiddens):
+    count, slots, width = rows[0].shape
+    units = hiddens[0].shape[2]
+    tile = 512
+    planes = len(rows)
+
+    def body(*refs):
+        rows_in = refs[:planes]
+        grads_in = refs[planes : 2 * planes]
+        gate_in = refs[2 * planes : 3 * planes]
+        up_in = refs[3 * planes : 4 * planes]
+        hidden_in = refs[4 * planes : 5 * planes]
+        gate_ref, up_ref, down_ref = refs[5 * planes :]
+        for left, right, out in (
+            (gate_in, rows_in, gate_ref),
+            (up_in, rows_in, up_ref),
+            (hidden_in, grads_in, down_ref),
+        ):
+            total = dot_first(left[0][0], right[0][0])
+            for p in range(1, planes):
+                total = total + dot_first(left[p][0], right[p][0])
+            out[0] = total
+
+    wide = pl.BlockSpec((1, slots, tile), lambda j, d: (j, 0, d))
+    inner = pl.BlockSpec((1, slots, units), lambda j, d: (j, 0, 0))
+    result = pl.BlockSpec((1, units, tile), lambda j, d: (j, 0, d))
+    return pl.pallas_call(
+        body,
+        grid=(count, width // tile),
+        in_specs=[wide] * (2 * planes) + [inner] * (3 * planes),
+        out_specs=[result] * 3,
+        out_shape=[jax.ShapeDtypeStruct((count, units, width), jnp.float32)] * 3,
+        compiler_params=kernel_params(),
+        cost_estimate=pl.CostEstimate(
+            flops=6 * count * planes * slots * units * width,
+            bytes_accessed=count * (12 * units * width + planes * slots * (4 * width + 6 * units)),
+            transcendentals=0,
+        ),
+    )(*rows, *grads, *gate_backs, *up_backs, *hiddens)
+
+
 def on_device(
+    inputs,
+    segment_ids,
+    routes,
+    norm_gain,
+    query_weight,
+    latent_weight,
+    latent_gain,
+    expand_weight,
+    output_weight,
+    ffn_gain,
+    router_weight,
+    expert_gate,
+    expert_up,
+    expert_down,
+    shared_gate,
+    shared_up,
+    shared_down,
+    out_grad,
+):
+    bf16 = jnp.bfloat16
+    f32 = jnp.float32
+    rows_count = inputs.shape[0]
+    row_devices = lax.axis_size("row")
+    row_place = lax.axis_index("row")
+    first = lax.axis_index("col") == 0
+    local_heads = query_weight.shape[1] // (NOPE + ROPE)
+    expert_count = EXP_DEV * row_devices
+    capacity = 4 * rows_count * TOPK // (3 * expert_count)
+    score_scale = (NOPE + ROPE) ** (-0.5)
+    segment_row = segment_ids[0]
+    places = jnp.arange(rows_count, dtype=jnp.int32)
+
+    steps = jnp.arange(row_devices, dtype=jnp.int32)
+    arrival = (
+        ((row_place // 4 - steps // 4) % 4) * 4 + ((row_place % 4) ^ (steps % 4))
+    ).astype(jnp.int32)
+    place_of = (((row_place // 4 - steps // 4) % 4) * 4 + ((row_place % 4) ^ (steps % 4))).astype(
+        jnp.int32
+    )
+
+    query_width = query_weight.shape[1]
+    latent_width = latent_weight.shape[1]
+    expand_width = expand_weight.shape[1] * expand_weight.shape[0] // latent_weight.shape[0]
+    output_width = output_weight.shape[0]
+    packed = jnp.concatenate(
+        [
+            query_weight,
+            latent_weight,
+            router_weight,
+            expand_weight.reshape(latent_weight.shape[0], expand_width),
+            output_weight.T,
+        ],
+        axis=1,
+    )
+    packed_full = lax.all_gather(packed, "row", axis=0, tiled=True)
+    edge = query_width
+    query_full = packed_full[:, :edge]
+    latent_full = packed_full[:, edge : edge + latent_width]
+    edge += latent_width
+    router_full = packed_full[:, edge : edge + expert_count]
+    edge += expert_count
+    expand_full = packed_full[:, edge : edge + expand_width].reshape(RANK, -1)
+    edge += expand_width
+    output_turned = packed_full[:, edge:]
+
+    shared_share = shared_gate.shape[1] // row_devices
+    shared_packed = jnp.stack([shared_gate.T, shared_up.T, shared_down], axis=0)
+    shared_packed = shared_packed.reshape(3, row_devices, shared_share, -1).transpose(1, 0, 2, 3)
+    shared_here = lax.all_to_all(shared_packed, "row", split_axis=0, concat_axis=0, tiled=True)
+    shared_here = shared_here.transpose(1, 2, 0, 3).reshape(3, shared_share, D)
+    shared_here = jnp.pad(shared_here, ((0, 0), (0, SHARED_PAD - shared_share), (0, 0)))
+    shared_pair = shared_here[:2].reshape(2 * SHARED_PAD, D)
+    shared_last = shared_here[2]
+
+    upstream_bf16 = join_cols(out_grad, first)
+    upstream = upstream_bf16.astype(f32)
+    grad_planes = spread_rows(sent_rows(upstream_bf16, first))
+
+    routes_all = lax.all_gather(routes, "row", axis=0)[arrival]
+    routes_all = local_tokens(routes_all, 1, first)
+    held_experts = row_place * EXP_DEV + jnp.arange(EXP_DEV, dtype=jnp.int32)
+    hits = jnp.any(routes_all[:, :, :, None] == held_experts, axis=2)
+    lower = (places[:, None] >= places[None, :]).astype(bf16)
+    ranks = jnp.einsum("ut,stj->suj", lower, hits.astype(bf16), preferred_element_type=f32)
+    codes = jnp.where(hits, ranks.astype(jnp.int32) - 1, -1)
+    codes = jnp.pad(codes.transpose(0, 2, 1), ((0, 0), (0, 8 - EXP_DEV), (0, 0)), constant_values=-1)
+
+    source = join_cols(inputs, first).astype(f32)
+    scale_one = lax.rsqrt(jnp.mean(source * source, axis=1, keepdims=True) + epsilon)
+    unit_one = source * scale_one
+    gain_one = join_cols(norm_gain[None], first)
+    gain_two = join_cols(ffn_gain[None], first)
+    normed_one = (unit_one * gain_one).astype(bf16)
+    query = jnp.dot(normed_one, query_full, preferred_element_type=f32).reshape(
+        rows_count, local_heads, NOPE + ROPE
+    )
+    latent = jnp.dot(normed_one, latent_full, preferred_element_type=f32).astype(bf16)
+    cosine, sine = rotation(rows_count, ROPE)
+    head_cos = cosine[:, None, :]
+    head_sin = sine[:, None, :]
+    compressed = latent[:, :RANK].astype(f32)
+    latent_scale = lax.rsqrt(jnp.mean(compressed * compressed, axis=1, keepdims=True) + epsilon)
+    latent_unit = compressed * latent_scale
+    latent_normed = (latent_unit * latent_gain).astype(bf16)
+    key_rope = rotate(latent[:, RANK:].astype(f32), cosine, sine).astype(bf16)
+    expanded = jnp.dot(latent_normed, expand_full, preferred_element_type=f32).reshape(
+        rows_count, local_heads, NOPE + VDIM
+    )
+    key_nope = expanded[..., :NOPE].astype(bf16)
+    values_all = expanded[..., NOPE:].astype(bf16)
+    query_nope = query[..., :NOPE].astype(bf16)
+    query_rope = rotate(query[..., NOPE:], head_cos, head_sin).astype(bf16)
+    raw = jnp.einsum("qhd,khd->hqk", query_nope, key_nope, preferred_element_type=f32)
+    raw = raw + jnp.einsum("qhd,kd->hqk", query_rope, key_rope, preferred_element_type=f32)
+    allowed = (segment_row[:, None] == segment_row[None, :]) & (places[None, :] <= places[:, None])
+    scores = jnp.where(allowed[None], raw * score_scale, -1e30)
+    top = jnp.max(scores, axis=2, keepdims=True)
+    exponent = jnp.exp(scores - top)
+    total = jnp.sum(exponent, axis=2, keepdims=True)
+    weights = exponent / total
+    log_blocks = top + jnp.log(total)
+    mixed = (
+        jnp.einsum("hqk,khd->qhd", weights.astype(bf16), values_all, preferred_element_type=f32)
+        .astype(bf16)
+        .reshape(rows_count, local_heads * VDIM)
+    )
+    attended_part = jnp.einsum(
+        "tv,dv->td", mixed, output_turned, preferred_element_type=f32
+    ).astype(bf16)
+    attended = attended_part.astype(f32) + swap_cols(attended_part).astype(f32)
+    middle = source + attended
+    scale_two = lax.rsqrt(jnp.mean(middle * middle, axis=1, keepdims=True) + epsilon)
+    unit_two = middle * scale_two
+    normed_two = (unit_two * gain_two).astype(bf16)
+    row_planes = spread_rows(sent_rows(normed_two, first))
+
+    logits = jnp.dot(normed_two, router_full, preferred_element_type=f32)
+    log_total = jax.nn.logsumexp(logits, axis=1, keepdims=True)
+    chances = jnp.exp(logits - log_total)
+
+    router_turned = router_full.T
+    router_held = lax.dynamic_slice_in_dim(
+        jnp.concatenate([router_turned, router_turned], axis=0),
+        row_place * EXP_DEV,
+        expert_count,
+        0,
+    )
+    sum_planes = [None] * PLANES
+    back_planes = [None] * PLANES
+    gate_grad_dense = []
+    kept_rows, kept_grads, kept_hidden, kept_gate, kept_up = [], [], [], [], []
+    shared_grads = 0.0
+    for plane in range(PLANES):
+        plane_codes = codes[plane * FAMILIES : (plane + 1) * FAMILIES]
+        slot_grads, hidden_grads = pick_grads(
+            grad_planes[plane], plane_codes, shared_last, capacity
+        )
+        slot_rows, gate_slots, shared_hidden, shared_back, shared_grad = pick_rows(
+            row_planes[plane],
+            grad_planes[plane],
+            plane_codes,
+            router_held,
+            shared_pair,
+            hidden_grads,
+            capacity,
+        )
+        expert_sum, row_back, scaled_hidden, gate_back, up_back, gate_grad = run_experts(
+            slot_rows, slot_grads, gate_slots, expert_gate, expert_up, expert_down
+        )
+        sibling, mine, dense = sum_tokens(
+            row_back, plane_codes, shared_back, shared_pair, gate_grad, capacity
+        )
+        back_planes[plane] = (sibling, mine)
+        sum_planes[plane] = sum_tokens(
+            expert_sum, plane_codes, shared_hidden, shared_last, None, capacity
+        )
+        gate_grad_dense.append(dense[:, :EXP_DEV])
+        shared_grads = shared_grads + shared_grad
+        kept_rows.append(slot_rows)
+        kept_grads.append(slot_grads)
+        kept_hidden.append(scaled_hidden)
+        kept_gate.append(gate_back)
+        kept_up.append(up_back)
+
+    back_sent = collect_rows(back_planes)
+    sum_sent = collect_rows(sum_planes)
+
+    gate_grad_dense = jnp.concatenate(gate_grad_dense, axis=0)
+    gate_grad_dense = local_tokens(gate_grad_dense, 2, first)[place_of]
+    gate_grad_dense = lax.all_to_all(
+        gate_grad_dense, "row", split_axis=0, concat_axis=0, tiled=True
+    ).reshape(expert_count, rows_count)
+    gate_grad_dense = gate_grad_dense + swap_cols(gate_grad_dense)
+    weighted_gates = gate_grad_dense.T * chances
+    logit_grads = (
+        weighted_gates - chances * jnp.sum(weighted_gates, axis=1, keepdims=True)
+    ).astype(bf16)
+    router_back = jnp.einsum("te,de->td", logit_grads, router_full, preferred_element_type=f32)
+    router_grad_part = jnp.einsum("td,te->de", normed_two, logit_grads, preferred_element_type=f32)
+
+    expert_gate_grad, expert_up_grad, expert_down_grad = expert_weight_grads(
+        kept_rows, kept_grads, kept_gate, kept_up, kept_hidden
+    )
+    shared_grads = shared_grads.reshape(3, SHARED_PAD, D)[:, :shared_share]
+    shared_grads = (
+        shared_grads.astype(bf16)
+        .reshape(3, shared_share, row_devices, -1)
+        .transpose(2, 0, 1, 3)
+    )
+    shared_grads = lax.all_to_all(shared_grads, "row", split_axis=0, concat_axis=0, tiled=True)
+    shared_grads = shared_grads.transpose(1, 0, 2, 3).reshape(3, row_devices * shared_share, -1)
+    shared_grads = shared_grads.astype(f32)
+    shared_gate_grad = shared_grads[0].T
+    shared_up_grad = shared_grads[1].T
+    shared_down_grad = shared_grads[2]
+
+    combined = merge_rows(
+        own_columns(sum_sent, first), swap_cols(other_columns(sum_sent, first)), first
+    )
+    output = (own_columns(middle, first) + combined).astype(bf16)
+
+    normed_two_back = merge_rows(back_sent, swap_cols(back_sent), first) + router_back
+    ffn_gain_part = jnp.sum(normed_two_back * unit_two, axis=0)
+    weighted = normed_two_back * gain_two
+    average = jnp.mean(weighted * unit_two, axis=1, keepdims=True)
+    middle_back = upstream + scale_two * (weighted - unit_two * average)
+    attended_back = middle_back.astype(bf16)
+    mixed_back = (
+        jnp.einsum("td,dv->tv", attended_back, output_turned, preferred_element_type=f32)
+        .astype(bf16)
+        .reshape(rows_count, local_heads, VDIM)
+    )
+    output_grad_part = jnp.einsum("td,tv->dv", attended_back, mixed, preferred_element_type=f32)
+
+    weights = jnp.exp(scores - log_blocks)
+    weight_back = jnp.einsum("qhd,khd->hqk", mixed_back, values_all, preferred_element_type=f32)
+    center = jnp.sum(weight_back * weights, axis=2, keepdims=True)
+    raw_back = (weights * (weight_back - center) * score_scale).astype(bf16)
+    query_nope_back = jnp.einsum("hqk,khd->qhd", raw_back, key_nope, preferred_element_type=f32)
+    query_rope_back = jnp.einsum("hqk,kd->qhd", raw_back, key_rope, preferred_element_type=f32)
+    key_nope_back = jnp.einsum("hqk,qhd->khd", raw_back, query_nope, preferred_element_type=f32)
+    key_rope_back = jnp.einsum("hqk,qhd->kd", raw_back, query_rope, preferred_element_type=f32)
+    values_back = jnp.einsum(
+        "hqk,qhd->khd", weights.astype(bf16), mixed_back, preferred_element_type=f32
+    )
+    query_back = jnp.concatenate(
+        [query_nope_back, unrotate(query_rope_back, head_cos, head_sin)], axis=2
+    )
+    query_back = query_back.astype(bf16).reshape(rows_count, local_heads * (NOPE + ROPE))
+    expanded_back = (
+        jnp.concatenate([key_nope_back, values_back], axis=2)
+        .astype(bf16)
+        .reshape(rows_count, local_heads * (NOPE + VDIM))
+    )
+    latent_normed_back = jnp.einsum(
+        "tc,rc->tr", expanded_back, expand_full, preferred_element_type=f32
+    )
+    expand_grad_part = jnp.einsum(
+        "tr,tc->rc", latent_normed, expanded_back, preferred_element_type=f32
+    )
+    latent_gain_part = jnp.sum(latent_normed_back * latent_unit, axis=0)
+    latent_weighted = latent_normed_back * latent_gain
+    compressed_back = latent_scale * (
+        latent_weighted
+        - latent_unit * jnp.mean(latent_weighted * latent_unit, axis=1, keepdims=True)
+    )
+    rope_back = unrotate(key_rope_back, cosine, sine)
+    latent_part = jnp.concatenate([compressed_back, rope_back], axis=1).astype(bf16)
+    latent_back = (latent_part.astype(f32) + swap_cols(latent_part).astype(f32)).astype(bf16)
+    latent_grad_part = jnp.einsum("td,tc->dc", normed_one, latent_back, preferred_element_type=f32)
+    query_grad_part = jnp.einsum("td,tc->dc", normed_one, query_back, preferred_element_type=f32)
+    input_part = jnp.einsum("tc,dc->td", query_back, query_full, preferred_element_type=f32)
+    input_part = input_part.astype(bf16)
+    latent_input = jnp.einsum("tc,dc->td", latent_back, latent_full, preferred_element_type=f32)
+    weighted_part = jnp.sum(input_part.astype(f32) * gain_one * unit_one, axis=1)
+    weighted_sum = weighted_part + swap_cols(weighted_part)
+    weighted_sum = weighted_sum + jnp.sum(latent_input * gain_one * unit_one, axis=1)
+    normed_one_back = (
+        own_columns(input_part, first).astype(f32)
+        + swap_cols(other_columns(input_part, first)).astype(f32)
+        + own_columns(latent_input, first)
+    )
+    own_unit = own_columns(unit_one, first)
+    norm_gain_part = jnp.sum(normed_one_back * own_unit, axis=0)
+    input_grad = own_columns(middle_back, first) + scale_one * (
+        normed_one_back * norm_gain - own_unit * (weighted_sum / D)[:, None]
+    )
+    gains = jnp.concatenate(
+        [
+            norm_gain_part,
+            own_columns(ffn_gain_part, first),
+            latent_gain_part + swap_cols(latent_gain_part),
+        ]
+    )
+    gains = lax.psum(gains, "row")
+    width_share = norm_gain.shape[0]
+    norm_gain_grad = gains[:width_share]
+    ffn_gain_grad = gains[width_share : 2 * width_share]
+    latent_gain_grad = gains[2 * width_share :]
+
+    def to_owners(values):
+        return lax.psum_scatter(
+            values.astype(bf16), "row", scatter_dimension=0, tiled=True
+        ).astype(f32)
+
+    output_grad = to_owners(output_grad_part).T
+    dense_part = jnp.concatenate(
+        [
+            query_grad_part,
+            latent_grad_part,
+            router_grad_part,
+            expand_grad_part.reshape(D, expand_width),
+        ],
+        axis=1,
+    )
+    dense_grad = to_owners(dense_part)
+    edge = query_width
+    query_grad = dense_grad[:, :edge]
+    latent_grad = dense_grad[:, edge : edge + latent_width]
+    edge += latent_width
+    router_grad = dense_grad[:, edge : edge + expert_count]
+    edge += expert_count
+    expand_grad = dense_grad[:, edge:].reshape(expand_weight.shape)
+    return (
+        output,
+        input_grad,
+        norm_gain_grad,
+        query_grad,
+        latent_grad,
+        latent_gain_grad,
+        expand_grad,
+        output_grad,
+        ffn_gain_grad,
+        router_grad,
+        expert_gate_grad,
+        expert_up_grad,
+        expert_down_grad,
+        shared_gate_grad,
+        shared_up_grad,
+        shared_down_grad,
+    )
+
+
+def on_device_general(
     inputs,
     segment_ids,
     routes,
@@ -479,6 +1286,7 @@
         P("row", "col"),
         P("col", "row"),
     )
+    plan = on_device if dict(mesh.shape) == {"row": 16, "col": 2} else on_device_general
     return jax.shard_map(
-        on_device, mesh=mesh, in_specs=in_specs, out_specs=out_specs, check_vma=False
-    )
+        plan, mesh=mesh, in_specs=in_specs, out_specs=out_specs, check_vma=False
+    )

time: 3640 us -> 1540 us (0.42)
  waiting for transfers between devices: 2340 us -> 551 us
  Pallas kernels: 0 us -> 373 us
  matrix products: 478 us -> 146 us
  local copies, waits for them, and re-layouts: 296 us -> 108 us
  blocking collectives: 262 us -> 92 us
    reduce_scatter x20 -> x1, waiting for transfers between devices: 1120 us -> 0.01 us  [to_owners(): lax.psum_scatter(values.astype(bf16), 'row', scatter_dimension=0, tiled=T...]
    all_gather x14 -> x1, waiting for transfers between devices: 914 us -> 75 us  [on_device(): packed_full = lax.all_gather(packed, 'row', axis=0, tiled=True)]
    ppermute x0 -> x104, waiting for transfers between devices: none -> 476 us  [the longest x36 272 us: swap_cols(): return lax.ppermute(values, 'col', [(0, 1), (1, 0)])]
    pallas_call x0 -> x21, Pallas kernels: none -> 373 us  [the longest x4 111 us: run_experts(): pl.pallas_call(body, grid=(count,), in_specs=[wide, wide, narrow, matrix,...]
    dot_general x34 -> x8, matrix products: 370 us -> 25.7 us  [the longest x1 6.8 us: on_device(): jnp.einsum('td,dv->tv', attended_back, output_turned, preferred_element_t...]
    unnamed x43 -> x4, waiting for transfers between devices: 156 us -> 0.05 us
    all_to_all x4 -> x3, waiting for transfers between devices: 151 us -> 0.01 us  [the longest x1 0.01 us: on_device(): lax.all_to_all(shared_packed, 'row', split_axis=0, concat_axis=0, tiled=T...]
    all_gather x1, blocking collectives: 166 us -> 34.4 us  [on_device(): routes_all = lax.all_gather(routes, 'row', axis=0)[arrival]]
  transfers between devices with their start and end apart: 43 -> 110, of which waited for: 31 -> 33; matrix products, arithmetic and copies ran while one was open for 23% -> 24% of each run, Pallas kernels for 0% -> 24%
where the time goes in v1:
time: 1540 us; the launch traced here: 1530 us
  waiting for transfers between devices  551 us (36%)
  Pallas kernels  373 us (24%)
  matrix products  146 us (9%)
  other arithmetic  142 us (9%)
  local copies, waits for them, and re-layouts  108 us (7%)
  starting transfers between devices  104 us (7%)
  blocking collectives  92 us (6%)
  between operations  16.9 us (1%)
    ppermute x36, waiting for transfers between devices, swap_cols(): return lax.ppermute(values, 'col', [(0, 1), (1, 0)])  272 us
    ppermute x12, waiting for transfers between devices, turn_planes(): return lax.ppermute(values, 'row', [(i, (i + 4) % 16) for i in range(16)])  149 us
    pallas_call x4, Pallas kernels, run_experts(): pl.pallas_call(body, grid=(count,), in_specs=[wide, wide, narrow, matrix,...  111 us
    pallas_call x4, Pallas kernels, pick_rows(): pl.pallas_call(body, grid=(FAMILIES,), in_specs=[pl.BlockSpec(memory_spac...  89.5 us
    pallas_call x8, Pallas kernels, sum_tokens(): pl.pallas_call(body, grid=(FAMILIES,), in_specs=in_specs, out_specs=out_s...  81.3 us
    all_gather x1, waiting for transfers between devices, on_device(): packed_full = lax.all_gather(packed, 'row', axis=0, tiled=True)  75 us
    psum x1, blocking collectives, on_device(): gains = lax.psum(gains, 'row')  57.6 us
    pallas_call x1, Pallas kernels, expert_weight_grads(): pl.pallas_call(body, grid=(count, width // tile), in_specs=[wide] * (2 *...  55 us
  transfers between devices with their start and end apart: 110, of which 33 were waited for; matrix products, arithmetic and copies ran while one was open for 24% of the time, Pallas kernels for 24%

profile of v1, /device:TPU:0, one launch (start us, length us, event | category | flops | bytes accessed | tf_op | source)
XLA Modules:
  0.0 1533.0 jit_solution(1670611174109868461)
XLA Ops:
  16.4 24.1 %collective-permute-done.11 = bf16[512,1024]{1,0:T(8,128)(2,1)S(1)} collective-permute-done((bf16[512,1024]{1,0:T(8,128)(2,1)}, bf16[512,1024]{1,0:T(8,128)(2,1)S(1)}, u32[]{:S(2)}, u32[]{:S(2)}) %collective-permute-start.11) | collective-permute-done | bytes 1048608 | tf_op jit(solution)/shard_map/ppermute | solution.py:92
  76.5 27.7 %collective-permute-done.32.refs_0_.refs_8_ = bf16[352,2048]{1,0:T(8,128)(2,1)} collective-permute-done((bf16[352,2048]{1,0:T(8,128)(2,1)}, bf16[352,2048]{1,0:T(8,128)(2,1)}, u32[]{:S(2)}, u32[]{:S(2)}) %collective-permute-start.32) | collective-permute-done | bytes 1441824 | tf_op jit(solution)/shard_map/ppermute | solution.py:100
  116.6 75.0 %all-gather.3.cloned.1.call-done = bf16[2048,3712]{0,1:T(8,128)(2,1)} async-done(((bf16[128,3712]{0,1:T(8,128)(2,1)}), bf16[2048,3712]{0,1:T(8,128)(2,1)}) %all-gather.3.cloned.1.call-update) | async-done | bytes 15204368 | tf_op jit(solution)/shard_map/all_gather | solution.py:600
  244.6 15.7 %collective-permute-done.34.refs_0_.refs_8_ = bf16[352,2048]{1,0:T(8,128)(2,1)} collective-permute-done((bf16[352,2048]{1,0:T(8,128)(2,1)}, bf16[352,2048]{1,0:T(8,128)(2,1)}, u32[]{:S(2)}, u32[]{:S(2)}) %collective-permute-start.34) | collective-permute-done | bytes 1441824 | tf_op jit(solution)/shard_map/ppermute | solution.py:100
  271.8 33.8 %collective-permute-done.73.refs_5_.refs_13_ = bf16[160,2048]{1,0:T(8,128)(2,1)} collective-permute-done((bf16[160,2048]{1,0:T(8,128)(2,1)}, bf16[160,2048]{1,0:T(8,128)(2,1)}, u32[]{:S(2)}, u32[]{:S(2)}) %collective-permute-start.73) | collective-permute-done | bytes 655392 | tf_op jit(solution)/shard_map/ppermute | solution.py:92
  307.0 24.9 %collective-permute-done.38.refs_4_.refs_12_ = bf16[352,2048]{1,0:T(8,128)(2,1)} collective-permute-done((bf16[352,2048]{1,0:T(8,128)(2,1)}, bf16[352,2048]{1,0:T(8,128)(2,1)}, u32[]{:S(2)}, u32[]{:S(2)}) %collective-permute-start.38) | collective-permute-done | bytes 1441824 | tf_op jit(solution)/shard_map/ppermute | solution.py:96
  344.6 14.3 collective-permute-done.56.refs_5_.refs_13_
  389.7 34.4 %all-gather = s32[8192,6]{0,1:T(8,128)S(1)} all-gather(s32[512,6]{0,1:T(8,128)S(1)} %copy-done.86), channel_id=2, replica_groups=mesh['row'=16,'col'=2] {'row'}, dimensions={0}, use_global_device_ids=true | all-gather | bytes 208896 | tf_op jit(solution)/shard_map/all_gather | solution.py:624
  427.6 14.7 collective-permute-done.4.refs_1_
  502.0 14.5 collective-permute-done.66.refs_5_
  517.6 22.4 %shard_map.298 = (bf16[4,256,2048]{2,1,0:T(8,128)(2,1)}, f32[4,256,128]{2,1,0:T(8,128)}, bf16[4,512,128]{2,1,0:T(8,128)(2,1)}, bf16[4,512,256]{2,1,0:T(8,128)(2,1)}, f32[384,2048]{1,0:T(8,128)}) custom-call(bf16[352,2048]{1,0:T(8,128)(2,1)} %pad_maximum_fusion.10.refs_0_, bf16[160,2048]{1,0:T(8,128)(2,1)} %collective-permute-done.4.refs_1_, ...), custom_call_target="tpu_custom_call" | custom-call | flops 9663676416 | bytes 25165824 | tf_op jit(solution)/shard_map/pallas_call | solution.py:330
  544.9 22.3 %shard_map.310 = (bf16[4,256,2048]{2,1,0:T(8,128)(2,1)}, f32[4,256,128]{2,1,0:T(8,128)}, bf16[4,512,128]{2,1,0:T(8,128)(2,1)}, bf16[4,512,256]{2,1,0:T(8,128)(2,1)}, f32[384,2048]{1,0:T(8,128)}) custom-call(bf16[352,2048]{1,0:T(8,128)(2,1)} %collective-permute-done.22.refs_0_, bf16[160,2048]{1,0:T(8,128)(2,1)} %copy-done.120, ...), custom_call_target="tpu_custom_call" | custom-call | flops 9663676416 | bytes 25165824 | tf_op jit(solution)/shard_map/pallas_call | solution.py:330
  567.9 27.7 %shard_map.311 = (bf16[4,256,2048]{2,1,0:T(8,128)(2,1)}, bf16[4,256,2048]{2,1,0:T(8,128)(2,1)}, bf16[4,256,704]{2,1,0:T(8,128)(2,1)}, bf16[4,256,704]{2,1,0:T(8,...) custom-call(bf16[4,256,2048]{2,1,0:T(8,128)(2,1)} %get-tuple-element.116.rows_ref.refs_1_, ...), custom_call_target="tpu_custom_call" | custom-call | flops 17716740096 | bytes 51380224 | tf_op jit(solution)/shard_map/pallas_call | solution.py:413
  609.5 22.4 %shard_map.306 = (bf16[4,256,2048]{2,1,0:T(8,128)(2,1)}, f32[4,256,128]{2,1,0:T(8,128)}, bf16[4,512,128]{2,1,0:T(8,128)(2,1)}, bf16[4,512,256]{2,1,0:T(8,128)(2,1)}, f32[384,2048]{1,0:T(8,128)}) custom-call(bf16[352,2048]{1,0:T(8,128)(2,1)} %copy-done.64, bf16[160,2048]{1,0:T(8,128)(2,1)} %collective-permute-done.45.refs_1_, ...), custom_call_target="tpu_custom_call" | custom-call | flops 9663676416 | bytes 25165824 | tf_op jit(solution)/shard_map/pallas_call | solution.py:330
  632.4 27.9 %shard_map.307 = (bf16[4,256,2048]{2,1,0:T(8,128)(2,1)}, bf16[4,256,2048]{2,1,0:T(8,128)(2,1)}, bf16[4,256,704]{2,1,0:T(8,128)(2,1)}, bf16[4,256,704]{2,1,0:T(8,...) custom-call(bf16[4,256,2048]{2,1,0:T(8,128)(2,1)} %get-tuple-element.108.rows_ref.refs_2_, ...), custom_call_target="tpu_custom_call" | custom-call | flops 17716740096 | bytes 51380224 | tf_op jit(solution)/shard_map/pallas_call | solution.py:413
  672.3 22.4 %shard_map.302 = (bf16[4,256,2048]{2,1,0:T(8,128)(2,1)}, f32[4,256,128]{2,1,0:T(8,128)}, bf16[4,512,128]{2,1,0:T(8,128)(2,1)}, bf16[4,512,256]{2,1,0:T(8,128)(2,1)}, f32[384,2048]{1,0:T(8,128)}) custom-call(bf16[352,2048]{1,0:T(8,128)(2,1)} %collective-permute-done.24.refs_0_, bf16[160,2048]{1,0:T(8,128)(2,1)} %collective-permute-done.25.refs_1_, ...), custom_call_target="tpu_custom_call" | custom-call | flops 9663676416 | bytes 25165824 | tf_op jit(solution)/shard_map/pallas_call | solution.py:330
  694.7 27.7 %shard_map.303 = (bf16[4,256,2048]{2,1,0:T(8,128)(2,1)}, bf16[4,256,2048]{2,1,0:T(8,128)(2,1)}, bf16[4,256,704]{2,1,0:T(8,128)(2,1)}, bf16[4,256,704]{2,1,0:T(8,...) custom-call(bf16[4,256,2048]{2,1,0:T(8,128)(2,1)} %get-tuple-element.100.rows_ref.refs_3_, ...), custom_call_target="tpu_custom_call" | custom-call | flops 17716740096 | bytes 51380224 | tf_op jit(solution)/shard_map/pallas_call | solution.py:413
  741.4 27.7 %shard_map.299 = (bf16[4,256,2048]{2,1,0:T(8,128)(2,1)}, bf16[4,256,2048]{2,1,0:T(8,128)(2,1)}, bf16[4,256,704]{2,1,0:T(8,128)(2,1)}, bf16[4,256,704]{2,1,0:T(8,...) custom-call(bf16[4,256,2048]{2,1,0:T(8,128)(2,1)} %get-tuple-element.92.rows_ref.refs_0_, ...), custom_call_target="tpu_custom_call" | custom-call | flops 17716740096 | bytes 51380224 | tf_op jit(solution)/shard_map/pallas_call | solution.py:413
  791.6 26.3 %collective-permute-done.90 = bf16[2,160,2048]{2,1,0:T(8,128)(2,1)S(1)} collective-permute-done((bf16[2,160,2048]{2,1,0:T(8,128)(2,1)S(1)}, bf16[2,160,2048]{2,1,0:T(8,128)(2,1)S(1)}, u32[]{:S(2)}, u32[]{:S(2)}) %collective-permute-start.90) | collective-permute-done | bytes 1310752 | tf_op jit(solution)/shard_map/ppermute | solution.py:92
  949.9 17.3 %collective-permute-done.99 = f32[64,512]{1,0:T(8,128)S(1)} collective-permute-done((f32[64,512]{1,0:T(8,128)}, f32[64,512]{1,0:T(8,128)S(1)}, u32[]{:S(2)}, u32[]{:S(2)}) %collective-permute-start.99) | collective-permute-done | bytes 131104 | tf_op jit(solution)/shard_map/ppermute | solution.py:92
  980.4 21.3 %collective-permute-done.98 = bf16[352,2048]{1,0:T(8,128)(2,1)S(1)} collective-permute-done((bf16[352,2048]{1,0:T(8,128)(2,1)S(1)}, bf16[352,2048]{1,0:T(8,128)(2,1)S(1)}, u32[]{:S(2)}, u32[]{:S(2)}) %collective-permute-start.98) | collective-permute-done | bytes 1441824 | tf_op jit(solution)/shard_map/ppermute | solution.py:92
  1030.7 17.9 %fusion.48 = bf16[512,8,128]{0,2,1:T(8,128)(2,1)} fusion(f32[8,512,512]{1,2,0:T(8,128)} %fusion.130, f32[8,512,512]{1,2,0:T(8,128)} %copy-done.3, f32[8,512]{1,0:T(8,128)S(1)} %log_add_fusion, f32[512,8,192]{0,2,1:T(8,128)} %bitcast.181), kind=kOutput, calls=%fused_computation.89 | convolution fusion | flops 551555584 | bytes 35684352 | tf_op jit(solution)/shard_map/hqk,qhd->khd/dot_general | solution.py:786
  1055.5 15.5 %fusion.112 = f32[512,64]{0,1:T(8,128)} fusion(f32[8,512,512]{1,2,0:T(8,128)} %fusion.130, f32[8,512,512]{1,2,0:T(8,128)} %copy-done.3, f32[8,512]{1,0:T(8,128)S(1)} %log_add_fusion, bf16[512,8,32]{0,2,1:T(8,128)(2,1)} %copy-done.54, bf16[512,8,32]{0,2,1:T(8,128)(2,1)} %copy-done.53), kind=kOutput, calls=%fused_computation.164 | convolution fusion | flops 284168704 | bytes 17448960 | tf_op jit(solution)/shard_map/hqk,qhd->kd/dot_general | solution.py:787
  1079.8 15.7 %fusion.102 = f32[512,8,64]{0,2,1:T(8,128)} fusion(f32[8,512,512]{1,2,0:T(8,128)} %fusion.130, f32[8,512,512]{1,2,0:T(8,128)} %copy-done.3, f32[8,512]{1,0:T(8,128)S(1)} %log_add_fusion, bf16[512,32]{0,1:T(8,128)(2,1)S(1)} %copy-done.72, bf16[512,32]{0,1:T(8,128)(2,1)S(1)} %copy-done.70), kind=kOutput, calls=%fused_computation.145 | convolution fusion | flops 283251200 | bytes 17907712 | tf_op jit(solution)/shard_map/hqk,kd->qhd/dot_general | solution.py:785
  1095.5 16.1 %fusion.99 = bf16[512,8,128]{0,2,1:T(8,128)(2,1)} fusion(f32[8,512,512]{1,2,0:T(8,128)} %fusion.130, f32[8,512,512]{1,2,0:T(8,128)} %copy-done.3, f32[8,512]{1,0:T(8,128)S(1)} %log_add_fusion, bf16[512,8,256]{2,0,1:T(8,128)(2,1)} %copy-done.44), kind=kOutput, calls=%fused_computation.144 | convolution fusion | flops 552079872 | bytes 35684352 | tf_op jit(solution)/shard_map/hqk,khd->qhd/dot_general | solution.py:784
  1136.0 23.8 %pad_maximum_fusion = bf16[2048,2688]{0,1:T(8,128)(2,1)} fusion(bf16[2048,512]{0,1:T(8,128)(2,1)S(1)} %copy-done.25, bf16[2048,64]{0,1:T(8,128)(2,1)S(1)} %copy-done.52, bf16[2048,576]{0,1:T(8,128)(2,1)S(1)} %convolution_convert_fusion.2, bf16[2048,1536]{0,1:T(8,128)(2,1)} %convolution_convert_fusion), kind=kLoop, calls=%fused_computation.3 | loop fusion | flops 44040192 | bytes 22020096 | tf_op jit(solution)/shard_map/concatenate | solution.py:852
  1159.8 14.3 copy.266
  1197.8 17.3 %collective-permute-done.43 = bf16[2,160,2048]{2,1,0:T(8,128)(2,1)} collective-permute-done((bf16[2,160,2048]{2,1,0:T(8,128)(2,1)}, bf16[2,160,2048]{2,1,0:T(8,128)(2,1)}, u32[]{:S(2)}, u32[]{:S(2)}) %collective-permute-start.43) | collective-permute-done | bytes 1310752 | tf_op jit(solution)/shard_map/ppermute | solution.py:92
  1264.9 33.5 %collective-permute-done.80 = bf16[352,2048]{1,0:T(8,128)(2,1)S(1)} collective-permute-done((bf16[352,2048]{1,0:T(8,128)(2,1)S(1)}, bf16[352,2048]{1,0:T(8,128)(2,1)S(1)}, u32[]{:S(2)}, u32[]{:S(2)}) %collective-permute-start.80) | collective-permute-done | bytes 1441824 | tf_op jit(solution)/shard_map/ppermute | solution.py:100
  1311.1 47.9 %collective-permute-done.81 = bf16[352,2048]{1,0:T(8,128)(2,1)} collective-permute-done((bf16[352,2048]{1,0:T(8,128)(2,1)}, bf16[352,2048]{1,0:T(8,128)(2,1)}, u32[]{:S(2)}, u32[]{:S(2)}) %collective-permute-start.81) | collective-permute-done | bytes 1441824 | tf_op jit(solution)/shard_map/ppermute | solution.py:100
  1363.7 55.0 %shard_map.317 = (f32[4,704,2048]{2,1,0:T(8,128)}, f32[4,704,2048]{2,1,0:T(8,128)}, f32[4,704,2048]{2,1,0:T(8,128)}) custom-call(bf16[4,256,2048]{2,1,0:T(8,128)(2,1)} %get-tuple-element.92.rows_ref.refs_0_, bf16[4,256,2048]{2,1,0:T(8,128)(2,1)} %get-tuple-element.116.rows_ref.refs_1_, bf16[4,256,2048]{2,1,0:T(8,128)(2,1)} %get-tuple-element.108.rows_ref.refs_2_, ...), custom_call_target="tpu_custom_call" | custom-call | flops 35433480192 | bytes 120061952 | tf_op jit(solution)/shard_map/pallas_call | solution.py:530
  1452.9 57.6 %psum.7 = f32[2560]{0:T(1024)S(1)} all-reduce(f32[2560]{0:T(1024)S(1)} %pad_maximum_fusion.18), channel_id=1, replica_groups=mesh['row'=16,'col'=2] {'row'}, use_global_device_ids=true, to_apply=%region_17.18 | all-reduce | flops 2560 | bytes 20480 | tf_op jit(solution)/shard_map/psum | solution.py:840
  (690 shorter events, 656.9 us)
Async XLA Ops:
  7.2 184.4 %all-gather.3.cloned.1.call-start = ((), (), s32[]{:S(2)}) async-start(), calls=%async_computation.5 | async-start | bytes 16154624 | tf_op jit(solution)/shard_map/all_gather | solution.py:600
  63.1 158.9 %collective-permute-start.3 = (f32[1,1024]{1,0:T(1,128)}, f32[1,1024]{1,0:T(1,128)}, u32[]{:S(2)}, u32[]{:S(2)}) collective-permute-start(f32[1,1024]{1,0:T(1,128)} %bitcast.12), channel_id=1, source_target_pairs={{0,1},{1,0},{2,3},{3,2},{4,5},{5,4},{6,7},{7,6},{8,9},{9,8},{10,11... | collective-permute-start | bytes 12296 | tf_op jit(solution)/shard_map/ppermute | solution.py:92
  65.2 161.5 %collective-permute-start.13 = (bf16[352,2048]{1,0:T(8,128)(2,1)}, bf16[352,2048]{1,0:T(8,128)(2,1)}, u32[]{:S(2)}, u32[]{:S(2)}) collective-permute-start(bf16[352,2048]{1,0:T(8,128)(2,1)} %pad_maximum_fusion.11.refs_0_.refs_8_), channel_id=1, source_target_pairs={{0,2},{2,0},{4,6},{6,4},{8,10},{10,8},{12,14},{14,12},{16,18},{18,... | collective-permute-start | bytes 4325384 | tf_op jit(solution)/shard_map/ppermute | solution.py:96
  76.5 150.2 %collective-permute-start.14 = (bf16[160,2048]{1,0:T(8,128)(2,1)}, bf16[160,2048]{1,0:T(8,128)(2,1)}, u32[]{:S(2)}, u32[]{:S(2)}) collective-permute-start(bf16[160,2048]{1,0:T(8,128)(2,1)} %collective-permute-done.12.refs_1_.refs_9_), channel_id=1, source_target_pairs={{0,2},{2,0},{4,6},{6,4},{8,10},{10,8},{12,14},{14,12},{16,18},{18,... | collective-permute-start | bytes 1966088 | tf_op jit(solution)/shard_map/ppermute | solution.py:96
  106.2 117.6 %collective-permute-start.69 = (bf16[160,2048]{1,0:T(8,128)(2,1)}, bf16[160,2048]{1,0:T(8,128)(2,1)}, u32[]{:S(2)}, u32[]{:S(2)}) collective-permute-start(bf16[160,2048]{1,0:T(8,128)(2,1)} %slice.578), channel_id=1, source_target_pairs={{0,1},{1,0},{2,3},{3,2},{4,5},{5,4},{6,7},{7,6},{8,9},{9,8},{10,11... | collective-permute-start | bytes 1966088 | tf_op jit(solution)/shard_map/ppermute | solution.py:92
  107.8 116.1 %collective-permute-start.33 = (bf16[352,2048]{1,0:T(8,128)(2,1)}, bf16[352,2048]{1,0:T(8,128)(2,1)}, u32[]{:S(2)}, u32[]{:S(2)}) collective-permute-start(bf16[352,2048]{1,0:T(8,128)(2,1)} %collective-permute-done.32.refs_0_.refs_8_), channel_id=1, source_target_pairs={{0,8},{2,10},{4,12},{6,14},{8,16},{10,18},{12,20},{14,22},{16,24},... | collective-permute-start | bytes 4325384 | tf_op jit(solution)/shard_map/ppermute | solution.py:100
  243.1 88.8 %collective-permute-start.2 = (bf16[512,2048]{1,0:T(8,128)(2,1)}, bf16[512,2048]{1,0:T(8,128)(2,1)}, u32[]{:S(2)}, u32[]{:S(2)}) collective-permute-start(bf16[512,2048]{1,0:T(8,128)(2,1)} %fusion.22), channel_id=1, source_target_pairs={{0,1},{1,0},{2,3},{3,2},{4,5},{5,4},{6,7},{7,6},{8,9},{9,8},{10,11... | collective-permute-start | bytes 6291464 | tf_op jit(solution)/shard_map/ppermute | solution.py:92
  244.6 62.4 %collective-permute-start.55 = (bf16[352,2048]{1,0:T(8,128)(2,1)}, bf16[352,2048]{1,0:T(8,128)(2,1)}, u32[]{:S(2)}, u32[]{:S(2)}) collective-permute-start(bf16[352,2048]{1,0:T(8,128)(2,1)} %collective-permute-done.33.refs_0_.refs_8_), channel_id=1, source_target_pairs={{0,4},{2,6},{4,0},{6,2},{8,12},{10,14},{12,8},{14,10},{16,20},{18,... | collective-permute-start | bytes 4325384 | tf_op jit(solution)/shard_map/ppermute | solution.py:96
  260.3 71.6 %collective-permute-start.38 = (bf16[352,2048]{1,0:T(8,128)(2,1)}, bf16[352,2048]{1,0:T(8,128)(2,1)}, u32[]{:S(2)}, u32[]{:S(2)}) collective-permute-start(bf16[352,2048]{1,0:T(8,128)(2,1)} %collective-permute-done.34.refs_0_.refs_8_), channel_id=1, source_target_pairs={{0,4},{2,6},{4,0},{6,2},{8,12},{10,14},{12,8},{14,10},{16,20},{18,... | collective-permute-start | bytes 4325384 | tf_op jit(solution)/shard_map/ppermute | solution.py:96
  261.3 80.0 %collective-permute-start.17 = (bf16[352,2048]{1,0:T(8,128)(2,1)}, bf16[352,2048]{1,0:T(8,128)(2,1)}, u32[]{:S(2)}, u32[]{:S(2)}) collective-permute-start(bf16[352,2048]{1,0:T(8,128)(2,1)} %collective-permute-done.15.refs_4_.refs_12_), channel_id=1, source_target_pairs={{0,2},{2,0},{4,6},{6,4},{8,10},{10,8},{12,14},{14,12},{16,18},{18,... | collective-permute-start | bytes 4325384 | tf_op jit(solution)/shard_map/ppermute | solution.py:96
  266.9 175.6 %all-to-all-start = ((bf16[16,3,88,128]{3,2,1,0:T(8,128)(2,1)}), bf16[16,3,88,128]{3,2,1,0:T(8,128)(2,1)S(1)}, u32[]{:S(2)}, u32[]{:S(2)}) async-start(bf16[16,3,88,128]{3,2,1,0:T(8,128)(2,1)} %copy.236), calls=%async_computation | async-start | bytes 2162688 | tf_op jit(solution)/shard_map/all_to_all | solution.py:614
  344.0 81.1 %collective-permute-start.57 = (bf16[352,2048]{1,0:T(8,128)(2,1)}, bf16[352,2048]{1,0:T(8,128)(2,1)}, u32[]{:S(2)}, u32[]{:S(2)}) collective-permute-start(bf16[352,2048]{1,0:T(8,128)(2,1)} %collective-permute-done.55.refs_4_.refs_12_), channel_id=1, source_target_pairs={{0,2},{2,0},{4,6},{6,4},{8,10},{10,8},{12,14},{14,12},{16,18},{18,... | collective-permute-start | bytes 4325384 | tf_op jit(solution)/shard_map/ppermute | solution.py:96
  344.1 81.8 %collective-permute-start.36 = (bf16[352,2048]{1,0:T(8,128)(2,1)}, bf16[352,2048]{1,0:T(8,128)(2,1)}, u32[]{:S(2)}, u32[]{:S(2)}) collective-permute-start(bf16[352,2048]{1,0:T(8,128)(2,1)} %collective-permute-done.34.refs_0_.refs_8_), channel_id=1, source_target_pairs={{0,2},{2,0},{4,6},{6,4},{8,10},{10,8},{12,14},{14,12},{16,18},{18,... | collective-permute-start | bytes 4325384 | tf_op jit(solution)/shard_map/ppermute | solution.py:96
  375.4 66.9 %collective-permute-start.22 = (bf16[352,2048]{1,0:T(8,128)(2,1)}, bf16[352,2048]{1,0:T(8,128)(2,1)}, u32[]{:S(2)}, u32[]{:S(2)}) collective-permute-start(bf16[352,2048]{1,0:T(8,128)(2,1)} %pad_maximum_fusion.10.refs_0_), channel_id=1, source_target_pairs={{0,8},{2,10},{4,12},{6,14},{8,16},{10,18},{12,20},{14,22},{16,24},... | collective-permute-start | bytes 4325384 | tf_op jit(solution)/shard_map/ppermute | solution.py:100
  375.5 66.8 %collective-permute-start.7 = (bf16[352,2048]{1,0:T(8,128)(2,1)}, bf16[352,2048]{1,0:T(8,128)(2,1)}, u32[]{:S(2)}, u32[]{:S(2)}) collective-permute-start(bf16[352,2048]{1,0:T(8,128)(2,1)} %pad_maximum_fusion.10.refs_0_), channel_id=1, source_target_pairs={{0,4},{2,6},{4,0},{6,2},{8,12},{10,14},{12,8},{14,10},{16,20},{18,... | collective-permute-start | bytes 4325384 | tf_op jit(solution)/shard_map/ppermute | solution.py:96
  542.3 65.0 %collective-permute-start.46 = (bf16[352,2048]{1,0:T(8,128)(2,1)S(1)}, bf16[352,2048]{1,0:T(8,128)(2,1)}, u32[]{:S(2)}, u32[]{:S(2)}) collective-permute-start(bf16[352,2048]{1,0:T(8,128)(2,1)S(1)} %collective-permute-done.23.refs_0_), channel_id=1, source_target_pairs={{0,2},{2,0},{4,6},{6,4},{8,10},{10,8},{12,14},{14,12},{16,18},{18,... | collective-permute-start | bytes 4325384 | tf_op jit(solution)/shard_map/ppermute | solution.py:96
  542.5 64.6 %collective-permute-start.47 = (bf16[160,2048]{1,0:T(8,128)(2,1)}, bf16[160,2048]{1,0:T(8,128)(2,1)}, u32[]{:S(2)}, u32[]{:S(2)}) collective-permute-start(bf16[160,2048]{1,0:T(8,128)(2,1)} %collective-permute-done.45.refs_1_), channel_id=1, source_target_pairs={{0,2},{2,0},{4,6},{6,4},{8,10},{10,8},{12,14},{14,12},{16,18},{18,... | collective-permute-start | bytes 1966088 | tf_op jit(solution)/shard_map/ppermute | solution.py:96
  544.4 63.4 %collective-permute-start.25 = (bf16[160,2048]{1,0:T(8,128)(2,1)S(1)}, bf16[160,2048]{1,0:T(8,128)(2,1)}, u32[]{:S(2)}, u32[]{:S(2)}) collective-permute-start(bf16[160,2048]{1,0:T(8,128)(2,1)S(1)} %slice.558), channel_id=1, source_target_pairs={{0,1},{1,0},{2,3},{3,2},{4,5},{5,4},{6,7},{7,6},{8,9},{9,8},{10,11... | collective-permute-start | bytes 1966088 | tf_op jit(solution)/shard_map/ppermute | solution.py:92
  607.2 126.1 %collective-permute-start.92 = (bf16[2,512,2048]{2,1,0:T(8,128)(2,1)}, bf16[2,512,2048]{2,1,0:T(8,128)(2,1)}, u32[]{:S(2)}, u32[]{:S(2)}) collective-permute-start(bf16[2,512,2048]{2,1,0:T(8,128)(2,1)} %get-tuple-element.142), channel_id=1, source_target_pairs={{0,2},{2,0},{4,6},{6,4},{8,10},{10,8},{12,14},{14,12},{16,18},{18,... | collective-permute-start | bytes 12582920 | tf_op jit(solution)/shard_map/ppermute | solution.py:96
  607.3 63.6 %collective-permute-start.26 = (bf16[352,2048]{1,0:T(8,128)(2,1)}, bf16[352,2048]{1,0:T(8,128)(2,1)S(1)}, u32[]{:S(2)}, u32[]{:S(2)}) collective-permute-start(bf16[352,2048]{1,0:T(8,128)(2,1)} %collective-permute-done.24.refs_0_), channel_id=1, source_target_pairs={{0,2},{2,0},{4,6},{6,4},{8,10},{10,8},{12,14},{14,12},{16,18},{18,... | collective-permute-start | bytes 4325384 | tf_op jit(solution)/shard_map/ppermute | solution.py:96
  607.8 63.0 %collective-permute-start.27 = (bf16[160,2048]{1,0:T(8,128)(2,1)}, bf16[160,2048]{1,0:T(8,128)(2,1)S(1)}, u32[]{:S(2)}, u32[]{:S(2)}) collective-permute-start(bf16[160,2048]{1,0:T(8,128)(2,1)} %collective-permute-done.25.refs_1_), channel_id=1, source_target_pairs={{0,2},{2,0},{4,6},{6,4},{8,10},{10,8},{12,14},{14,12},{16,18},{18,... | collective-permute-start | bytes 1966088 | tf_op jit(solution)/shard_map/ppermute | solution.py:96
  670.8 110.4 %collective-permute-start.89 = (bf16[2,512,2048]{2,1,0:T(8,128)(2,1)}, bf16[2,512,2048]{2,1,0:T(8,128)(2,1)}, u32[]{:S(2)}, u32[]{:S(2)}) collective-permute-start(bf16[2,512,2048]{2,1,0:T(8,128)(2,1)} %get-tuple-element.137), channel_id=1, source_target_pairs={{0,2},{2,0},{4,6},{6,4},{8,10},{10,8},{12,14},{14,12},{16,18},{18,... | collective-permute-start | bytes 12582920 | tf_op jit(solution)/shard_map/ppermute | solution.py:96
  733.0 85.1 %collective-permute-start.86 = (bf16[2,512,2048]{2,1,0:T(8,128)(2,1)}, bf16[2,512,2048]{2,1,0:T(8,128)(2,1)}, u32[]{:S(2)}, u32[]{:S(2)}) collective-permute-start(bf16[2,512,2048]{2,1,0:T(8,128)(2,1)} %get-tuple-element.132), channel_id=1, source_target_pairs={{0,2},{2,0},{4,6},{6,4},{8,10},{10,8},{12,14},{14,12},{16,18},{18,... | collective-permute-start | bytes 12582920 | tf_op jit(solution)/shard_map/ppermute | solution.py:96
  838.6 86.0 %collective-permute-start.76 = (bf16[2,512,2048]{2,1,0:T(8,128)(2,1)}, bf16[2,512,2048]{2,1,0:T(8,128)(2,1)}, u32[]{:S(2)}, u32[]{:S(2)}) collective-permute-start(bf16[2,512,2048]{2,1,0:T(8,128)(2,1)} %get-tuple-element.122), channel_id=1, source_target_pairs={{0,2},{2,0},{4,6},{6,4},{8,10},{10,8},{12,14},{14,12},{16,18},{18,... | collective-permute-start | bytes 12582920 | tf_op jit(solution)/shard_map/ppermute | solution.py:96
  879.1 95.6 %collective-permute-start.59 = (bf16[2,512,2048]{2,1,0:T(8,128)(2,1)}, bf16[2,512,2048]{2,1,0:T(8,128)(2,1)}, u32[]{:S(2)}, u32[]{:S(2)}) collective-permute-start(bf16[2,512,2048]{2,1,0:T(8,128)(2,1)} %get-tuple-element.114), channel_id=1, source_target_pairs={{0,2},{2,0},{4,6},{6,4},{8,10},{10,8},{12,14},{14,12},{16,18},{18,... | collective-permute-start | bytes 12582920 | tf_op jit(solution)/shard_map/ppermute | solution.py:96
  915.8 275.3 %collective-permute-start.19 = (bf16[2,512,2048]{2,1,0:T(8,128)(2,1)}, bf16[2,512,2048]{2,1,0:T(8,128)(2,1)}, u32[]{:S(2)}, u32[]{:S(2)}) collective-permute-start(bf16[2,512,2048]{2,1,0:T(8,128)(2,1)} %get-tuple-element.98), channel_id=1, source_target_pairs={{0,2},{2,0},{4,6},{6,4},{8,10},{10,8},{12,14},{14,12},{16,18},{18,... | collective-permute-start | bytes 12582920 | tf_op jit(solution)/shard_map/ppermute | solution.py:96
  924.5 592.5 %reduce-scatter.5.cloned.1.call-start = ((), (), s32[]{:S(2)}) async-start(), calls=%async_computation.6 | async-start | bytes 4456448 | tf_op jit(solution)/shard_map/reduce_scatter | solution.py:847
  946.4 231.3 %collective-permute-start.42 = (bf16[2,512,2048]{2,1,0:T(8,128)(2,1)}, bf16[2,512,2048]{2,1,0:T(8,128)(2,1)}, u32[]{:S(2)}, u32[]{:S(2)}) collective-permute-start(bf16[2,512,2048]{2,1,0:T(8,128)(2,1)} %get-tuple-element.106), channel_id=1, source_target_pairs={{0,2},{2,0},{4,6},{6,4},{8,10},{10,8},{12,14},{14,12},{16,18},{18,... | collective-permute-start | bytes 12582920 | tf_op jit(solution)/shard_map/ppermute | solution.py:96
  973.0 213.1 %collective-permute-start.78 = (bf16[352,2048]{1,0:T(8,128)(2,1)}, bf16[352,2048]{1,0:T(8,128)(2,1)}, u32[]{:S(2)}, u32[]{:S(2)}) collective-permute-start(bf16[352,2048]{1,0:T(8,128)(2,1)} %fusion.95), channel_id=1, source_target_pairs={{0,4},{2,6},{4,0},{6,2},{8,12},{10,14},{12,8},{14,10},{16,20},{18,... | collective-permute-start | bytes 4325384 | tf_op jit(solution)/shard_map/ppermute | solution.py:96
  980.0 195.8 %collective-permute-start.60 = (bf16[2,160,2048]{2,1,0:T(8,128)(2,1)}, bf16[2,160,2048]{2,1,0:T(8,128)(2,1)}, u32[]{:S(2)}, u32[]{:S(2)}) collective-permute-start(bf16[2,160,2048]{2,1,0:T(8,128)(2,1)} %slice.573), channel_id=1, source_target_pairs={{0,1},{1,0},{2,3},{3,2},{4,5},{5,4},{6,7},{7,6},{8,9},{9,8},{10,11... | collective-permute-start | bytes 3932168 | tf_op jit(solution)/shard_map/ppermute | solution.py:92
  1024.3 494.8 %reduce-scatter.7.cloned.1.call-start = ((), (), s32[]{:S(2)}) async-start(), calls=%async_computation.7 | async-start | bytes 11698176
  1305.2 113.6 %all-to-all-start.2 = ((bf16[16,3,88,128]{3,2,1,0:T(8,128)(2,1)}), bf16[16,3,88,128]{3,2,1,0:T(8,128)(2,1)}, u32[]{:S(2)}, u32[]{:S(2)}) async-start(bf16[16,3,88,128]{3,2,1,0:T(8,128)(2,1)} %copy.248), calls=%async_computation.3 | async-start | bytes 2162688 | tf_op jit(solution)/shard_map/all_to_all | solution.py:755
  (211 other events, 4696.4 us)
Sparse Core Ops, SparseCore 0:
  13.5 178.0 all-gather.2
  1024.4 73.6 reduce-scatter.4
  1174.2 199.6 reduce-scatter.6

commit v2 on v1

--- a/solution.py
+++ b/solution.py
@@ -86,6 +86,8 @@
 UNIQUE = 160
 SENT = COMMON + UNIQUE
 SHARED_PAD = 128
+QUERY_COLUMNS = 1536
+SCORE_SCALE = (NOPE + ROPE) ** (-0.5)
 
 
 def swap_cols(values):
@@ -134,37 +136,86 @@
     )
 
 
-def spread_rows(rows):
-    planes = []
-    current = rows
-    for plane in range(PLANES):
-        if plane > 0:
-            current = turn_planes(current)
-        across = swap_rows(current, 2)
-        held = [
-            (current, swap_cols(current[COMMON:])),
-            (across, swap_cols(across[COMMON:])),
-        ]
-        family = []
-        for sent, unique in held:
-            family.append((sent, unique))
-            family.append((swap_rows(sent, 1), swap_rows(unique, 1)))
-        planes.append(family)
-    return planes
-
-
-def collect_rows(planes):
-    moving = None
-    for plane in (1, 2, 3, 0):
-        sibling, mine = planes[plane]
-        total = mine + swap_rows(sibling, 1)
-        unique = swap_cols(total[:, SENT:])
-        total = jnp.concatenate([total[:, :COMMON], total[:, COMMON:SENT] + unique], axis=1)
-        total = total[0] + swap_rows(total[1], 2)
-        if moving is not None:
-            total = total + turn_planes(moving)
-        moving = total
-    return moving
+def together(*values):
+    return lax.optimization_barrier(values)
+
+
+def after(values, *others):
+    return lax.optimization_barrier((values, *others))[0]
+
+
+def batch(values):
+    starts = [0]
+    for value in values:
+        starts.append(starts[-1] + value.shape[0])
+    return jnp.concatenate(values, axis=0), starts[:-1]
+
+
+class Spread:
+    def __init__(self, rows):
+        self.held = {(0, 0): rows}
+        self.unique = {}
+        self.sibling = {}
+
+    def turn(self, plane):
+        return turn_planes(self.held[plane - 1, 0])
+
+    def cross(self, plane):
+        return swap_rows(self.held[plane, 0], 2)
+
+    def sent(self, *keys):
+        return [self.held[key][COMMON:] for key in keys]
+
+    def got(self, array, starts, *keys):
+        for key, start in zip(keys, starts):
+            self.unique[key] = (array, start)
+
+    def passed(self, *keys):
+        pieces = []
+        for key in keys:
+            if key[2]:
+                array, start = self.unique[key[:2]]
+                pieces.append(array[start : start + UNIQUE])
+            else:
+                pieces.append(self.held[key[:2]])
+        return pieces
+
+    def taken(self, array, starts, *keys):
+        for key, start in zip(keys, starts):
+            self.sibling[key] = (array, start)
+
+    def family(self, plane):
+        result = []
+        for across in (0, 1):
+            result.append(((self.held[plane, across], 0), self.unique[plane, across]))
+            result.append((self.sibling[plane, across, 0], self.sibling[plane, across, 1]))
+        return result
+
+
+def add_unique(rest, unique, across):
+    return jnp.concatenate([rest[across, :COMMON], rest[across, COMMON:] + unique[across]], axis=0)
+
+
+def column_pieces(weight, bounds):
+    return jnp.concatenate([weight[:, a:b] for a, b in bounds], axis=1)
+
+
+def pair_columns(weight):
+    head = NOPE + ROPE
+    bounds = []
+    for start in range(0, weight.shape[1], 2 * head):
+        bounds += [(start, start + NOPE), (start + head, start + head + NOPE)]
+        bounds += [(start + NOPE, start + head), (start + head + NOPE, start + 2 * head)]
+    return column_pieces(weight, bounds)
+
+
+def head_columns(weight):
+    bounds = []
+    for start in range(0, weight.shape[1], 2 * (NOPE + ROPE)):
+        turned = start + 2 * NOPE
+        bounds += [(start, start + NOPE), (turned, turned + ROPE)]
+        bounds += [(start + NOPE, turned), (turned + ROPE, turned + 2 * ROPE)]
+    return column_pieces(weight, bounds)
 
 
 def merge_rows(own, received, first):
@@ -186,6 +237,10 @@
     return pltpu.CompilerParams(vmem_limit_bytes=VMEM_BYTES, **extra)
 
 
+def short_cost():
+    return pl.CostEstimate(flops=10**9, bytes_accessed=10**6, transcendentals=0)
+
+
 def dot_last(left, right):
     return lax.dot_general(
         left, right, (((1,), (1,)), ((), ())), preferred_element_type=jnp.float32
@@ -213,21 +268,39 @@
     return jnp.concatenate(one, axis=0)
 
 
-def start_rows(pieces, held, sems):
+def row_copies(refs, starts, held, sems, f):
+    return [
+        pltpu.make_async_copy(
+            refs[2 * f].at[pl.ds(starts[2 * f], SENT)],
+            held.at[f, pl.ds(0, SENT)],
+            sems.at[f, 0],
+        ),
+        pltpu.make_async_copy(
+            refs[2 * f + 1].at[pl.ds(starts[2 * f + 1], UNIQUE)],
+            held.at[f, pl.ds(SENT, UNIQUE)],
+            sems.at[f, 1],
+        ),
+    ]
+
+
+def start_rows(refs, starts, held, sems):
     for f in range(FAMILIES):
-        pltpu.make_async_copy(pieces[2 * f], held.at[f, pl.ds(0, SENT)], sems.at[f, 0]).start()
-        pltpu.make_async_copy(
-            pieces[2 * f + 1], held.at[f, pl.ds(SENT, UNIQUE)], sems.at[f, 1]
-        ).start()
-
-
-def wait_rows(pieces, held, sems, f):
-    pltpu.make_async_copy(pieces[0], held.at[f, pl.ds(0, SENT)], sems.at[f, 0]).wait()
-    pltpu.make_async_copy(pieces[1], held.at[f, pl.ds(SENT, UNIQUE)], sems.at[f, 1]).wait()
+        for copy in row_copies(refs, starts, held, sems, f):
+            copy.start()
+
+
+def wait_rows(refs, starts, held, sems, f):
+    for family in range(FAMILIES):
+
+        @pl.when(f == family)
+        def _():
+            for copy in row_copies(refs, starts, held, sems, family):
+                copy.wait()
 
 
 def pick_grads(plane, codes, last, capacity):
-    pieces = [piece for family in plane for piece in family]
+    pieces = [piece[0] for family in plane for piece in family]
+    starts = [piece[1] for family in plane for piece in family]
     tokens = SENT + UNIQUE
     width = last.shape[1]
     pad = last.shape[0]
@@ -239,9 +312,9 @@
 
         @pl.when(f == 0)
         def _():
-            start_rows(rows_in, held, sems)
-
-        wait_rows(rows_in, held, sems, f)
+            start_rows(rows_in, starts, held, sems)
+
+        wait_rows(rows_in, starts, held, sems, f)
         rows = held[f]
         picks = as_picks(slot_matches(codes_ref, capacity))
         taken = dot_plain(picks, rows).astype(jnp.bfloat16)
@@ -269,17 +342,15 @@
             pltpu.SemaphoreType.DMA((FAMILIES, 2)),
         ],
         compiler_params=kernel_params(),
-        cost_estimate=pl.CostEstimate(
-            flops=FAMILIES * 2 * tokens * width * (EXP_DEV * capacity + 2 * pad),
-            bytes_accessed=FAMILIES * tokens * width * 4,
-            transcendentals=0,
-        ),
+        cost_estimate=short_cost(),
     )(*pieces, codes, last)
 
 
 def pick_rows(plane, grad_plane, codes, router, pair, hidden_grads, capacity):
-    pieces = [piece for family in plane for piece in family]
-    grad_pieces = [piece for family in grad_plane for piece in family]
+    pieces = [piece[0] for family in plane for piece in family]
+    starts = [piece[1] for family in plane for piece in family]
+    grad_pieces = [piece[0] for family in grad_plane for piece in family]
+    grad_starts = [piece[1] for family in grad_plane for piece in family]
     tokens = SENT + UNIQUE
     width = pair.shape[1]
     pad = pair.shape[0] // 2
@@ -294,11 +365,11 @@
 
         @pl.when(f == 0)
         def _():
-            start_rows(rows_in, held, sems)
-            start_rows(grads_in, held_grads, grad_sems)
+            start_rows(rows_in, starts, held, sems)
+            start_rows(grads_in, grad_starts, held_grads, grad_sems)
             grad_ref[...] = jnp.zeros_like(grad_ref)
 
-        wait_rows(rows_in, held, sems, f)
+        wait_rows(rows_in, starts, held, sems, f)
         rows = held[f]
         matches = slot_matches(codes_ref, capacity)
         taken = dot_plain(as_picks(matches), rows).astype(jnp.bfloat16)
@@ -324,7 +395,7 @@
         hidden_ref[0] = hidden
         back_ref[0] = back
         grad_ref[: 2 * pad] += dot_first(back, rows)
-        wait_rows(grads_in, held_grads, grad_sems, f)
+        wait_rows(grads_in, grad_starts, held_grads, grad_sems, f)
         grad_ref[2 * pad :] += dot_first(hidden, held_grads[f])
 
     return pl.pallas_call(
@@ -358,11 +429,7 @@
             pltpu.SemaphoreType.DMA((FAMILIES, 2)),
         ],
         compiler_params=kernel_params(),
-        cost_estimate=pl.CostEstimate(
-            flops=FAMILIES * 2 * tokens * width * (EXP_DEV * capacity + 7 * pad),
-            bytes_accessed=FAMILIES * tokens * width * 6,
-            transcendentals=FAMILIES * tokens * 4 * pad,
-        ),
+        cost_estimate=short_cost(),
     )(*pieces, *grad_pieces, codes, router, pair, hidden_grads)
 
 
@@ -424,85 +491,279 @@
             jax.ShapeDtypeStruct((count, slots, 128), jnp.float32),
         ],
         compiler_params=kernel_params(),
-        cost_estimate=pl.CostEstimate(
-            flops=12 * count * slots * units * width,
-            bytes_accessed=count * width * (6 * units + 8 * slots),
-            transcendentals=count * slots * units,
-        ),
+        cost_estimate=short_cost(),
     )(slot_rows, slot_grads, gates, expert_gate, expert_up, expert_down)
 
 
-def sum_tokens(values, codes, shared, matrix, gate_grads, capacity):
+def sum_tokens(values, codes, shared, matrix, capacity, core, received=None, gate_grads=None):
     tokens = codes.shape[2]
     width = values.shape[2]
     inner = matrix.shape[0]
+    with_rows = received is not None
     with_gates = gate_grads is not None
-
-    def family(i):
-        return 2 * (i % 2) + 1 - i // 2
 
     def body(*refs):
         values_ref, codes_ref, shared_ref, matrix_ref = refs[:4]
-        sibling_ref, mine_ref = refs[4 + with_gates : 6 + with_gates]
-        i = pl.program_id(0)
+        outs = refs[4 + with_rows + with_gates :]
         matches = slot_matches(codes_ref, capacity)
         rows = values_ref[...].reshape(EXP_DEV * capacity, width)
         total = dot_first(as_picks(matches), rows)
         total = total + dot_plain(shared_ref[0], matrix_ref[...])
-        total = total.astype(jnp.bfloat16)
-
-        @pl.when(i < 2)
-        def _():
-            sibling_ref[0] = total
-
-        @pl.when(i >= 2)
-        def _():
-            mine_ref[0] = total
-
+        if with_rows:
+            total = (total + refs[4][0].astype(jnp.float32)).astype(jnp.bfloat16)
+            outs[0][0] = total[:SENT]
+            outs[1][0] = total[SENT:]
+        else:
+            outs[0][0] = total.astype(jnp.bfloat16)
         if with_gates:
-            gate_grads_ref, dense_ref = refs[4], refs[7]
             dense = [
                 jnp.sum(
-                    jnp.where(matches[j], gate_grads_ref[j][:, :1], 0.0), axis=0, keepdims=True
+                    jnp.where(matches[j], refs[4 + with_rows][j][:, :1], 0.0),
+                    axis=0,
+                    keepdims=True,
                 )
                 for j in range(EXP_DEV)
             ]
-            dense_ref[0] = jnp.concatenate(dense + [jnp.zeros((4, tokens), jnp.float32)], axis=0)
+            outs[-1][0] = jnp.concatenate(dense + [jnp.zeros((4, tokens), jnp.float32)], axis=0)
 
     in_specs = [
-        pl.BlockSpec((EXP_DEV, capacity, width), lambda i: (0, family(i), 0)),
-        pl.BlockSpec((1, 8, tokens), lambda i: (family(i), 0, 0)),
-        pl.BlockSpec((1, tokens, inner), lambda i: (family(i), 0, 0)),
+        pl.BlockSpec((EXP_DEV, capacity, width), lambda i: (0, 2 * i + core, 0)),
+        pl.BlockSpec((1, 8, tokens), lambda i: (2 * i + core, 0, 0)),
+        pl.BlockSpec((1, tokens, inner), lambda i: (2 * i + core, 0, 0)),
         pl.BlockSpec((inner, width), lambda i: (0, 0)),
     ]
-    out_specs = [
-        pl.BlockSpec((1, tokens, width), lambda i: (jnp.minimum(i, 1), 0, 0)),
-        pl.BlockSpec((1, tokens, width), lambda i: (jnp.maximum(i - 2, 0), 0, 0)),
-    ]
-    out_shape = [jax.ShapeDtypeStruct((2, tokens, width), jnp.bfloat16)] * 2
     operands = [values, codes, shared, matrix]
+    pieces = [tokens]
+    if with_rows:
+        in_specs.append(pl.BlockSpec((1, tokens, width), lambda i: (i, 0, 0)))
+        operands.append(received)
+        pieces = [SENT, UNIQUE]
+    out_specs = [pl.BlockSpec((1, piece, width), lambda i: (i, 0, 0)) for piece in pieces]
+    out_shape = [jax.ShapeDtypeStruct((2, piece, width), jnp.bfloat16) for piece in pieces]
     if with_gates:
-        in_specs.append(pl.BlockSpec((EXP_DEV, capacity, 128), lambda i: (0, family(i), 0)))
-        out_specs.append(pl.BlockSpec((1, 8, tokens), lambda i: (family(i), 0, 0)))
-        out_shape.append(jax.ShapeDtypeStruct((FAMILIES, 8, tokens), jnp.float32))
+        in_specs.append(pl.BlockSpec((EXP_DEV, capacity, 128), lambda i: (0, 2 * i + core, 0)))
         operands.append(gate_grads)
+        out_specs.append(pl.BlockSpec((1, 8, tokens), lambda i: (i, 0, 0)))
+        out_shape.append(jax.ShapeDtypeStruct((2, 8, tokens), jnp.float32))
     return pl.pallas_call(
         body,
-        grid=(FAMILIES,),
+        grid=(2,),
         in_specs=in_specs,
         out_specs=out_specs,
         out_shape=out_shape,
         compiler_params=kernel_params(),
-        cost_estimate=pl.CostEstimate(
-            flops=FAMILIES * 2 * tokens * width * (EXP_DEV * capacity + inner),
-            bytes_accessed=FAMILIES * width * (4 * tokens + 2 * EXP_DEV * capacity),
-            transcendentals=0,
+        cost_estimate=short_cost(),
+    )(*operands)
+
+
+def pack_weights(query_weight, expand_weight, output_weight, latent_weight, router_weight, routes):
+    block = latent_weight.shape[0]
+    share = expand_weight.shape[0]
+    widths = [
+        query_weight.shape[1],
+        expand_weight.shape[1] * share // block,
+        output_weight.shape[0],
+        latent_weight.shape[1],
+        router_weight.shape[1],
+        routes.shape[1],
+    ]
+    columns = (sum(widths) + 127) // 128 * 128
+
+    def body(query_ref, expand_ref, output_ref, latent_ref, router_ref, routes_ref, out_ref):
+        out_ref[:, : widths[0]] = pair_columns(query_ref[...])
+        start = widths[0]
+        for i in range(block // share):
+            out_ref[share * i : share * (i + 1), start : start + widths[1]] = expand_ref[
+                :, widths[1] * i : widths[1] * (i + 1)
+            ]
+        start += widths[1]
+        out_ref[:, start : start + widths[2]] = output_ref[...].T
+        start += widths[2]
+        out_ref[:, start : start + widths[3] + widths[4]] = jnp.concatenate(
+            [latent_ref[...], router_ref[...]], axis=1
+        )
+        start += widths[3] + widths[4]
+        last = jnp.zeros((block, columns - start - widths[5]), jnp.bfloat16)
+        out_ref[:, start:] = jnp.concatenate([routes_ref[...], last], axis=1)
+
+    return pl.pallas_call(
+        body,
+        out_shape=jax.ShapeDtypeStruct((block, columns), jnp.bfloat16),
+        compiler_params=kernel_params(),
+        cost_estimate=short_cost(),
+    )(query_weight, expand_weight, output_weight, latent_weight, router_weight, routes)
+
+
+def unpack_grads(output, wide, narrow, widths):
+    block = wide.shape[0]
+    query_width, expand_width, latent_width = widths
+    parts = 4
+    share = block // parts
+
+    def body(sum_ref, wide_ref, narrow_ref, output_ref, query_ref, expand_ref, latent_ref, router_ref):
+        output_ref[...] = sum_ref[...].astype(jnp.float32).T
+        query_ref[...] = head_columns(wide_ref[:, :query_width]).astype(jnp.float32)
+        for i in range(parts):
+            expand_ref[:, expand_width * i : expand_width * (i + 1)] = wide_ref[
+                share * i : share * (i + 1), query_width:
+            ].astype(jnp.float32)
+        latent_ref[...] = narrow_ref[:, :latent_width].astype(jnp.float32)
+        router_ref[...] = narrow_ref[:, latent_width:].astype(jnp.float32)
+
+    shapes = [
+        (output.shape[1], block),
+        (block, query_width),
+        (share, expand_width * parts),
+        (block, latent_width),
+        (block, narrow.shape[1] - latent_width),
+    ]
+    return pl.pallas_call(
+        body,
+        out_shape=[jax.ShapeDtypeStruct(shape, jnp.float32) for shape in shapes],
+        compiler_params=kernel_params(),
+        cost_estimate=short_cost(),
+    )(output, wide, narrow)
+
+
+def block_grads(places, left, right, tile, core, turned=None, expanded=None, received=None):
+    count, width = left.shape
+    block = width // (4 * PLANES)
+    blocks = 2 * PLANES
+    columns = right.shape[1]
+    steps = columns // tile
+    with_expand = turned is not None
+    share = turned.shape[0] // (4 * PLANES) if with_expand else 0
+    quarter = expanded.shape[1] // steps if with_expand else 0
+
+    def body(places_ref, left_ref, right_ref, *refs):
+        held = refs[-2]
+        held_turned = refs[-1]
+        out_ref = refs[-3]
+        step = pl.program_id(0)
+
+        @pl.when(step == 0)
+        def _():
+            for i in range(blocks):
+                place = places_ref[2 * i + core]
+                start = pl.multiple_of(place * block, block)
+                held[:, block * i : block * (i + 1)] = left_ref[:, pl.ds(start, block)]
+                if with_expand:
+                    start = pl.multiple_of(place * share, share)
+                    held_turned[share * i : share * (i + 1)] = refs[0][pl.ds(start, share)]
+
+        part = dot_first(held[...], right_ref[...]).reshape(blocks, block, tile)
+        lanes = pl.ds(pl.multiple_of(step * tile, 128), tile)
+        if received is not None:
+            got_ref = refs[-4]
+            part = part + got_ref[:, :, lanes].astype(jnp.float32)
+        out_ref[:, :, lanes] = part.astype(jnp.bfloat16)
+        if with_expand:
+            part = dot_plain(held_turned[...], refs[1][...]).reshape(blocks, share, quarter)
+            lines = pl.ds(pl.multiple_of(step * share, share), share)
+            if received is not None:
+                part = part + got_ref[:, lines, columns:].astype(jnp.float32)
+            out_ref[:, lines, columns:] = part.astype(jnp.bfloat16)
+
+    whole = lambda shape: pl.BlockSpec(shape, lambda h, places_ref: (0,) * len(shape))
+    in_specs = [
+        whole(left.shape),
+        pl.BlockSpec((count, tile), lambda h, places_ref: (0, h)),
+    ]
+    operands = [left, right]
+    if with_expand:
+        in_specs += [
+            whole(turned.shape),
+            pl.BlockSpec((count, quarter), lambda h, places_ref: (0, h)),
+        ]
+        operands += [turned, expanded]
+    shape = (blocks, block, columns + quarter)
+    if received is not None:
+        in_specs.append(whole(shape))
+        operands.append(received)
+    return pl.pallas_call(
+        body,
+        grid_spec=pltpu.PrefetchScalarGridSpec(
+            num_scalar_prefetch=1,
+            grid=(steps,),
+            in_specs=in_specs,
+            out_specs=whole(shape),
+            scratch_shapes=[
+                pltpu.VMEM((count, blocks * block), jnp.bfloat16),
+                pltpu.VMEM((max(blocks * share, 16), count), jnp.bfloat16),
+            ],
         ),
-    )(*operands)
-
-
-def expert_weight_grads(rows, grads, gate_backs, up_backs, hiddens):
-    count, slots, width = rows[0].shape
+        out_shape=jax.ShapeDtypeStruct(shape, jnp.bfloat16),
+        compiler_params=kernel_params(),
+        cost_estimate=short_cost(),
+    )(places, *operands)
+
+
+def narrow_grads(places, normed, latent_back, normed_two, logit_grads, core):
+    count, width = normed.shape
+    block = width // (4 * PLANES)
+    widths = [latent_back.shape[1], logit_grads.shape[1]]
+
+    def body(places_ref, normed_ref, two_ref, latent_ref, logit_ref, out_ref):
+        parts = [
+            dot_first(normed_ref[...], latent_ref[...]),
+            dot_first(two_ref[...], logit_ref[...]),
+        ]
+        out_ref[0] = jnp.concatenate(parts, axis=1).astype(jnp.bfloat16)
+
+    piece = pl.BlockSpec((count, block), lambda i, places_ref: (0, places_ref[2 * i + core]))
+    whole = lambda columns: pl.BlockSpec((count, columns), lambda i, places_ref: (0, 0))
+    return pl.pallas_call(
+        body,
+        grid_spec=pltpu.PrefetchScalarGridSpec(
+            num_scalar_prefetch=1,
+            grid=(2 * PLANES,),
+            in_specs=[piece, piece, whole(widths[0]), whole(widths[1])],
+            out_specs=pl.BlockSpec((1, block, sum(widths)), lambda i, places_ref: (i, 0, 0)),
+        ),
+        out_shape=jax.ShapeDtypeStruct((2 * PLANES, block, sum(widths)), jnp.bfloat16),
+        compiler_params=kernel_params(),
+        cost_estimate=short_cost(),
+    )(places, normed, normed_two, latent_back, logit_grads)
+
+
+def assemble(blocks, places):
+    count = len(blocks)
+
+    def body(places_ref, *refs):
+        out, held, sems, out_sems = refs[count:]
+        arrivals = [
+            pltpu.make_async_copy(refs[i], held.at[i], sems.at[i]) for i in range(count)
+        ]
+        leaving = [
+            pltpu.make_async_copy(held.at[i], out.at[places_ref[i]], out_sems.at[i])
+            for i in range(count)
+        ]
+        for copy in arrivals:
+            copy.start()
+        for i in range(count):
+            arrivals[i].wait()
+            leaving[i].start()
+        for copy in leaving:
+            copy.wait()
+
+    return pl.pallas_call(
+        body,
+        in_specs=[pl.BlockSpec(memory_space=pltpu.SMEM)]
+        + [pl.BlockSpec(memory_space=pl.ANY)] * len(blocks),
+        out_specs=pl.BlockSpec(memory_space=pl.ANY),
+        out_shape=jax.ShapeDtypeStruct((len(blocks),) + blocks[0].shape, blocks[0].dtype),
+        scratch_shapes=[
+            pltpu.VMEM((count,) + blocks[0].shape, blocks[0].dtype),
+            pltpu.SemaphoreType.DMA((count,)),
+            pltpu.SemaphoreType.DMA((count,)),
+        ],
+        compiler_params=kernel_params(),
+        cost_estimate=short_cost(),
+    )(places, *blocks)
+
+
+def expert_weight_grads(rows, grads, gate_backs, up_backs, hiddens, begin, count, earlier):
+    experts, slots, width = rows[0].shape
     units = hiddens[0].shape[2]
     tile = 512
     planes = len(rows)
@@ -513,7 +774,7 @@
         gate_in = refs[2 * planes : 3 * planes]
         up_in = refs[3 * planes : 4 * planes]
         hidden_in = refs[4 * planes : 5 * planes]
-        gate_ref, up_ref, down_ref = refs[5 * planes :]
+        gate_ref, up_ref, down_ref = refs[-3:]
         for left, right, out in (
             (gate_in, rows_in, gate_ref),
             (up_in, rows_in, up_ref),
@@ -524,22 +785,262 @@
                 total = total + dot_first(left[p][0], right[p][0])
             out[0] = total
 
-    wide = pl.BlockSpec((1, slots, tile), lambda j, d: (j, 0, d))
-    inner = pl.BlockSpec((1, slots, units), lambda j, d: (j, 0, 0))
-    result = pl.BlockSpec((1, units, tile), lambda j, d: (j, 0, d))
+    wide = pl.BlockSpec((1, slots, tile), lambda j, d: (begin + j, 0, d))
+    inner = pl.BlockSpec((1, slots, units), lambda j, d: (begin + j, 0, 0))
+    result = pl.BlockSpec((1, units, tile), lambda j, d: (begin + j, 0, d))
     return pl.pallas_call(
         body,
         grid=(count, width // tile),
-        in_specs=[wide] * (2 * planes) + [inner] * (3 * planes),
+        in_specs=[wide] * (2 * planes)
+        + [inner] * (3 * planes)
+        + [pl.BlockSpec(memory_space=pl.ANY)] * len(earlier),
         out_specs=[result] * 3,
-        out_shape=[jax.ShapeDtypeStruct((count, units, width), jnp.float32)] * 3,
+        out_shape=[jax.ShapeDtypeStruct((experts, units, width), jnp.float32)] * 3,
+        input_output_aliases={5 * planes + i: i for i in range(len(earlier))},
         compiler_params=kernel_params(),
-        cost_estimate=pl.CostEstimate(
-            flops=6 * count * planes * slots * units * width,
-            bytes_accessed=count * (12 * units * width + planes * slots * (4 * width + 6 * units)),
-            transcendentals=0,
-        ),
-    )(*rows, *grads, *gate_backs, *up_backs, *hiddens)
+        cost_estimate=short_cost(),
+    )(*rows, *grads, *gate_backs, *up_backs, *hiddens, *earlier)
+
+
+def swap_halves(values):
+    lanes = lax.broadcasted_iota(jnp.int32, values.shape, 1)
+    return jnp.where(lanes % 64 < 32, pltpu.roll(values, 96, 1), pltpu.roll(values, 32, 1))
+
+
+def masked_weights(segment_column, segment_line, query, keys, rope, head_rope):
+    count = query.shape[0]
+    raw = dot_last(query, keys) + dot_last(rope, head_rope)
+    after_key = lax.broadcasted_iota(jnp.int32, (count, count), 0) >= lax.broadcasted_iota(
+        jnp.int32, (count, count), 1
+    )
+    allowed = (segment_column == segment_line) & after_key
+    scores = jnp.where(allowed, raw * SCORE_SCALE, -1e30)
+    exponent = jnp.exp(scores - jnp.max(scores, axis=1, keepdims=True))
+    return exponent / jnp.sum(exponent, axis=1, keepdims=True)
+
+
+def head_ropes(key_rope):
+    zeros = jnp.zeros_like(key_rope)
+    return [
+        jnp.concatenate([key_rope, zeros], axis=1),
+        jnp.concatenate([zeros, key_rope], axis=1),
+    ]
+
+
+def attend(normed, latent_normed, ropes, turns, segments, dense):
+    count, width = normed.shape
+    rows, block, columns = dense.shape
+    pairs = QUERY_COLUMNS // 384
+    rank = latent_normed.shape[1]
+    share = rank // rows
+    flat = dense.reshape(rows * block, columns)
+    quarters = dense.reshape(rows, block // share, share, columns)
+
+    def body(
+        normed_ref,
+        latent_ref,
+        rope0_ref,
+        rope1_ref,
+        cosine_ref,
+        sine_ref,
+        column_ref,
+        line_ref,
+        query_weight_ref,
+        expand_ref,
+        output_ref,
+        query_ref,
+        keys_ref,
+        mixed_ref,
+        attended_ref,
+        total,
+    ):
+        step = pl.program_id(0)
+        query = dot_plain(normed_ref[...], query_weight_ref[...])
+        rope = query[:, 256:]
+        rope = rope * cosine_ref[...] + swap_halves(rope) * sine_ref[...]
+        query = jnp.concatenate([query[:, :256], rope], axis=1).astype(jnp.bfloat16)
+        expand = expand_ref[...].reshape(rank, 512)
+        keys = dot_plain(latent_ref[...], expand).astype(jnp.bfloat16)
+        query_ref[...] = query
+        keys_ref[...] = keys
+        mixed = []
+        for head, rope_ref in enumerate((rope0_ref, rope1_ref)):
+            weights = masked_weights(
+                column_ref[:, :1],
+                line_ref[:1],
+                query[:, 128 * head : 128 * head + 128],
+                keys[:, 256 * head : 256 * head + 128],
+                query[:, 256:],
+                rope_ref[...],
+            )
+            values = keys[:, 256 * head + 128 : 256 * head + 256]
+            mixed.append(dot_plain(weights.astype(jnp.bfloat16), values).astype(jnp.bfloat16))
+        mixed = jnp.concatenate(mixed, axis=1)
+        mixed_ref[...] = mixed
+        part = dot_last(mixed, output_ref[...])
+
+        @pl.when(step == 0)
+        def _():
+            total[...] = part
+
+        @pl.when(step > 0)
+        def _():
+            total[...] += part
+
+        @pl.when(step == pairs - 1)
+        def _():
+            attended_ref[...] = total[...].astype(jnp.bfloat16)
+
+    whole = lambda shape: pl.BlockSpec(shape, lambda h: (0,) * len(shape))
+    return pl.pallas_call(
+        body,
+        grid=(pairs,),
+        in_specs=[
+            whole((count, width)),
+            whole((count, rank)),
+            whole((count, 128)),
+            whole((count, 128)),
+            whole((count, 128)),
+            whole((count, 128)),
+            whole((count, 128)),
+            whole((8, count)),
+            pl.BlockSpec((width, 384), lambda h: (0, h)),
+            pl.BlockSpec((rows, 1, share, 512), lambda h: (0, h, 0, QUERY_COLUMNS // 512)),
+            pl.BlockSpec((width, 256), lambda h: (0, (QUERY_COLUMNS + 512) // 256 + h)),
+        ],
+        out_specs=[
+            pl.BlockSpec((count, 384), lambda h: (0, h)),
+            pl.BlockSpec((count, 512), lambda h: (0, h)),
+            pl.BlockSpec((count, 256), lambda h: (0, h)),
+            whole((count, width)),
+        ],
+        out_shape=[
+            jax.ShapeDtypeStruct((count, 384 * pairs), jnp.bfloat16),
+            jax.ShapeDtypeStruct((count, 512 * pairs), jnp.bfloat16),
+            jax.ShapeDtypeStruct((count, 256 * pairs), jnp.bfloat16),
+            jax.ShapeDtypeStruct((count, width), jnp.bfloat16),
+        ],
+        scratch_shapes=[pltpu.VMEM((count, width), jnp.float32)],
+        compiler_params=kernel_params(),
+        cost_estimate=short_cost(),
+    )(normed, latent_normed, *ropes, *turns, *segments, flat, quarters, flat)
+
+
+def attend_back(upstream, query, keys, ropes, turns, segments, dense, rank):
+    count, width = upstream.shape
+    rows, block, columns = dense.shape
+    pairs = QUERY_COLUMNS // 384
+    share = rank // rows
+    flat = dense.reshape(rows * block, columns)
+    quarters = dense.reshape(rows, block // share, share, columns)
+
+    def body(
+        upstream_ref,
+        query_ref,
+        keys_ref,
+        rope0_ref,
+        rope1_ref,
+        cosine_ref,
+        sine_ref,
+        column_ref,
+        line_ref,
+        query_weight_ref,
+        expand_ref,
+        output_ref,
+        query_back_ref,
+        keys_back_ref,
+        rope_back_ref,
+        latent_back_ref,
+        input_ref,
+        total,
+    ):
+        step = pl.program_id(0)
+        mixed_back = dot_plain(upstream_ref[...], output_ref[...]).astype(jnp.bfloat16)
+        query = query_ref[...]
+        keys = keys_ref[...]
+        rope = query[:, 256:]
+        lanes = lax.broadcasted_iota(jnp.int32, (count, 128), 1)
+        query_back = []
+        keys_back = []
+        rope_back = 0.0
+        key_rope_back = 0.0
+        for head, rope_ref in enumerate((rope0_ref, rope1_ref)):
+            query_nope = query[:, 128 * head : 128 * head + 128]
+            key_nope = keys[:, 256 * head : 256 * head + 128]
+            values = keys[:, 256 * head + 128 : 256 * head + 256]
+            mixed_head = mixed_back[:, 128 * head : 128 * head + 128]
+            weights = masked_weights(
+                column_ref[:, :1], line_ref[:1], query_nope, key_nope, rope, rope_ref[...]
+            )
+            weight_back = dot_last(mixed_head, values)
+            center = jnp.sum(weight_back * weights, axis=1, keepdims=True)
+            raw_back = (weights * (weight_back - center) * SCORE_SCALE).astype(jnp.bfloat16)
+            query_back.append(dot_plain(raw_back, key_nope))
+            rope_back = rope_back + dot_plain(raw_back, rope_ref[...])
+            keys_back.append(dot_first(raw_back, query_nope))
+            keys_back.append(dot_first(weights.astype(jnp.bfloat16), mixed_head))
+            mine = lanes // 64 == head
+            key_rope_back = key_rope_back + jnp.where(mine, dot_first(raw_back, rope), 0.0)
+        rope_back = rope_back * cosine_ref[...] - swap_halves(rope_back) * sine_ref[...]
+        query_back = jnp.concatenate(query_back + [rope_back], axis=1).astype(jnp.bfloat16)
+        keys_back = jnp.concatenate(keys_back, axis=1).astype(jnp.bfloat16)
+        query_back_ref[...] = query_back
+        keys_back_ref[...] = keys_back
+        latent_part = dot_last(keys_back, expand_ref[...].reshape(rank, 512))
+        input_part = dot_last(query_back, query_weight_ref[...])
+
+        @pl.when(step == 0)
+        def _():
+            rope_back_ref[...] = key_rope_back
+            latent_back_ref[...] = latent_part
+            total[...] = input_part
+
+        @pl.when(step > 0)
+        def _():
+            rope_back_ref[...] += key_rope_back
+            latent_back_ref[...] += latent_part
+            total[...] += input_part
+
+        @pl.when(step == pairs - 1)
+        def _():
+            input_ref[...] = total[...].astype(jnp.bfloat16)
+
+    whole = lambda shape: pl.BlockSpec(shape, lambda h: (0,) * len(shape))
+    return pl.pallas_call(
+        body,
+        grid=(pairs,),
+        in_specs=[
+            whole((count, width)),
+            pl.BlockSpec((count, 384), lambda h: (0, h)),
+            pl.BlockSpec((count, 512), lambda h: (0, h)),
+            whole((count, 128)),
+            whole((count, 128)),
+            whole((count, 128)),
+            whole((count, 128)),
+            whole((count, 128)),
+            whole((8, count)),
+            pl.BlockSpec((width, 384), lambda h: (0, h)),
+            pl.BlockSpec((rows, 1, share, 512), lambda h: (0, h, 0, QUERY_COLUMNS // 512)),
+            pl.BlockSpec((width, 256), lambda h: (0, (QUERY_COLUMNS + 512) // 256 + h)),
+        ],
+        out_specs=[
+            pl.BlockSpec((count, 384), lambda h: (0, h)),
+            pl.BlockSpec((count, 512), lambda h: (0, h)),
+            whole((count, 128)),
+            whole((count, rank)),
+            whole((count, width)),
+        ],
+        out_shape=[
+            jax.ShapeDtypeStruct((count, 384 * pairs), jnp.bfloat16),
+            jax.ShapeDtypeStruct((count, 512 * pairs), jnp.bfloat16),
+            jax.ShapeDtypeStruct((count, 128), jnp.float32),
+            jax.ShapeDtypeStruct((count, rank), jnp.float32),
+            jax.ShapeDtypeStruct((count, width), jnp.bfloat16),
+        ],
+        scratch_shapes=[pltpu.VMEM((count, width), jnp.float32)],
+        compiler_params=kernel_params(),
+        cost_estimate=short_cost(),
+    )(upstream, query, keys, *ropes, *turns, *segments, flat, quarters, flat)
 
 
 def on_device(
@@ -568,121 +1069,227 @@
     row_devices = lax.axis_size("row")
     row_place = lax.axis_index("row")
     first = lax.axis_index("col") == 0
-    local_heads = query_weight.shape[1] // (NOPE + ROPE)
     expert_count = EXP_DEV * row_devices
     capacity = 4 * rows_count * TOPK // (3 * expert_count)
-    score_scale = (NOPE + ROPE) ** (-0.5)
     segment_row = segment_ids[0]
     places = jnp.arange(rows_count, dtype=jnp.int32)
 
     steps = jnp.arange(row_devices, dtype=jnp.int32)
-    arrival = (
-        ((row_place // 4 - steps // 4) % 4) * 4 + ((row_place % 4) ^ (steps % 4))
-    ).astype(jnp.int32)
-    place_of = (((row_place // 4 - steps // 4) % 4) * 4 + ((row_place % 4) ^ (steps % 4))).astype(
+    arrival = (((row_place // 4 - steps // 4) % 4) * 4 + ((row_place % 4) ^ (steps % 4))).astype(
         jnp.int32
     )
-
+    block = latent_weight.shape[0]
+    share = expand_weight.shape[0]
+    quarter = expand_weight.shape[1] * share // block
     query_width = query_weight.shape[1]
     latent_width = latent_weight.shape[1]
-    expand_width = expand_weight.shape[1] * expand_weight.shape[0] // latent_weight.shape[0]
-    output_width = output_weight.shape[0]
-    packed = jnp.concatenate(
-        [
-            query_weight,
-            latent_weight,
-            router_weight,
-            expand_weight.reshape(latent_weight.shape[0], expand_width),
-            output_weight.T,
-        ],
-        axis=1,
-    )
-    packed_full = lax.all_gather(packed, "row", axis=0, tiled=True)
-    edge = query_width
-    query_full = packed_full[:, :edge]
-    latent_full = packed_full[:, edge : edge + latent_width]
-    edge += latent_width
-    router_full = packed_full[:, edge : edge + expert_count]
-    edge += expert_count
-    expand_full = packed_full[:, edge : edge + expand_width].reshape(RANK, -1)
-    edge += expand_width
-    output_turned = packed_full[:, edge:]
-
+
+    slab = pack_weights(
+        query_weight,
+        expand_weight,
+        output_weight,
+        latent_weight,
+        router_weight,
+        routes.astype(bf16).reshape(block, -1),
+    )
     shared_share = shared_gate.shape[1] // row_devices
-    shared_packed = jnp.stack([shared_gate.T, shared_up.T, shared_down], axis=0)
+    blocks = {}
+    blocks[0] = slab
+    blocks[4], blocks[2], inputs_other, gains_other = together(
+        turn_planes(slab),
+        swap_rows(slab, 2),
+        swap_cols(inputs),
+        swap_cols(jnp.stack([norm_gain, ffn_gain])),
+    )
+    shared_packed = jnp.stack(
+        [after(shared_gate, inputs_other).T, after(shared_up, inputs_other).T, shared_down], axis=0
+    )
     shared_packed = shared_packed.reshape(3, row_devices, shared_share, -1).transpose(1, 0, 2, 3)
-    shared_here = lax.all_to_all(shared_packed, "row", split_axis=0, concat_axis=0, tiled=True)
-    shared_here = shared_here.transpose(1, 2, 0, 3).reshape(3, shared_share, D)
-    shared_here = jnp.pad(shared_here, ((0, 0), (0, SHARED_PAD - shared_share), (0, 0)))
-    shared_pair = shared_here[:2].reshape(2 * SHARED_PAD, D)
-    shared_last = shared_here[2]
-
-    upstream_bf16 = join_cols(out_grad, first)
-    upstream = upstream_bf16.astype(f32)
-    grad_planes = spread_rows(sent_rows(upstream_bf16, first))
-
-    routes_all = lax.all_gather(routes, "row", axis=0)[arrival]
-    routes_all = local_tokens(routes_all, 1, first)
-    held_experts = row_place * EXP_DEV + jnp.arange(EXP_DEV, dtype=jnp.int32)
-    hits = jnp.any(routes_all[:, :, :, None] == held_experts, axis=2)
-    lower = (places[:, None] >= places[None, :]).astype(bf16)
-    ranks = jnp.einsum("ut,stj->suj", lower, hits.astype(bf16), preferred_element_type=f32)
-    codes = jnp.where(hits, ranks.astype(jnp.int32) - 1, -1)
-    codes = jnp.pad(codes.transpose(0, 2, 1), ((0, 0), (0, 8 - EXP_DEV), (0, 0)), constant_values=-1)
-
-    source = join_cols(inputs, first).astype(f32)
+    (
+        blocks[8],
+        blocks[6],
+        blocks[1],
+        blocks[3],
+        out_grad_other,
+    ) = together(
+        turn_planes(blocks[4]),
+        swap_rows(blocks[4], 2),
+        swap_rows(blocks[0], 1),
+        swap_rows(blocks[2], 1),
+        swap_cols(after(out_grad, inputs_other)),
+    )
+    upstream_bf16 = jnp.where(
+        first,
+        jnp.concatenate([out_grad, out_grad_other], axis=1),
+        jnp.concatenate([out_grad_other, out_grad], axis=1),
+    )
+    grad_rows = Spread(sent_rows(upstream_bf16, first))
+    blocks[12], blocks[10], blocks[5], blocks[7], got = together(
+        turn_planes(blocks[8]),
+        swap_rows(blocks[8], 2),
+        swap_rows(blocks[4], 1),
+        swap_rows(blocks[6], 1),
+        swap_cols(grad_rows.sent((0, 0))[0]),
+    )
+    grad_rows.got(got, [0], (0, 0))
+    source = jnp.where(
+        first,
+        jnp.concatenate([inputs, inputs_other], axis=1),
+        jnp.concatenate([inputs_other, inputs], axis=1),
+    ).astype(f32)
+    gains = jnp.stack([norm_gain, ffn_gain])
+    gains = jnp.where(
+        first,
+        jnp.concatenate([gains, gains_other], axis=1),
+        jnp.concatenate([gains_other, gains], axis=1),
+    )
+    gain_one = gains[:1]
+    gain_two = gains[1:]
     scale_one = lax.rsqrt(jnp.mean(source * source, axis=1, keepdims=True) + epsilon)
     unit_one = source * scale_one
-    gain_one = join_cols(norm_gain[None], first)
-    gain_two = join_cols(ffn_gain[None], first)
     normed_one = (unit_one * gain_one).astype(bf16)
-    query = jnp.dot(normed_one, query_full, preferred_element_type=f32).reshape(
-        rows_count, local_heads, NOPE + ROPE
-    )
+    cosine, sine = rotation(rows_count, ROPE)
+    turns = (
+        jnp.concatenate([cosine] * 4, axis=1),
+        jnp.concatenate([-sine, sine, -sine, sine], axis=1),
+    )
+    segments = (
+        jnp.broadcast_to(segment_row[:, None], (rows_count, 128)),
+        jnp.broadcast_to(segment_row[None], (8, rows_count)),
+    )
+    passed, starts = batch(grad_rows.passed((0, 0, 0), (0, 0, 1)))
+    (
+        blocks[14],
+        blocks[9],
+        blocks[11],
+        passed,
+        shared_packed,
+        normed_one,
+        cosine,
+        sine,
+        turns,
+        segments,
+    ) = together(
+        swap_rows(blocks[12], 2),
+        swap_rows(blocks[8], 1),
+        swap_rows(blocks[10], 1),
+        swap_rows(passed, 1),
+        shared_packed,
+        normed_one,
+        cosine,
+        sine,
+        turns,
+        segments,
+    )
+    grad_rows.taken(passed, starts, (0, 0, 0), (0, 0, 1))
+    grad_rows.held[0, 0] = after(grad_rows.held[0, 0], blocks[14])
+    grad_turned = grad_rows.turn(1)
+    blocks[13], blocks[15] = together(swap_rows(blocks[12], 1), swap_rows(blocks[14], 1))
+    dense = assemble([blocks[i] for i in range(4 * PLANES)], arrival)
+    flat_dense = dense.reshape(D, -1)
+    latent_full = flat_dense[:, QUERY_COLUMNS + 1536 : QUERY_COLUMNS + 1536 + latent_width]
+    router_full = flat_dense[
+        :, QUERY_COLUMNS + 1536 + latent_width : QUERY_COLUMNS + 1536 + latent_width + expert_count
+    ]
     latent = jnp.dot(normed_one, latent_full, preferred_element_type=f32).astype(bf16)
-    cosine, sine = rotation(rows_count, ROPE)
-    head_cos = cosine[:, None, :]
-    head_sin = sine[:, None, :]
     compressed = latent[:, :RANK].astype(f32)
     latent_scale = lax.rsqrt(jnp.mean(compressed * compressed, axis=1, keepdims=True) + epsilon)
     latent_unit = compressed * latent_scale
     latent_normed = (latent_unit * latent_gain).astype(bf16)
     key_rope = rotate(latent[:, RANK:].astype(f32), cosine, sine).astype(bf16)
-    expanded = jnp.dot(latent_normed, expand_full, preferred_element_type=f32).reshape(
-        rows_count, local_heads, NOPE + VDIM
-    )
-    key_nope = expanded[..., :NOPE].astype(bf16)
-    values_all = expanded[..., NOPE:].astype(bf16)
-    query_nope = query[..., :NOPE].astype(bf16)
-    query_rope = rotate(query[..., NOPE:], head_cos, head_sin).astype(bf16)
-    raw = jnp.einsum("qhd,khd->hqk", query_nope, key_nope, preferred_element_type=f32)
-    raw = raw + jnp.einsum("qhd,kd->hqk", query_rope, key_rope, preferred_element_type=f32)
-    allowed = (segment_row[:, None] == segment_row[None, :]) & (places[None, :] <= places[:, None])
-    scores = jnp.where(allowed[None], raw * score_scale, -1e30)
-    top = jnp.max(scores, axis=2, keepdims=True)
-    exponent = jnp.exp(scores - top)
-    total = jnp.sum(exponent, axis=2, keepdims=True)
-    weights = exponent / total
-    log_blocks = top + jnp.log(total)
-    mixed = (
-        jnp.einsum("hqk,khd->qhd", weights.astype(bf16), values_all, preferred_element_type=f32)
-        .astype(bf16)
-        .reshape(rows_count, local_heads * VDIM)
-    )
-    attended_part = jnp.einsum(
-        "tv,dv->td", mixed, output_turned, preferred_element_type=f32
-    ).astype(bf16)
-    attended = attended_part.astype(f32) + swap_cols(attended_part).astype(f32)
-    middle = source + attended
-    scale_two = lax.rsqrt(jnp.mean(middle * middle, axis=1, keepdims=True) + epsilon)
-    unit_two = middle * scale_two
-    normed_two = (unit_two * gain_two).astype(bf16)
-    row_planes = spread_rows(sent_rows(normed_two, first))
-
-    logits = jnp.dot(normed_two, router_full, preferred_element_type=f32)
-    log_total = jax.nn.logsumexp(logits, axis=1, keepdims=True)
-    chances = jnp.exp(logits - log_total)
-
+    ropes = head_ropes(key_rope)
+    routes_all = flat_dense[
+        :, QUERY_COLUMNS + 1536 + latent_width + expert_count :
+    ][:, : rows_count * TOPK // block]
+    routes_all = routes_all.reshape(row_devices, rows_count, TOPK).transpose(0, 2, 1)[arrival]
+    routes_all = routes_all.astype(jnp.int32)
+
+    routes_all = local_tokens(routes_all, 2, first)
+    held_experts = row_place * EXP_DEV + jnp.arange(EXP_DEV, dtype=jnp.int32)
+    hits = jnp.any(routes_all[:, :, None, :] == held_experts[None, None, :, None], axis=1)
+    upper = (places[:, None] <= places[None, :]).astype(bf16)
+    ranks = jnp.einsum("sjt,tu->sju", hits.astype(bf16), upper, preferred_element_type=f32)
+    codes = jnp.where(hits, ranks.astype(jnp.int32) - 1, -1)
+    codes = jnp.pad(codes, ((0, 0), (0, 8 - EXP_DEV), (0, 0)), constant_values=-1)
+    plane_codes = [codes[p * FAMILIES : (p + 1) * FAMILIES] for p in range(PLANES)]
+
+    latent_normed, plane_codes, grad_rows.held[0, 1], grad_rows.held[1, 0] = together(
+        latent_normed, plane_codes, grad_rows.cross(0), grad_turned
+    )
+
+    query, keys, mixed, attended_part = attend(
+        normed_one, latent_normed, ropes, turns, segments, dense
+    )
+    sent, starts = batch(grad_rows.sent((0, 1), (1, 0)))
+    passed, passed_starts = batch(grad_rows.passed((0, 1, 0), (1, 0, 0)))
+    (
+        query,
+        attended_part,
+        grad_rows.held[2, 0],
+        grad_rows.held[1, 1],
+        got,
+        passed,
+    ) = together(
+        query,
+        attended_part,
+        grad_rows.turn(2),
+        grad_rows.cross(1),
+        swap_cols(sent),
+        swap_rows(passed, 1),
+    )
+    grad_rows.got(got, starts, (0, 1), (1, 0))
+    grad_rows.taken(passed, passed_starts, (0, 1, 0), (1, 0, 0))
+
+    picked = {}
+
+    def pick(plane, *others):
+        picked[plane] = pick_grads(
+            grad_rows.family(plane), after(plane_codes[plane], *others), shared_last, capacity
+        )
+        return picked[plane]
+
+    def pass_alone(spread, key):
+        spread.taken(swap_rows(spread.passed(key)[0], 1), [0], key)
+
+    passed, starts = batch(grad_rows.passed((0, 1, 1), (1, 0, 1), (1, 1, 0)))
+    partner_part = jnp.concatenate(
+        [
+            attended_part[:COMMON],
+            jnp.where(first, attended_part[SENT:], attended_part[COMMON:SENT]),
+        ],
+        axis=0,
+    )
+    (
+        attended_other,
+        shared_here,
+        grad_rows.held[2, 1],
+        passed,
+    ) = together(
+        swap_cols(partner_part),
+        lax.all_to_all(
+            after(shared_packed, attended_part), "row", split_axis=0, concat_axis=0, tiled=True
+        ),
+        grad_rows.cross(2),
+        swap_rows(passed, 1),
+    )
+    grad_rows.taken(passed, starts, (0, 1, 1), (1, 0, 1), (1, 1, 0))
+    attended_sent = sent_rows(attended_part, first).astype(f32) + attended_other.astype(f32)
+    middle_sent = sent_rows(source, first) + attended_sent
+    scale_sent = lax.rsqrt(jnp.mean(middle_sent * middle_sent, axis=1, keepdims=True) + epsilon)
+    normed_sent = (middle_sent * scale_sent * gain_two).astype(bf16)
+    rows = Spread(normed_sent)
+
+    shared_here = shared_here.transpose(1, 2, 0, 3).reshape(3, shared_share, D)
+    shared_here = jnp.pad(shared_here, ((0, 0), (0, SHARED_PAD - shared_share), (0, 0)))
+    shared_pair = shared_here[:2].reshape(2 * SHARED_PAD, D)
+    shared_last = shared_here[2]
+
+    sent, starts = batch(rows.sent((0, 0)) + grad_rows.sent((1, 1)))
+    rows.held[1, 0], rows.held[0, 1], got, shared_pair, shared_last = together(
+        rows.turn(1), rows.cross(0), swap_cols(sent), shared_pair, shared_last
+    )
+    rows.got(got, starts, (0, 0))
+    grad_rows.got(got, starts[1:], (1, 1))
     router_turned = router_full.T
     router_held = lax.dynamic_slice_in_dim(
         jnp.concatenate([router_turned, router_turned], axis=0),
@@ -690,139 +1297,424 @@
         expert_count,
         0,
     )
-    sum_planes = [None] * PLANES
-    back_planes = [None] * PLANES
-    gate_grad_dense = []
-    kept_rows, kept_grads, kept_hidden, kept_gate, kept_up = [], [], [], [], []
-    shared_grads = 0.0
-    for plane in range(PLANES):
-        plane_codes = codes[plane * FAMILIES : (plane + 1) * FAMILIES]
-        slot_grads, hidden_grads = pick_grads(
-            grad_planes[plane], plane_codes, shared_last, capacity
-        )
-        slot_rows, gate_slots, shared_hidden, shared_back, shared_grad = pick_rows(
-            row_planes[plane],
-            grad_planes[plane],
-            plane_codes,
+    pass_alone(grad_rows, (1, 1, 1))
+    sent, starts = batch(rows.sent((0, 1), (1, 0)))
+    passed, passed_starts = batch(rows.passed((0, 0, 0), (0, 0, 1), (0, 1, 0)))
+    (
+        rows.held[2, 0],
+        rows.held[1, 1],
+        got,
+        passed,
+        picked[0],
+        picked[1],
+        router_held,
+    ) = together(
+        rows.turn(2),
+        rows.cross(1),
+        swap_cols(sent),
+        swap_rows(passed, 1),
+        pick(0),
+        pick(1),
+        router_held,
+    )
+    rows.got(got, starts, (0, 1), (1, 0))
+    rows.taken(passed, passed_starts, (0, 0, 0), (0, 0, 1), (0, 1, 0))
+
+    experts = (expert_gate, expert_up, expert_down)
+    begun = {}
+    ran = {}
+
+    def start_plane(plane, *others):
+        begun[plane] = pick_rows(
+            rows.family(plane),
+            grad_rows.family(plane),
+            after(plane_codes[plane], *others),
             router_held,
             shared_pair,
-            hidden_grads,
+            picked[plane][1],
             capacity,
         )
-        expert_sum, row_back, scaled_hidden, gate_back, up_back, gate_grad = run_experts(
-            slot_rows, slot_grads, gate_slots, expert_gate, expert_up, expert_down
+        return begun[plane]
+
+    def run_plane(plane):
+        ran[plane] = run_experts(begun[plane][0], picked[plane][0], begun[plane][1], *experts)
+        return ran[plane]
+
+    def back_sibling(plane):
+        return sum_tokens(
+            ran[plane][1],
+            plane_codes[plane],
+            begun[plane][3],
+            shared_pair,
+            capacity,
+            1,
+            None,
+            ran[plane][5],
         )
-        sibling, mine, dense = sum_tokens(
-            row_back, plane_codes, shared_back, shared_pair, gate_grad, capacity
+
+    def back_mine(plane, received):
+        return sum_tokens(
+            ran[plane][1],
+            plane_codes[plane],
+            begun[plane][3],
+            shared_pair,
+            capacity,
+            0,
+            received,
+            ran[plane][5],
         )
-        back_planes[plane] = (sibling, mine)
-        sum_planes[plane] = sum_tokens(
-            expert_sum, plane_codes, shared_hidden, shared_last, None, capacity
+
+    def sum_sibling(plane):
+        return sum_tokens(
+            ran[plane][0], plane_codes[plane], begun[plane][2], shared_last, capacity, 1
+        )[0]
+
+    def sum_mine(plane, received):
+        return sum_tokens(
+            ran[plane][0], plane_codes[plane], begun[plane][2], shared_last, capacity, 0, received
         )
-        gate_grad_dense.append(dense[:, :EXP_DEV])
-        shared_grads = shared_grads + shared_grad
-        kept_rows.append(slot_rows)
-        kept_grads.append(slot_grads)
-        kept_hidden.append(scaled_hidden)
-        kept_gate.append(gate_back)
-        kept_up.append(up_back)
-
-    back_sent = collect_rows(back_planes)
-    sum_sent = collect_rows(sum_planes)
-
-    gate_grad_dense = jnp.concatenate(gate_grad_dense, axis=0)
-    gate_grad_dense = local_tokens(gate_grad_dense, 2, first)[place_of]
+
+    def unique_out(mine):
+        return swap_cols(mine[1])
+
+    def across_out(mine, unique):
+        return swap_rows(add_unique(mine[0], unique, 1), 2)
+
+    def own_sum(mine, unique, crossed):
+        return add_unique(mine[0], unique, 0) + crossed
+
+    pass_alone(rows, (0, 1, 1))
+    sent, starts = batch(rows.sent((1, 1), (2, 0)))
+    passed, passed_starts = batch(rows.passed((1, 0, 0), (1, 1, 0), (1, 0, 1)))
+    rows.held[3, 0], rows.held[2, 1], got, passed = together(
+        rows.turn(3), rows.cross(2), swap_cols(sent), swap_rows(passed, 1)
+    )
+    rows.got(got, starts, (1, 1), (2, 0))
+    rows.taken(passed, passed_starts, (1, 0, 0), (1, 1, 0), (1, 0, 1))
+
+    pass_alone(rows, (1, 1, 1))
+    sent, starts = batch(rows.sent((2, 1), (3, 0)))
+    passed, passed_starts = batch(rows.passed((2, 0, 0), (2, 1, 0), (2, 0, 1)))
+    begun[1], rows.held[3, 1], grad_rows.held[3, 0], got, passed = together(
+        start_plane(1), rows.cross(3), grad_rows.turn(3), swap_cols(sent), swap_rows(passed, 1)
+    )
+    rows.got(got, starts, (2, 1), (3, 0))
+    rows.taken(passed, passed_starts, (2, 0, 0), (2, 1, 0), (2, 0, 1))
+
+    ran[1] = run_plane(1)
+    back_1 = back_sibling(1)
+    sent, starts = batch(rows.sent((3, 1)) + grad_rows.sent((2, 0), (2, 1)))
+    passed = [
+        batch(rows.passed((2, 1, 1), (3, 0, 1))),
+        batch(rows.passed((3, 0, 0), (3, 1, 0))),
+        batch(grad_rows.passed((2, 0, 0), (2, 1, 0))),
+    ]
+    ran[1], back_1, grad_rows.held[3, 1], got, passed_got = together(
+        ran[1],
+        back_1,
+        grad_rows.cross(3),
+        swap_cols(sent),
+        [swap_rows(rows_passed, 1) for rows_passed, _ in passed],
+    )
+    rows.got(got, starts, (3, 1))
+    grad_rows.got(got, starts[1:], (2, 0), (2, 1))
+    rows.taken(passed_got[0], passed[0][1], (2, 1, 1), (3, 0, 1))
+    rows.taken(passed_got[1], passed[1][1], (3, 0, 0), (3, 1, 0))
+    grad_rows.taken(passed_got[2], passed[2][1], (2, 0, 0), (2, 1, 0))
+
+    passed, passed_starts = batch(grad_rows.passed((2, 0, 1), (2, 1, 1)))
+    grad_rows.taken(swap_rows(passed, 1), passed_starts, (2, 0, 1), (2, 1, 1))
+    sent, starts = batch(grad_rows.sent((3, 0), (3, 1)))
+    passed, passed_starts = batch(
+        rows.passed((3, 1, 1)) + grad_rows.passed((3, 0, 0), (3, 1, 0))
+    )
+    picked[2] = pick(2)
+    begun[2] = start_plane(2)
+    picked[2], begun[2], back_got, got, passed = together(
+        picked[2], begun[2], swap_rows(back_1[0], 1), swap_cols(sent), swap_rows(passed, 1)
+    )
+    grad_rows.got(got, starts, (3, 0), (3, 1))
+    rows.taken(passed, passed_starts, (3, 1, 1))
+    grad_rows.taken(passed, passed_starts[1:], (3, 0, 0), (3, 1, 0))
+    passed, passed_starts = batch(grad_rows.passed((3, 0, 1), (3, 1, 1)))
+    grad_rows.taken(swap_rows(passed, 1), passed_starts, (3, 0, 1), (3, 1, 1))
+    back_mine_1 = back_mine(1, back_got)
+    sum_1 = sum_sibling(1)
+    back_mine_1, sum_1 = together(back_mine_1, sum_1)
+
+    ran[2] = run_plane(2)
+    back_2 = back_sibling(2)
+    ran[2], back_2, back_unique, sum_got = together(
+        ran[2], back_2, unique_out(back_mine_1), swap_rows(sum_1, 1)
+    )
+    sum_mine_1 = sum_mine(1, sum_got)
+
+    picked[3] = pick(3)
+    begun[3] = start_plane(3)
+    picked[3], begun[3], back_got, back_crossed, sum_unique = together(
+        picked[3],
+        begun[3],
+        swap_rows(back_2[0], 1),
+        across_out(back_mine_1, back_unique),
+        unique_out(sum_mine_1),
+    )
+    back = own_sum(back_mine_1, back_unique, back_crossed)
+    back_mine_2 = back_mine(2, back_got)
+    sum_2 = sum_sibling(2)
+    attended_rest = after(attended_sent[COMMON:], picked[3]).astype(bf16)
+    back_mine_2, sum_2, back, attended_rest = together(
+        back_mine_2, sum_2, back, swap_cols(attended_rest)
+    )
+
+    ran[3] = run_plane(3)
+    back_3 = back_sibling(3)
+    ran[3], back_3, back, back_unique, sum_got, sum_crossed = together(
+        ran[3],
+        back_3,
+        turn_planes(back),
+        unique_out(back_mine_2),
+        swap_rows(sum_2, 1),
+        across_out(sum_mine_1, sum_unique),
+    )
+    result = own_sum(sum_mine_1, sum_unique, sum_crossed)
+    sum_mine_2 = sum_mine(2, sum_got)
+    sum_mine_2, result = together(sum_mine_2, result)
+
+    attended_rest = after(attended_rest, sum_mine_2).astype(f32)
+    attended_mine = attended_sent[COMMON:]
+    middle = source + jnp.concatenate(
+        [
+            attended_sent[:COMMON],
+            jnp.where(first, attended_mine, attended_rest),
+            jnp.where(first, attended_rest, attended_mine),
+        ],
+        axis=0,
+    )
+    scale_two = lax.rsqrt(jnp.mean(middle * middle, axis=1, keepdims=True) + epsilon)
+    unit_two = middle * scale_two
+    normed_two = (unit_two * gain_two).astype(bf16)
+    logits = jnp.dot(normed_two, router_full, preferred_element_type=f32)
+    log_total = jax.nn.logsumexp(logits, axis=1, keepdims=True)
+    chances = jnp.exp(logits - log_total)
+
+    begun[0] = start_plane(0, sum_mine_2)
+    begun[0], back_got, back_crossed, sum_unique, result, normed_two, chances = together(
+        begun[0],
+        swap_rows(back_3[0], 1),
+        across_out(back_mine_2, back_unique),
+        unique_out(sum_mine_2),
+        turn_planes(result),
+        normed_two,
+        chances,
+    )
+    back = back + own_sum(back_mine_2, back_unique, back_crossed)
+    back_mine_3 = back_mine(3, back_got)
+    sum_3 = sum_sibling(3)
+    back_mine_3, sum_3, back = together(back_mine_3, sum_3, back)
+
+    ran[0] = run_plane(0)
+    back_0 = back_sibling(0)
+    ran[0], back_0, back, back_unique, sum_got, sum_crossed = together(
+        ran[0],
+        back_0,
+        turn_planes(back),
+        unique_out(back_mine_3),
+        swap_rows(sum_3, 1),
+        across_out(sum_mine_2, sum_unique),
+    )
+    result = result + own_sum(sum_mine_2, sum_unique, sum_crossed)
+    sum_mine_3 = sum_mine(3, sum_got)
+    sum_mine_3, result = together(sum_mine_3, result)
+
+    kept = [
+        (begun[plane][0], picked[plane][0], ran[plane][3], ran[plane][4], ran[plane][2])
+        for plane in range(PLANES)
+    ]
+    kept = [list(part) for part in zip(*kept)]
+    half = EXP_DEV // 2
+    expert_parts = expert_weight_grads(*kept, 0, half, [])
+    expert_parts, back_got, back_crossed, sum_unique, result = together(
+        expert_parts,
+        swap_rows(back_0[0], 1),
+        across_out(back_mine_3, back_unique),
+        unique_out(sum_mine_3),
+        turn_planes(result),
+    )
+    back = back + own_sum(back_mine_3, back_unique, back_crossed)
+    back_mine_0 = back_mine(0, back_got)
+    sum_0 = sum_sibling(0)
+    back_mine_0, sum_0, back = together(back_mine_0, sum_0, back)
+
+    expert_parts = expert_weight_grads(*kept, half, EXP_DEV - half, expert_parts)
+    expert_parts, back, back_unique, sum_got, common_crossed = together(
+        expert_parts,
+        turn_planes(back),
+        unique_out(back_mine_0),
+        swap_rows(sum_0, 1),
+        swap_rows(back_mine_0[0][1, :COMMON], 2),
+    )
+    expert_gate_grad, expert_up_grad, expert_down_grad = expert_parts
+    common = back[:COMMON] + back_mine_0[0][0, :COMMON] + common_crossed
+    unique_rest = back_mine_0[0][:, COMMON:] + back_unique
+    sum_mine_0 = sum_mine(0, sum_got)
+
+    gate_grad_dense = [
+        jnp.stack([mine[2], sibling[1]], axis=1)[:, :, :EXP_DEV]
+        for mine, sibling in (
+            (back_mine_0, back_0),
+            (back_mine_1, back_1),
+            (back_mine_2, back_2),
+            (back_mine_3, back_3),
+        )
+    ]
+    gate_grad_dense = jnp.stack(gate_grad_dense).reshape(row_devices, EXP_DEV, rows_count)
+    gate_grad_dense = local_tokens(gate_grad_dense, 2, first)[arrival]
     gate_grad_dense = lax.all_to_all(
         gate_grad_dense, "row", split_axis=0, concat_axis=0, tiled=True
     ).reshape(expert_count, rows_count)
+    shared_grads = sum([begun[p][4] for p in range(1, PLANES)], begun[0][4])
+    shared_grads = shared_grads.reshape(3, SHARED_PAD, D)[:, :shared_share]
+    shared_grads = (
+        shared_grads.astype(bf16)
+        .reshape(3, shared_share, row_devices, -1)
+        .transpose(2, 0, 1, 3)
+    )
     gate_grad_dense = gate_grad_dense + swap_cols(gate_grad_dense)
     weighted_gates = gate_grad_dense.T * chances
     logit_grads = (
         weighted_gates - chances * jnp.sum(weighted_gates, axis=1, keepdims=True)
     ).astype(bf16)
     router_back = jnp.einsum("te,de->td", logit_grads, router_full, preferred_element_type=f32)
-    router_grad_part = jnp.einsum("td,te->de", normed_two, logit_grads, preferred_element_type=f32)
-
-    expert_gate_grad, expert_up_grad, expert_down_grad = expert_weight_grads(
-        kept_rows, kept_grads, kept_gate, kept_up, kept_hidden
-    )
-    shared_grads = shared_grads.reshape(3, SHARED_PAD, D)[:, :shared_share]
-    shared_grads = (
-        shared_grads.astype(bf16)
-        .reshape(3, shared_share, row_devices, -1)
-        .transpose(2, 0, 1, 3)
-    )
+    unique_crossed, common_other, sum_mine_0, shared_grads, router_back, logit_grads = together(
+        swap_rows(unique_rest[1], 2),
+        swap_cols(common),
+        sum_mine_0,
+        shared_grads,
+        router_back,
+        logit_grads,
+    )
+    unique_mine = back[COMMON:] + unique_rest[0] + unique_crossed
     shared_grads = lax.all_to_all(shared_grads, "row", split_axis=0, concat_axis=0, tiled=True)
+    unique_other = swap_cols(unique_mine)
     shared_grads = shared_grads.transpose(1, 0, 2, 3).reshape(3, row_devices * shared_share, -1)
     shared_grads = shared_grads.astype(f32)
     shared_gate_grad = shared_grads[0].T
     shared_up_grad = shared_grads[1].T
     shared_down_grad = shared_grads[2]
 
-    combined = merge_rows(
-        own_columns(sum_sent, first), swap_cols(other_columns(sum_sent, first)), first
-    )
-    output = (own_columns(middle, first) + combined).astype(bf16)
-
-    normed_two_back = merge_rows(back_sent, swap_cols(back_sent), first) + router_back
+    upstream = upstream_bf16.astype(f32)
+    normed_two_back = router_back + jnp.concatenate(
+        [
+            common.astype(f32) + common_other.astype(f32),
+            jnp.where(first, unique_mine, unique_other).astype(f32),
+            jnp.where(first, unique_other, unique_mine).astype(f32),
+        ],
+        axis=0,
+    )
     ffn_gain_part = jnp.sum(normed_two_back * unit_two, axis=0)
     weighted = normed_two_back * gain_two
     average = jnp.mean(weighted * unit_two, axis=1, keepdims=True)
     middle_back = upstream + scale_two * (weighted - unit_two * average)
     attended_back = middle_back.astype(bf16)
-    mixed_back = (
-        jnp.einsum("td,dv->tv", attended_back, output_turned, preferred_element_type=f32)
-        .astype(bf16)
-        .reshape(rows_count, local_heads, VDIM)
-    )
-    output_grad_part = jnp.einsum("td,tv->dv", attended_back, mixed, preferred_element_type=f32)
-
-    weights = jnp.exp(scores - log_blocks)
-    weight_back = jnp.einsum("qhd,khd->hqk", mixed_back, values_all, preferred_element_type=f32)
-    center = jnp.sum(weight_back * weights, axis=2, keepdims=True)
-    raw_back = (weights * (weight_back - center) * score_scale).astype(bf16)
-    query_nope_back = jnp.einsum("hqk,khd->qhd", raw_back, key_nope, preferred_element_type=f32)
-    query_rope_back = jnp.einsum("hqk,kd->qhd", raw_back, key_rope, preferred_element_type=f32)
-    key_nope_back = jnp.einsum("hqk,qhd->khd", raw_back, query_nope, preferred_element_type=f32)
-    key_rope_back = jnp.einsum("hqk,qhd->kd", raw_back, query_rope, preferred_element_type=f32)
-    values_back = jnp.einsum(
-        "hqk,qhd->khd", weights.astype(bf16), mixed_back, preferred_element_type=f32
-    )
-    query_back = jnp.concatenate(
-        [query_nope_back, unrotate(query_rope_back, head_cos, head_sin)], axis=2
-    )
-    query_back = query_back.astype(bf16).reshape(rows_count, local_heads * (NOPE + ROPE))
-    expanded_back = (
-        jnp.concatenate([key_nope_back, values_back], axis=2)
-        .astype(bf16)
-        .reshape(rows_count, local_heads * (NOPE + VDIM))
-    )
-    latent_normed_back = jnp.einsum(
-        "tc,rc->tr", expanded_back, expand_full, preferred_element_type=f32
-    )
-    expand_grad_part = jnp.einsum(
-        "tr,tc->rc", latent_normed, expanded_back, preferred_element_type=f32
-    )
+
+    def by_plane(total):
+        return total.reshape((PLANES, 2) + total.shape[1:])
+
+    output_sibling = block_grads(arrival, attended_back, mixed, 256, 1)
+    query_back, expanded_back, key_rope_back, latent_normed_back, input_part = attend_back(
+        attended_back, query, keys, ropes, turns, segments, dense, RANK
+    )
+    query_back, last_unique, output_got, sum_crossed = together(
+        query_back,
+        unique_out(sum_mine_0),
+        swap_rows(output_sibling, 1),
+        across_out(sum_mine_3, sum_unique),
+    )
+    result = result + own_sum(sum_mine_3, sum_unique, sum_crossed)
+
     latent_gain_part = jnp.sum(latent_normed_back * latent_unit, axis=0)
     latent_weighted = latent_normed_back * latent_gain
     compressed_back = latent_scale * (
         latent_weighted
         - latent_unit * jnp.mean(latent_weighted * latent_unit, axis=1, keepdims=True)
     )
+    key_rope_back = key_rope_back[:, :ROPE] + key_rope_back[:, ROPE:]
     rope_back = unrotate(key_rope_back, cosine, sine)
     latent_part = jnp.concatenate([compressed_back, rope_back], axis=1).astype(bf16)
-    latent_back = (latent_part.astype(f32) + swap_cols(latent_part).astype(f32)).astype(bf16)
-    latent_grad_part = jnp.einsum("td,tc->dc", normed_one, latent_back, preferred_element_type=f32)
-    query_grad_part = jnp.einsum("td,tc->dc", normed_one, query_back, preferred_element_type=f32)
-    input_part = jnp.einsum("tc,dc->td", query_back, query_full, preferred_element_type=f32)
-    input_part = input_part.astype(bf16)
+    latent_turned = latent_normed.T
+    wide_sibling = block_grads(
+        arrival, normed_one, query_back, 384, 1, latent_turned, expanded_back
+    )
+    wide_sibling, latent_part = together(wide_sibling, latent_part)
+    output_total = by_plane(
+        block_grads(
+            arrival, after(attended_back, wide_sibling), mixed, 256, 0, received=output_got
+        )
+    )
+    weighted_part = jnp.sum(
+        after(input_part, wide_sibling).astype(f32) * gain_one * unit_one, axis=1
+    )
+    wide_got, latent_other, output_total, weighted_part, result = together(
+        swap_rows(wide_sibling, 1),
+        swap_cols(latent_part),
+        output_total,
+        weighted_part,
+        turn_planes(result),
+    )
+    latent_back = (latent_part.astype(f32) + latent_other.astype(f32)).astype(bf16)
+    wide_total = by_plane(
+        block_grads(
+            arrival, normed_one, query_back, 384, 0, latent_turned, expanded_back, wide_got
+        )
+    )
+    narrow_sibling = narrow_grads(
+        arrival, normed_one, after(latent_back, wide_total), normed_two, logit_grads, 1
+    )
+    input_sent = other_columns(input_part, first)
+    half_rows = rows_count // 2
+    small_part = jnp.concatenate([weighted_part, latent_gain_part]).reshape(-1, 128)
+    wide_total, narrow_sibling, sum_crossed, crossed_output, input_low, small_other = together(
+        wide_total,
+        narrow_sibling,
+        across_out(sum_mine_0, last_unique),
+        [swap_rows(output_total[p, 1], 2) for p in (1, 2)],
+        swap_cols(input_sent[:half_rows]),
+        swap_cols(small_part),
+    )
+    sum_sent = result + own_sum(sum_mine_0, last_unique, sum_crossed)
+    output_sums = [output_total[p, 0] + crossed_output[p - 1] for p in (1, 2)]
+    narrow_mine = narrow_grads(
+        arrival, normed_one, latent_back, after(normed_two, wide_total), logit_grads, 0
+    )
+    crossed, crossed_output, moved_output, narrow_got, narrow_mine, input_high = together(
+        swap_rows(wide_total[1, 1], 2),
+        swap_rows(output_total[3, 1], 2),
+        turn_planes(output_sums[0]),
+        swap_rows(narrow_sibling, 1),
+        narrow_mine,
+        swap_cols(input_sent[half_rows:]),
+    )
+    output_sums.append(output_total[3, 0] + crossed_output)
+    moving = [wide_total[1, 0] + crossed]
+    moving_output = output_sums[1] + moved_output
+    narrow_total = by_plane(narrow_mine + narrow_got)
+    crossed, moved, moved_output, crossed_narrow, combined_other = together(
+        swap_rows(wide_total[2, 1], 2),
+        turn_planes(moving[0]),
+        turn_planes(moving_output),
+        swap_rows(narrow_total[1, 1], 2),
+        swap_cols(other_columns(sum_sent, first)),
+    )
+    moving = [wide_total[2, 0] + crossed + moved, narrow_total[1, 0] + crossed_narrow]
+    moving_output = output_sums[2] + moved_output
+
     latent_input = jnp.einsum("tc,dc->td", latent_back, latent_full, preferred_element_type=f32)
-    weighted_part = jnp.sum(input_part.astype(f32) * gain_one * unit_one, axis=1)
-    weighted_sum = weighted_part + swap_cols(weighted_part)
+    small_sum = (small_part + small_other).reshape(-1)
+    weighted_sum = small_sum[:rows_count]
     weighted_sum = weighted_sum + jnp.sum(latent_input * gain_one * unit_one, axis=1)
     normed_one_back = (
         own_columns(input_part, first).astype(f32)
-        + swap_cols(other_columns(input_part, first)).astype(f32)
+        + jnp.concatenate([input_low, input_high], axis=0).astype(f32)
         + own_columns(latent_input, first)
     )
     own_unit = own_columns(unit_one, first)
@@ -830,42 +1722,52 @@
     input_grad = own_columns(middle_back, first) + scale_one * (
         normed_one_back * norm_gain - own_unit * (weighted_sum / D)[:, None]
     )
-    gains = jnp.concatenate(
-        [
-            norm_gain_part,
-            own_columns(ffn_gain_part, first),
-            latent_gain_part + swap_cols(latent_gain_part),
-        ]
-    )
-    gains = lax.psum(gains, "row")
+    gain_grads = jnp.concatenate(
+        [norm_gain_part, own_columns(ffn_gain_part, first), small_sum[rows_count:]]
+    ).reshape(-1, 128)
+    crossed, crossed_narrow, moved, crossed_output, gain_grads = together(
+        swap_rows(wide_total[3, 1], 2),
+        swap_rows(narrow_total[2, 1], 2),
+        [turn_planes(part) for part in moving],
+        swap_rows(output_total[0, 1], 2),
+        gain_grads,
+    )
+    moving = [
+        wide_total[3, 0] + crossed + moved[0],
+        narrow_total[2, 0] + crossed_narrow + moved[1],
+    ]
+    crossed, crossed_narrow, moved, moved_output = together(
+        swap_rows(wide_total[0, 1], 2),
+        swap_rows(narrow_total[3, 1], 2),
+        [turn_planes(part) for part in moving],
+        turn_planes(moving_output),
+    )
+    moving_output = output_total[0, 0] + crossed_output + moved_output
+    moving = [
+        wide_total[0, 0] + crossed + moved[0],
+        narrow_total[3, 0] + crossed_narrow + moved[1],
+    ]
+    crossed_narrow, moved, others = together(
+        swap_rows(narrow_total[0, 1], 2),
+        turn_planes(moving[1]),
+        [swap_rows(gain_grads, bits) for bits in (1, 2, 3)],
+    )
+    moving[1] = narrow_total[0, 0] + crossed_narrow + moved
+    gain_grads = (gain_grads + others[0]) + (others[1] + others[2])
+    others = [swap_rows(gain_grads, bits) for bits in (4, 8, 12)]
+    gain_grads = (gain_grads + others[0]) + (others[1] + others[2])
+    gain_grads = gain_grads.reshape(-1)
+    output_grad, query_grad, expand_grad, latent_grad, router_grad = unpack_grads(
+        moving_output, *moving, (query_width, quarter, latent_width)
+    )
+
+    combined = merge_rows(own_columns(sum_sent, first), combined_other, first)
+    output = (own_columns(middle, first) + combined).astype(bf16)
+
     width_share = norm_gain.shape[0]
-    norm_gain_grad = gains[:width_share]
-    ffn_gain_grad = gains[width_share : 2 * width_share]
-    latent_gain_grad = gains[2 * width_share :]
-
-    def to_owners(values):
-        return lax.psum_scatter(
-            values.astype(bf16), "row", scatter_dimension=0, tiled=True
-        ).astype(f32)
-
-    output_grad = to_owners(output_grad_part).T
-    dense_part = jnp.concatenate(
-        [
-            query_grad_part,
-            latent_grad_part,
-            router_grad_part,
-            expand_grad_part.reshape(D, expand_width),
-        ],
-        axis=1,
-    )
-    dense_grad = to_owners(dense_part)
-    edge = query_width
-    query_grad = dense_grad[:, :edge]
-    latent_grad = dense_grad[:, edge : edge + latent_width]
-    edge += latent_width
-    router_grad = dense_grad[:, edge : edge + expert_count]
-    edge += expert_count
-    expand_grad = dense_grad[:, edge:].reshape(expand_weight.shape)
+    norm_gain_grad = gain_grads[:width_share]
+    ffn_gain_grad = gain_grads[width_share : 2 * width_share]
+    latent_gain_grad = gain_grads[2 * width_share :]
     return (
         output,
         input_grad,

time: 1540 us -> 1210 us (0.79)
  waiting for transfers between devices: 551 us -> 311 us
  Pallas kernels: 373 us -> 503 us
  matrix products: 146 us -> 16.1 us
  blocking collectives: 92 us -> 0 us
  other arithmetic: 142 us -> 161 us
    dot_general x21 -> x1, matrix products: 134 us -> 0.2 us  [on_device(): jnp.einsum('sjt,tu->sju', hits.astype(bf16), upper, preferred_element_typ...]
    pallas_call x8 -> x27, Pallas kernels: 81.3 us -> 210 us  [the longest x16 94.3 us: sum_tokens(): pl.pallas_call(body, grid=(2,), in_specs=in_specs, out_specs=out_specs, o...]
    ppermute x36 -> x29, waiting for transfers between devices: 272 us -> 148 us  [swap_cols(): return lax.ppermute(values, 'col', [(0, 1), (1, 0)])]
    all_gather x1 -> x0, waiting for transfers between devices: 75 us -> none  [on_device(): packed_full = lax.all_gather(packed, 'row', axis=0, tiled=True)]
    ppermute x12 -> x24, waiting for transfers between devices: 149 us -> 80.3 us  [turn_planes(): return lax.ppermute(values, 'row', [(i, (i + 4) % 16) for i in range(16)])]
    psum x1 -> x0, blocking collectives: 57.6 us -> none  [on_device(): gains = lax.psum(gains, 'row')]
    all_gather x1 -> x0, blocking collectives: 34.4 us -> none  [on_device(): routes_all = lax.all_gather(routes, 'row', axis=0)[arrival]]
    ppermute x56 -> x73, waiting for transfers between devices: 54.8 us -> 82.3 us  [swap_rows(): return lax.ppermute(values, 'row', [(i, i ^ bit) for i in range(16)])]
  transfers between devices with their start and end apart: 110 -> 129, of which waited for: 33 -> 43; matrix products, arithmetic and copies ran while one was open for 24% -> 18% of each run, Pallas kernels for 24% -> 40%
where the time goes in v2:
time: 1210 us; the launch traced here: 1200 us
  Pallas kernels  503 us (42%)
  waiting for transfers between devices  311 us (26%)
  other arithmetic  161 us (13%)
  starting transfers between devices  102 us (8%)
  local copies, waits for them, and re-layouts  100 us (8%)
  matrix products  16.1 us (1%)
    ppermute x29, waiting for transfers between devices, swap_cols(): return lax.ppermute(values, 'col', [(0, 1), (1, 0)])  148 us
    pallas_call x4, Pallas kernels, run_experts(): pl.pallas_call(body, grid=(count,), in_specs=[wide, wide, narrow, matrix,...  111 us
    pallas_call x16, Pallas kernels, sum_tokens(): pl.pallas_call(body, grid=(2,), in_specs=in_specs, out_specs=out_specs, o...  94.3 us
    pallas_call x4, Pallas kernels, pick_rows(): pl.pallas_call(body, grid=(FAMILIES,), in_specs=[pl.BlockSpec(memory_spac...  89.9 us
    ppermute x73, waiting for transfers between devices, swap_rows(): return lax.ppermute(values, 'row', [(i, i ^ bit) for i in range(16)])  82.3 us
    ppermute x24, waiting for transfers between devices, turn_planes(): return lax.ppermute(values, 'row', [(i, (i + 4) % 16) for i in range(16)])  80.3 us
    pallas_call x2, Pallas kernels, expert_weight_grads(): pl.pallas_call(body, grid=(count, width // tile), in_specs=[wide] * (2 *...  56.8 us
    ppermute x73, starting transfers between devices, swap_rows(): return lax.ppermute(values, 'row', [(i, i ^ bit) for i in range(16)])  41.4 us
  transfers between devices with their start and end apart: 129, of which 43 were waited for; matrix products, arithmetic and copies ran while one was open for 18% of the time, Pallas kernels for 40%

profile of v2, /device:TPU:0, one launch (start us, length us, event | category | flops | bytes accessed | tf_op | source)
XLA Modules:
  0.0 1195.6 jit_solution(8370722526682311859)
XLA Ops:
  14.6 12.6 %collective-permute-done.3 = f32[2,1024]{1,0:T(2,128)S(1)} collective-permute-done((f32[2,1024]{1,0:T(2,128)S(1)}, f32[2,1024]{1,0:T(2,128)S(1)}, u32[]{:S(2)}, u32[]{:S(2)}) %collective-permute-start.3) | collective-permute-done | bytes 8224 | tf_op jit(solution)/shard_map/ppermute | solution.py:94
  42.4 20.2 %collective-permute-done.5.refs_6_ = bf16[128,3840]{1,0:T(8,128)(2,1)} collective-permute-done((bf16[128,3840]{1,0:T(8,128)(2,1)}, bf16[128,3840]{1,0:T(8,128)(2,1)}, u32[]{:S(2)}, u32[]{:S(2)}) %collective-permute-start.5) | collective-permute-done | bytes 983072 | tf_op jit(solution)/shard_map/ppermute | solution.py:98
  68.7 15.5 %collective-permute-done.13.refs_1_.refs_9_ = bf16[160,2048]{1,0:T(8,128)(2,1)S(1)} collective-permute-done((bf16[160,2048]{1,0:T(8,128)(2,1)S(1)}, bf16[160,2048]{1,0:T(8,128)(2,1)S(1)}, u32[]{:S(2)}, u32[]{:S(2)}) %collective-permute-start.13) | collective-permute-done | bytes 655392 | tf_op jit(solution)/shard_map/ppermute | solution.py:94
  102.5 18.9 %collective-permute-done.14.refs_14_ = bf16[128,3840]{1,0:T(8,128)(2,1)} collective-permute-done((bf16[128,3840]{1,0:T(8,128)(2,1)}, bf16[128,3840]{1,0:T(8,128)(2,1)}, u32[]{:S(2)}, u32[]{:S(2)}) %collective-permute-start.14) | collective-permute-done | bytes 983072 | tf_op jit(solution)/shard_map/ppermute | solution.py:98
  126.9 11.9 shard_map.298
  174.3 20.2 %shard_map.299 = (bf16[512,1536]{1,0:T(8,128)(2,1)}, bf16[512,2048]{1,0:T(8,128)(2,1)}, bf16[512,1024]{1,0:T(8,128)(2,1)}, bf16[512,2048]{1,0:T(8,128)(2,1)}) custom-call(bf16[512,2048]{1,0:T(8,128)(2,1)} %copy-done.5, bf16[512,512]{1,0:T(8,128)(2,1)} %fusion.20.latent_ref, bf16[512,128]{1,0:T(8,128)(2,1)} %get-tuple-element.900.rope0_ref, ...), custom_call_target="tpu_custom_call" | custom-call | flops 1000000000 | bytes 1000000 | tf_op jit(solution)/shard_map/pallas_call | solution.py:895
  230.1 25.3 %collective-permute-done.26 = bf16[352,2048]{1,0:T(8,128)(2,1)} collective-permute-done((bf16[352,2048]{1,0:T(8,128)(2,1)S(1)}, bf16[352,2048]{1,0:T(8,128)(2,1)}, u32[]{:S(2)}, u32[]{:S(2)}) %collective-permute-start.26) | collective-permute-done | bytes 1441824 | tf_op jit(solution)/shard_map/ppermute | solution.py:94
  255.4 9.2 collective-permute-done.27.refs_4_.refs_12_
  279.8 25.5 %collective-permute-done.31.refs_5_.refs_13_.refs_1_ = bf16[320,2048]{1,0:T(8,128)(2,1)S(1)} collective-permute-done((bf16[320,2048]{1,0:T(8,128)(2,1)S(1)}, bf16[320,2048]{1,0:T(8,128)(2,1)S(1)}, u32[]{:S(2)}, u32[]{:S(2)}) %collective-permute-start.31) | collective-permute-done | bytes 1310752 | tf_op jit(solution)/shard_map/ppermute | solution.py:94
  318.9 8.9 shard_map.300
  327.9 8.9 shard_map.301
  336.8 9.9 collective-permute-done.34.refs_1_.refs_5_
  360.4 30.2 %collective-permute-done.39.refs_5_.refs_1_ = bf16[320,2048]{1,0:T(8,128)(2,1)S(1)} collective-permute-done((bf16[320,2048]{1,0:T(8,128)(2,1)S(1)}, bf16[320,2048]{1,0:T(8,128)(2,1)S(1)}, u32[]{:S(2)}, u32[]{:S(2)}) %collective-permute-start.39) | collective-permute-done | bytes 1310752 | tf_op jit(solution)/shard_map/ppermute | solution.py:94
  409.2 22.6 %shard_map.302 = (bf16[4,256,2048]{2,1,0:T(8,128)(2,1)}, f32[4,256,128]{2,1,0:T(8,128)}, bf16[4,512,128]{2,1,0:T(8,128)(2,1)}, bf16[4,512,256]{2,1,0:T(8,128)(2,1)}, f32[384,2048]{1,0:T(8,128)}) custom-call(bf16[352,2048]{1,0:T(8,128)(2,1)} %collective-permute-done.29.refs_0_, bf16[320,2048]{1,0:T(8,128)(2,1)} %collective-permute-done.34.refs_1_.refs_5_, ...), custom_call_target="tpu_custom_call" | custom-call | flops 1000000000 | bytes 1000000 | tf_op jit(solution)/shard_map/pallas_call | solution.py:401
  446.6 27.5 %shard_map.303 = (bf16[4,256,2048]{2,1,0:T(8,128)(2,1)}, bf16[4,256,2048]{2,1,0:T(8,128)(2,1)}, bf16[4,256,704]{2,1,0:T(8,128)(2,1)}, bf16[4,256,704]{2,1,0:T(8,...) custom-call(bf16[4,256,2048]{2,1,0:T(8,128)(2,1)} %get-tuple-element.439.rows_ref.refs_1_, ...), custom_call_target="tpu_custom_call" | custom-call | flops 1000000000 | bytes 1000000 | tf_op jit(solution)/shard_map/pallas_call | solution.py:480
  480.0 10.8 collective-permute-done.47.refs_1_.refs_5_.refs_9_.refs_13_
  505.5 9.1 shard_map.305
  514.7 22.5 %shard_map.306 = (bf16[4,256,2048]{2,1,0:T(8,128)(2,1)}, f32[4,256,128]{2,1,0:T(8,128)}, bf16[4,512,128]{2,1,0:T(8,128)(2,1)}, bf16[4,512,256]{2,1,0:T(8,128)(2,1)}, f32[384,2048]{1,0:T(8,128)}) custom-call(bf16[352,2048]{1,0:T(8,128)(2,1)} %collective-permute-done.32.refs_0_, bf16[320,2048]{1,0:T(8,128)(2,1)} %copy-done.35, bf16[864,2048]{1,0:T(8,128)(2,1)} %copy-done.12, ...), custom_call_target="tpu_custom_call" | custom-call | flops 1000000000 | bytes 1000000 | tf_op jit(solution)/shard_map/pallas_call | solution.py:401
  546.4 27.5 %shard_map.307 = (bf16[4,256,2048]{2,1,0:T(8,128)(2,1)}, bf16[4,256,2048]{2,1,0:T(8,128)(2,1)}, bf16[4,256,704]{2,1,0:T(8,128)(2,1)}, bf16[4,256,704]{2,1,0:T(8,...) custom-call(bf16[4,256,2048]{2,1,0:T(8,128)(2,1)} %get-tuple-element.469.rows_ref.refs_2_, ...), custom_call_target="tpu_custom_call" | custom-call | flops 1000000000 | bytes 1000000 | tf_op jit(solution)/shard_map/pallas_call | solution.py:480
  595.1 8.9 shard_map.311
  604.0 22.5 %shard_map.312 = (bf16[4,256,2048]{2,1,0:T(8,128)(2,1)}, f32[4,256,128]{2,1,0:T(8,128)}, bf16[4,512,128]{2,1,0:T(8,128)(2,1)}, bf16[4,512,256]{2,1,0:T(8,128)(2,1)}, f32[384,2048]{1,0:T(8,128)}) custom-call(bf16[352,2048]{1,0:T(8,128)(2,1)} %collective-permute-done.37.refs_0_, bf16[320,2048]{1,0:T(8,128)(2,1)} %collective-permute-done.44.refs_5_.refs_1_, ...), custom_call_target="tpu_custom_call" | custom-call | flops 1000000000 | bytes 1000000 | tf_op jit(solution)/shard_map/pallas_call | solution.py:401
  650.2 27.7 %shard_map.316 = (bf16[4,256,2048]{2,1,0:T(8,128)(2,1)}, bf16[4,256,2048]{2,1,0:T(8,128)(2,1)}, bf16[4,256,704]{2,1,0:T(8,128)(2,1)}, bf16[4,256,704]{2,1,0:T(8,...) custom-call(bf16[4,256,2048]{2,1,0:T(8,128)(2,1)} %get-tuple-element.519.rows_ref.refs_3_, ...), custom_call_target="tpu_custom_call" | custom-call | flops 1000000000 | bytes 1000000 | tf_op jit(solution)/shard_map/pallas_call | solution.py:480
  715.3 22.4 %shard_map.319 = (bf16[4,256,2048]{2,1,0:T(8,128)(2,1)}, f32[4,256,128]{2,1,0:T(8,128)}, bf16[4,512,128]{2,1,0:T(8,128)(2,1)}, bf16[4,512,256]{2,1,0:T(8,128)(2,1)}, f32[384,2048]{1,0:T(8,128)}) custom-call(bf16[352,2048]{1,0:T(8,128)(2,1)} %copy-done.28, bf16[320,2048]{1,0:T(8,128)(2,1)} %copy-done.22, bf16[864,2048]{1,0:T(8,128)(2,1)} %copy-done.11, ...), custom_call_target="tpu_custom_call" | custom-call | flops 1000000000 | bytes 1000000 | tf_op jit(solution)/shard_map/pallas_call | solution.py:401
  755.9 27.8 %shard_map.320 = (bf16[4,256,2048]{2,1,0:T(8,128)(2,1)}, bf16[4,256,2048]{2,1,0:T(8,128)(2,1)}, bf16[4,256,704]{2,1,0:T(8,128)(2,1)}, bf16[4,256,704]{2,1,0:T(8,...) custom-call(bf16[4,256,2048]{2,1,0:T(8,128)(2,1)} %get-tuple-element.554.rows_ref.refs_0_, ...), custom_call_target="tpu_custom_call" | custom-call | flops 1000000000 | bytes 1000000 | tf_op jit(solution)/shard_map/pallas_call | solution.py:480
  810.7 28.3 %shard_map.324 = (f32[4,704,2048]{2,1,0:T(8,128)}, f32[4,704,2048]{2,1,0:T(8,128)}, f32[4,704,2048]{2,1,0:T(8,128)}) custom-call(bf16[4,256,2048]{2,1,0:T(8,128)(2,1)} %get-tuple-element.554.rows_ref.refs_0_, bf16[4,256,2048]{2,1,0:T(8,128)(2,1)} %get-tuple-element.439.rows_ref.refs_1_, bf16[4,256,2048]{2,1,0:T(8,128)(2,1)} %get-tuple-element.469.rows_ref.refs_2_, ...), custom_call_target="tpu_custom_call" | custom-call | flops 1000000000 | bytes 1000000 | tf_op jit(solution)/shard_map/pallas_call | solution.py:791
  869.5 28.5 %shard_map.328 = (f32[4,704,2048]{2,1,0:T(8,128)}, f32[4,704,2048]{2,1,0:T(8,128)}, f32[4,704,2048]{2,1,0:T(8,128)}) custom-call(bf16[4,256,2048]{2,1,0:T(8,128)(2,1)} %get-tuple-element.554.rows_ref.refs_0_, bf16[4,256,2048]{2,1,0:T(8,128)(2,1)} %get-tuple-element.439.rows_ref.refs_1_, ...), custom_call_target="tpu_custom_call", output_to_operand_aliasing={{0}: (20, {}), {1}: (21, {}), {2}: (22, {})} | custom-call | flops 1000000000 | bytes 1000000 | tf_op jit(solution)/shard_map/pallas_call | solution.py:791
  927.9 9.3 collective-permute-done.86
  963.9 29.0 %shard_map.330 = (bf16[512,1536]{1,0:T(8,128)(2,1)}, bf16[512,2048]{1,0:T(8,128)(2,1)}, f32[512,128]{1,0:T(8,128)}, f32[512,512]{1,0:T(8,128)}, bf16[512,2048]{1,0:T(8,128)(2,1)}) custom-call(bf16[512,2048]{1,0:T(8,128)(2,1)} %get-tuple-element.660.upstream_ref.left_ref, bf16[512,1536]{1,0:T(8,128)(2,1)} %get-tuple-element.647.query_ref, ...), custom_call_target="tpu_custom_call" | custom-call | flops 1000000000 | bytes 1000000 | tf_op jit(solution)/shard_map/pallas_call | solution.py:1009
  998.2 8.8 shard_map.332
  1038.1 14.1 %collective-permute-done.92 = bf16[352,2048]{1,0:T(8,128)(2,1)} collective-permute-done((bf16[352,2048]{1,0:T(8,128)(2,1)}, bf16[352,2048]{1,0:T(8,128)(2,1)}, u32[]{:S(2)}, u32[]{:S(2)}) %collective-permute-start.92) | collective-permute-done | bytes 1441824 | tf_op jit(solution)/shard_map/ppermute | solution.py:102
  1065.3 10.2 shard_map.334
  1163.2 11.2 collective-permute-done.117
  (715 shorter events, 605.9 us)
Async XLA Ops:
  167.5 38.9 %collective-permute-start.25 = (bf16[704,2048]{1,0:T(8,128)(2,1)}, bf16[704,2048]{1,0:T(8,128)(2,1)S(1)}, u32[]{:S(2)}, u32[]{:S(2)}) collective-permute-start(bf16[704,2048]{1,0:T(8,128)(2,1)} %pad_maximum_fusion.4), channel_id=1, source_target_pairs={{0,2},{2,0},{4,6},{6,4},{8,10},{10,8},{12,14},{14,12},{16,18},{18,... | collective-permute-start | bytes 8650760 | tf_op jit(solution)/shard_map/ppermute | solution.py:98
  211.6 53.0 %collective-permute-start.28 = (bf16[672,2048]{1,0:T(8,128)(2,1)}, bf16[672,2048]{1,0:T(8,128)(2,1)S(1)}, u32[]{:S(2)}, u32[]{:S(2)}) collective-permute-start(bf16[672,2048]{1,0:T(8,128)(2,1)} %pad_maximum_fusion.7), channel_id=1, source_target_pairs={{0,2},{2,0},{4,6},{6,4},{8,10},{10,8},{12,14},{14,12},{16,18},{18,... | collective-permute-start | bytes 8257544 | tf_op jit(solution)/shard_map/ppermute | solution.py:98
  214.2 50.4 %all-to-all-start = ((bf16[16,3,88,128]{3,2,1,0:T(8,128)(2,1)}), bf16[16,3,88,128]{3,2,1,0:T(8,128)(2,1)}, u32[]{:S(2)}, u32[]{:S(2)}) async-start(bf16[16,3,88,128]{3,2,1,0:T(8,128)(2,1)} %copy.177), calls=%async_computation | async-start | bytes 2162688 | tf_op jit(solution)/shard_map/all_to_all | solution.py:1269
  222.9 41.7 %collective-permute-start.27 = (bf16[352,2048]{1,0:T(8,128)(2,1)}, bf16[352,2048]{1,0:T(8,128)(2,1)}, u32[]{:S(2)}, u32[]{:S(2)}) collective-permute-start(bf16[352,2048]{1,0:T(8,128)(2,1)} %collective-permute-done.22.refs_0_.refs_8_), channel_id=1, source_target_pairs={{0,4},{2,6},{4,0},{6,2},{8,12},{10,14},{12,8},{14,10},{16,20},{18,... | collective-permute-start | bytes 4325384 | tf_op jit(solution)/shard_map/ppermute | solution.py:98
  355.4 39.9 %collective-permute-start.40 = (bf16[864,2048]{1,0:T(8,128)(2,1)S(1)}, bf16[864,2048]{1,0:T(8,128)(2,1)}, u32[]{:S(2)}, u32[]{:S(2)}) collective-permute-start(bf16[864,2048]{1,0:T(8,128)(2,1)S(1)} %pad_maximum_fusion.1), channel_id=1, source_target_pairs={{0,2},{2,0},{4,6},{6,4},{8,10},{10,8},{12,14},{14,12},{16,18},{18,... | collective-permute-start | bytes 10616840 | tf_op jit(solution)/shard_map/ppermute | solution.py:98
  408.7 71.1 %collective-permute-start.50 = (bf16[704,2048]{1,0:T(8,128)(2,1)}, bf16[704,2048]{1,0:T(8,128)(2,1)}, u32[]{:S(2)}, u32[]{:S(2)}) collective-permute-start(bf16[704,2048]{1,0:T(8,128)(2,1)} %pad_maximum_fusion.6), channel_id=1, source_target_pairs={{0,2},{2,0},{4,6},{6,4},{8,10},{10,8},{12,14},{14,12},{16,18},{18,... | collective-permute-start | bytes 8650760 | tf_op jit(solution)/shard_map/ppermute | solution.py:98
  440.5 50.4 %collective-permute-start.49 = (bf16[704,2048]{1,0:T(8,128)(2,1)}, bf16[704,2048]{1,0:T(8,128)(2,1)}, u32[]{:S(2)}, u32[]{:S(2)}) collective-permute-start(bf16[704,2048]{1,0:T(8,128)(2,1)} %pad_maximum_fusion.5), channel_id=1, source_target_pairs={{0,2},{2,0},{4,6},{6,4},{8,10},{10,8},{12,14},{14,12},{16,18},{18,... | collective-permute-start | bytes 8650760 | tf_op jit(solution)/shard_map/ppermute | solution.py:98
  445.4 45.4 %collective-permute-start.47 = (bf16[480,2048]{1,0:T(8,128)(2,1)}, bf16[480,2048]{1,0:T(8,128)(2,1)S(1)}, u32[]{:S(2)}, u32[]{:S(2)}) collective-permute-start(bf16[480,2048]{1,0:T(8,128)(2,1)} %pad_maximum_fusion.9), channel_id=1, source_target_pairs={{0,1},{1,0},{2,3},{3,2},{4,5},{5,4},{6,7},{7,6},{8,9},{9,8},{10,11... | collective-permute-start | bytes 5898248 | tf_op jit(solution)/shard_map/ppermute | solution.py:94
  490.9 46.3 %collective-permute-start.52 = (bf16[2,512,2048]{2,1,0:T(8,128)(2,1)}, bf16[2,512,2048]{2,1,0:T(8,128)(2,1)}, u32[]{:S(2)}, u32[]{:S(2)}) collective-permute-start(bf16[2,512,2048]{2,1,0:T(8,128)(2,1)} %get-tuple-element.467), channel_id=1, source_target_pairs={{0,2},{2,0},{4,6},{6,4},{8,10},{10,8},{12,14},{14,12},{16,18},{18,... | collective-permute-start | bytes 12582920 | tf_op jit(solution)/shard_map/ppermute | solution.py:98
  495.3 41.8 %collective-permute-start.54 = (bf16[864,2048]{1,0:T(8,128)(2,1)}, bf16[864,2048]{1,0:T(8,128)(2,1)S(1)}, u32[]{:S(2)}, u32[]{:S(2)}) collective-permute-start(bf16[864,2048]{1,0:T(8,128)(2,1)} %pad_maximum_fusion.3), channel_id=1, source_target_pairs={{0,2},{2,0},{4,6},{6,4},{8,10},{10,8},{12,14},{14,12},{16,18},{18,... | collective-permute-start | bytes 10616840 | tf_op jit(solution)/shard_map/ppermute | solution.py:98
  579.5 47.0 %collective-permute-start.58 = (bf16[2,512,2048]{2,1,0:T(8,128)(2,1)}, bf16[2,512,2048]{2,1,0:T(8,128)(2,1)}, u32[]{:S(2)}, u32[]{:S(2)}) collective-permute-start(bf16[2,512,2048]{2,1,0:T(8,128)(2,1)} %get-tuple-element.503), channel_id=1, source_target_pairs={{0,2},{2,0},{4,6},{6,4},{8,10},{10,8},{12,14},{14,12},{16,18},{18,... | collective-permute-start | bytes 12582920 | tf_op jit(solution)/shard_map/ppermute | solution.py:98
  584.3 42.2 %collective-permute-start.59 = (bf16[352,2048]{1,0:T(8,128)(2,1)}, bf16[352,2048]{1,0:T(8,128)(2,1)}, u32[]{:S(2)}, u32[]{:S(2)}) collective-permute-start(bf16[352,2048]{1,0:T(8,128)(2,1)} %pad_maximum_fusion.13), channel_id=1, source_target_pairs={{0,4},{2,6},{4,0},{6,2},{8,12},{10,14},{12,8},{14,10},{16,20},{18,... | collective-permute-start | bytes 4325384 | tf_op jit(solution)/shard_map/ppermute | solution.py:98
  642.8 43.2 %collective-permute-start.64 = (bf16[2,512,2048]{2,1,0:T(8,128)(2,1)}, bf16[2,512,2048]{2,1,0:T(8,128)(2,1)}, u32[]{:S(2)}, u32[]{:S(2)}) collective-permute-start(bf16[2,512,2048]{2,1,0:T(8,128)(2,1)} %shard_map.315), channel_id=1, source_target_pairs={{0,2},{2,0},{4,6},{6,4},{8,10},{10,8},{12,14},{14,12},{16,18},{18,... | collective-permute-start | bytes 12582920 | tf_op jit(solution)/shard_map/ppermute | solution.py:98
  646.0 39.9 %collective-permute-start.65 = (bf16[352,2048]{1,0:T(8,128)(2,1)}, bf16[352,2048]{1,0:T(8,128)(2,1)}, u32[]{:S(2)}, u32[]{:S(2)}) collective-permute-start(bf16[352,2048]{1,0:T(8,128)(2,1)} %pad_maximum_fusion.14), channel_id=1, source_target_pairs={{0,4},{2,6},{4,0},{6,2},{8,12},{10,14},{12,8},{14,10},{16,20},{18,... | collective-permute-start | bytes 4325384 | tf_op jit(solution)/shard_map/ppermute | solution.py:98
  647.5 38.4 %collective-permute-start.62 = (bf16[352,2048]{1,0:T(8,128)(2,1)}, bf16[352,2048]{1,0:T(8,128)(2,1)}, u32[]{:S(2)}, u32[]{:S(2)}) collective-permute-start(bf16[352,2048]{1,0:T(8,128)(2,1)} %maximum_add_fusion.3), channel_id=1, source_target_pairs={{0,8},{2,10},{4,12},{6,14},{8,16},{10,18},{12,20},{14,22},{16,24},... | collective-permute-start | bytes 4325384 | tf_op jit(solution)/shard_map/ppermute | solution.py:102
  647.5 38.4 %collective-permute-start.63 = (bf16[2,160,2048]{2,1,0:T(8,128)(2,1)}, bf16[2,160,2048]{2,1,0:T(8,128)(2,1)}, u32[]{:S(2)}, u32[]{:S(2)}) collective-permute-start(bf16[2,160,2048]{2,1,0:T(8,128)(2,1)} %get-tuple-element.531), channel_id=1, source_target_pairs={{0,1},{1,0},{2,3},{3,2},{4,5},{5,4},{6,7},{7,6},{8,9},{9,8},{10,11... | collective-permute-start | bytes 3932168 | tf_op jit(solution)/shard_map/ppermute | solution.py:94
  650.2 65.2 %collective-permute-start.66 = (bf16[160,2048]{1,0:T(8,128)(2,1)}, bf16[160,2048]{1,0:T(8,128)(2,1)}, u32[]{:S(2)}, u32[]{:S(2)}) collective-permute-start(bf16[160,2048]{1,0:T(8,128)(2,1)} %get-tuple-element.885), channel_id=1, source_target_pairs={{0,2},{2,0},{4,6},{6,4},{8,10},{10,8},{12,14},{14,12},{16,18},{18,... | collective-permute-start | bytes 1966088 | tf_op jit(solution)/shard_map/ppermute | solution.py:98
  691.8 46.2 %collective-permute-start.67 = (bf16[2,512,2048]{2,1,0:T(8,128)(2,1)}, bf16[2,512,2048]{2,1,0:T(8,128)(2,1)}, u32[]{:S(2)}, u32[]{:S(2)}) collective-permute-start(bf16[2,512,2048]{2,1,0:T(8,128)(2,1)} %get-tuple-element.550), channel_id=1, source_target_pairs={{0,2},{2,0},{4,6},{6,4},{8,10},{10,8},{12,14},{14,12},{16,18},{18,... | collective-permute-start | bytes 12582920 | tf_op jit(solution)/shard_map/ppermute | solution.py:98
  695.8 42.2 %collective-permute-start.69 = (bf16[2,160,2048]{2,1,0:T(8,128)(2,1)}, bf16[2,160,2048]{2,1,0:T(8,128)(2,1)}, u32[]{:S(2)}, u32[]{:S(2)}) collective-permute-start(bf16[2,160,2048]{2,1,0:T(8,128)(2,1)} %get-tuple-element.540), channel_id=1, source_target_pairs={{0,1},{1,0},{2,3},{3,2},{4,5},{5,4},{6,7},{7,6},{8,9},{9,8},{10,11... | collective-permute-start | bytes 3932168 | tf_op jit(solution)/shard_map/ppermute | solution.py:94
  748.4 41.0 %collective-permute-start.73 = (bf16[2,512,2048]{2,1,0:T(8,128)(2,1)}, bf16[2,512,2048]{2,1,0:T(8,128)(2,1)}, u32[]{:S(2)}, u32[]{:S(2)}) collective-permute-start(bf16[2,512,2048]{2,1,0:T(8,128)(2,1)} %shard_map.323), channel_id=1, source_target_pairs={{0,2},{2,0},{4,6},{6,4},{8,10},{10,8},{12,14},{14,12},{16,18},{18,... | collective-permute-start | bytes 12582920 | tf_op jit(solution)/shard_map/ppermute | solution.py:98
  750.0 39.3 %collective-permute-start.74 = (bf16[352,2048]{1,0:T(8,128)(2,1)S(1)}, bf16[352,2048]{1,0:T(8,128)(2,1)}, u32[]{:S(2)}, u32[]{:S(2)}) collective-permute-start(bf16[352,2048]{1,0:T(8,128)(2,1)S(1)} %pad_maximum_fusion.16), channel_id=1, source_target_pairs={{0,4},{2,6},{4,0},{6,2},{8,12},{10,14},{12,8},{14,10},{16,20},{18,... | collective-permute-start | bytes 4325384 | tf_op jit(solution)/shard_map/ppermute | solution.py:98
  750.7 38.6 %collective-permute-start.71 = (bf16[352,2048]{1,0:T(8,128)(2,1)}, bf16[352,2048]{1,0:T(8,128)(2,1)}, u32[]{:S(2)}, u32[]{:S(2)}) collective-permute-start(bf16[352,2048]{1,0:T(8,128)(2,1)} %fusion.8), channel_id=1, source_target_pairs={{0,8},{2,10},{4,12},{6,14},{8,16},{10,18},{12,20},{14,22},{16,24},... | collective-permute-start | bytes 4325384 | tf_op jit(solution)/shard_map/ppermute | solution.py:102
  789.4 49.7 %collective-permute-start.75 = (bf16[2,512,2048]{2,1,0:T(8,128)(2,1)}, bf16[2,512,2048]{2,1,0:T(8,128)(2,1)}, u32[]{:S(2)}, u32[]{:S(2)}) collective-permute-start(bf16[2,512,2048]{2,1,0:T(8,128)(2,1)} %get-tuple-element.596), channel_id=1, source_target_pairs={{0,2},{2,0},{4,6},{6,4},{8,10},{10,8},{12,14},{14,12},{16,18},{18,... | collective-permute-start | bytes 12582920 | tf_op jit(solution)/shard_map/ppermute | solution.py:98
  849.3 49.0 %collective-permute-start.81 = (bf16[2,512,2048]{2,1,0:T(8,128)(2,1)}, bf16[2,512,2048]{2,1,0:T(8,128)(2,1)}, u32[]{:S(2)}, u32[]{:S(2)}) collective-permute-start(bf16[2,512,2048]{2,1,0:T(8,128)(2,1)} %shard_map.327), channel_id=1, source_target_pairs={{0,2},{2,0},{4,6},{6,4},{8,10},{10,8},{12,14},{14,12},{16,18},{18,... | collective-permute-start | bytes 12582920 | tf_op jit(solution)/shard_map/ppermute | solution.py:98
  856.3 41.9 %collective-permute-start.79 = (bf16[352,2048]{1,0:T(8,128)(2,1)}, bf16[352,2048]{1,0:T(8,128)(2,1)}, u32[]{:S(2)}, u32[]{:S(2)}) collective-permute-start(bf16[352,2048]{1,0:T(8,128)(2,1)} %fusion.10), channel_id=1, source_target_pairs={{0,8},{2,10},{4,12},{6,14},{8,16},{10,18},{12,20},{14,22},{16,24},... | collective-permute-start | bytes 4325384 | tf_op jit(solution)/shard_map/ppermute | solution.py:102
  860.3 37.8 %collective-permute-start.82 = (bf16[192,2048]{1,0:T(8,128)(2,1)}, bf16[192,2048]{1,0:T(8,128)(2,1)}, u32[]{:S(2)}, u32[]{:S(2)}) collective-permute-start(bf16[192,2048]{1,0:T(8,128)(2,1)} %slice_bitcast_fusion.4), channel_id=1, source_target_pairs={{0,4},{2,6},{4,0},{6,2},{8,12},{10,14},{12,8},{14,10},{16,20},{18,... | collective-permute-start | bytes 2359304 | tf_op jit(solution)/shard_map/ppermute | solution.py:98
  950.9 47.3 %collective-permute-start.88 = (bf16[8,128,1024]{2,1,0:T(8,128)(2,1)}, bf16[8,128,1024]{2,1,0:T(8,128)(2,1)}, u32[]{:S(2)}, u32[]{:S(2)}) collective-permute-start(bf16[8,128,1024]{2,1,0:T(8,128)(2,1)} %shard_map.331), channel_id=1, source_target_pairs={{0,2},{2,0},{4,6},{6,4},{8,10},{10,8},{12,14},{14,12},{16,18},{18,... | collective-permute-start | bytes 6291464 | tf_op jit(solution)/shard_map/ppermute | solution.py:98
  954.8 43.4 %collective-permute-start.89 = (bf16[352,2048]{1,0:T(8,128)(2,1)}, bf16[352,2048]{1,0:T(8,128)(2,1)}, u32[]{:S(2)}, u32[]{:S(2)}) collective-permute-start(bf16[352,2048]{1,0:T(8,128)(2,1)} %pad_maximum_fusion.18), channel_id=1, source_target_pairs={{0,4},{2,6},{4,0},{6,2},{8,12},{10,14},{12,8},{14,10},{16,20},{18,... | collective-permute-start | bytes 4325384 | tf_op jit(solution)/shard_map/ppermute | solution.py:98
  957.6 54.8 %all-to-all-start.2 = ((bf16[16,3,88,128]{3,2,1,0:T(8,128)(2,1)}), bf16[16,3,88,128]{3,2,1,0:T(8,128)(2,1)S(1)}, u32[]{:S(2)}, u32[]{:S(2)}) async-start(bf16[16,3,88,128]{3,2,1,0:T(8,128)(2,1)} %copy.191), calls=%async_computation.2 | async-start | bytes 2162688 | tf_op jit(solution)/shard_map/all_to_all | solution.py:1597
  1007.0 45.2 %collective-permute-start.90 = (bf16[8,128,2048]{2,1,0:T(8,128)(2,1)}, bf16[8,128,2048]{2,1,0:T(8,128)(2,1)}, u32[]{:S(2)}, u32[]{:S(2)}) collective-permute-start(bf16[8,128,2048]{2,1,0:T(8,128)(2,1)} %shard_map.332), channel_id=1, source_target_pairs={{0,2},{2,0},{4,6},{6,4},{8,10},{10,8},{12,14},{14,12},{16,18},{18,... | collective-permute-start | bytes 12582920 | tf_op jit(solution)/shard_map/ppermute | solution.py:98
  1011.1 72.6 %collective-permute-start.96 = (bf16[256,1024]{1,0:T(8,128)(2,1)}, bf16[256,1024]{1,0:T(8,128)(2,1)}, u32[]{:S(2)}, u32[]{:S(2)}) collective-permute-start(bf16[256,1024]{1,0:T(8,128)(2,1)} %get-tuple-element.892), channel_id=1, source_target_pairs={{0,1},{1,0},{2,3},{3,2},{4,5},{5,4},{6,7},{7,6},{8,9},{9,8},{10,11... | collective-permute-start | bytes 1572872 | tf_op jit(solution)/shard_map/ppermute | solution.py:94
  1027.3 57.0 %collective-permute-start.93 = (bf16[352,2048]{1,0:T(8,128)(2,1)}, bf16[352,2048]{1,0:T(8,128)(2,1)}, u32[]{:S(2)}, u32[]{:S(2)}) collective-permute-start(bf16[352,2048]{1,0:T(8,128)(2,1)} %pad_maximum_fusion.19), channel_id=1, source_target_pairs={{0,4},{2,6},{4,0},{6,2},{8,12},{10,14},{12,8},{14,10},{16,20},{18,... | collective-permute-start | bytes 4325384 | tf_op jit(solution)/shard_map/ppermute | solution.py:98
  (211 other events, 3248.2 us)

commit v3 on v2

--- a/solution.py
+++ b/solution.py
@@ -230,11 +230,10 @@
 
 
 FAMILIES = 4
-VMEM_BYTES = 60 * 1024 * 1024
-
-
-def kernel_params(**extra):
-    return pltpu.CompilerParams(vmem_limit_bytes=VMEM_BYTES, **extra)
+
+
+def kernel_params(mebibytes):
+    return pltpu.CompilerParams(vmem_limit_bytes=mebibytes * 1024 * 1024)
 
 
 def short_cost():
@@ -341,7 +340,7 @@
             pltpu.VMEM((FAMILIES, tokens, width), jnp.bfloat16),
             pltpu.SemaphoreType.DMA((FAMILIES, 2)),
         ],
-        compiler_params=kernel_params(),
+        compiler_params=kernel_params(32),
         cost_estimate=short_cost(),
     )(*pieces, codes, last)
 
@@ -428,7 +427,7 @@
             pltpu.SemaphoreType.DMA((FAMILIES, 2)),
             pltpu.SemaphoreType.DMA((FAMILIES, 2)),
         ],
-        compiler_params=kernel_params(),
+        compiler_params=kernel_params(48),
         cost_estimate=short_cost(),
     )(*pieces, *grad_pieces, codes, router, pair, hidden_grads)
 
@@ -490,7 +489,7 @@
             jax.ShapeDtypeStruct((count, slots, units), jnp.bfloat16),
             jax.ShapeDtypeStruct((count, slots, 128), jnp.float32),
         ],
-        compiler_params=kernel_params(),
+        compiler_params=kernel_params(56),
         cost_estimate=short_cost(),
     )(slot_rows, slot_grads, gates, expert_gate, expert_up, expert_down)
 
@@ -551,7 +550,7 @@
         in_specs=in_specs,
         out_specs=out_specs,
         out_shape=out_shape,
-        compiler_params=kernel_params(),
+        compiler_params=kernel_params(24),
         cost_estimate=short_cost(),
     )(*operands)
 
@@ -589,40 +588,42 @@
     return pl.pallas_call(
         body,
         out_shape=jax.ShapeDtypeStruct((block, columns), jnp.bfloat16),
-        compiler_params=kernel_params(),
+        compiler_params=kernel_params(16),
         cost_estimate=short_cost(),
     )(query_weight, expand_weight, output_weight, latent_weight, router_weight, routes)
 
 
-def unpack_grads(output, wide, narrow, widths):
-    block = wide.shape[0]
+def unpack_grads(output, joined, widths):
+    block = joined.shape[0]
     query_width, expand_width, latent_width = widths
+    edge = query_width + expand_width
     parts = 4
     share = block // parts
 
-    def body(sum_ref, wide_ref, narrow_ref, output_ref, query_ref, expand_ref, latent_ref, router_ref):
+    def body(sum_ref, joined_ref, output_ref, query_ref, expand_ref, latent_ref, router_ref):
         output_ref[...] = sum_ref[...].astype(jnp.float32).T
-        query_ref[...] = head_columns(wide_ref[:, :query_width]).astype(jnp.float32)
+        query_ref[...] = head_columns(joined_ref[:, :query_width]).astype(jnp.float32)
         for i in range(parts):
-            expand_ref[:, expand_width * i : expand_width * (i + 1)] = wide_ref[
-                share * i : share * (i + 1), query_width:
+            expand_ref[:, expand_width * i : expand_width * (i + 1)] = joined_ref[
+                share * i : share * (i + 1), query_width:edge
             ].astype(jnp.float32)
-        latent_ref[...] = narrow_ref[:, :latent_width].astype(jnp.float32)
-        router_ref[...] = narrow_ref[:, latent_width:].astype(jnp.float32)
+        narrow = joined_ref[:, edge:].astype(jnp.float32)
+        latent_ref[...] = narrow[:, :latent_width]
+        router_ref[...] = narrow[:, latent_width:]
 
     shapes = [
         (output.shape[1], block),
         (block, query_width),
         (share, expand_width * parts),
         (block, latent_width),
-        (block, narrow.shape[1] - latent_width),
+        (block, joined.shape[1] - edge - latent_width),
     ]
     return pl.pallas_call(
         body,
         out_shape=[jax.ShapeDtypeStruct(shape, jnp.float32) for shape in shapes],
-        compiler_params=kernel_params(),
+        compiler_params=kernel_params(16),
         cost_estimate=short_cost(),
-    )(output, wide, narrow)
+    )(output, joined)
 
 
 def block_grads(places, left, right, tile, core, turned=None, expanded=None, received=None):
@@ -693,9 +694,111 @@
             ],
         ),
         out_shape=jax.ShapeDtypeStruct(shape, jnp.bfloat16),
-        compiler_params=kernel_params(),
+        compiler_params=kernel_params(40),
         cost_estimate=short_cost(),
     )(places, *operands)
+
+
+def joined_grads(
+    places, normed, query_back, turned, expanded, latent_back, normed_two, logit_grads, wide, narrow
+):
+    count, width = normed.shape
+    block = width // (4 * PLANES)
+    blocks = 2 * PLANES
+    query_width = query_back.shape[1]
+    tile = 384
+    steps = query_width // tile
+    share = turned.shape[0] // (4 * PLANES)
+    quarter = expanded.shape[1] // steps
+    latent_width = latent_back.shape[1]
+    edge = query_width + quarter
+
+    def body(
+        places_ref,
+        normed_ref,
+        query_ref,
+        turned_ref,
+        expanded_ref,
+        latent_ref,
+        two_ref,
+        logit_ref,
+        wide_ref,
+        narrow_ref,
+        out_ref,
+        held,
+        held_turned,
+        held_two,
+    ):
+        step = pl.program_id(0)
+
+        @pl.when(step == 0)
+        def _():
+            for i in range(blocks):
+                place = places_ref[2 * i]
+                start = pl.multiple_of(place * block, block)
+                held[:, block * i : block * (i + 1)] = normed_ref[:, pl.ds(start, block)]
+                held_two[:, block * i : block * (i + 1)] = two_ref[:, pl.ds(start, block)]
+                start = pl.multiple_of(place * share, share)
+                held_turned[share * i : share * (i + 1)] = turned_ref[pl.ds(start, share)]
+            part = jnp.concatenate(
+                [
+                    dot_first(held[...], latent_ref[...]),
+                    dot_first(held_two[...], logit_ref[...]),
+                ],
+                axis=1,
+            ).reshape(blocks, block, narrow.shape[2])
+            part = part + narrow_ref[...].astype(jnp.float32)
+            out_ref[:, :, edge:] = part.astype(jnp.bfloat16)
+
+        lanes = pl.ds(pl.multiple_of(step * tile, 128), tile)
+        part = dot_first(held[...], query_ref[...]).reshape(blocks, block, tile)
+        part = part + wide_ref[:, :, lanes].astype(jnp.float32)
+        out_ref[:, :, lanes] = part.astype(jnp.bfloat16)
+        lines = pl.ds(pl.multiple_of(step * share, share), share)
+        part = dot_plain(held_turned[...], expanded_ref[...]).reshape(blocks, share, quarter)
+        part = part + wide_ref[:, lines, query_width:].astype(jnp.float32)
+        out_ref[:, lines, query_width:edge] = part.astype(jnp.bfloat16)
+
+    whole = lambda shape: pl.BlockSpec(shape, lambda h, places_ref: (0,) * len(shape))
+    shape = (blocks, block, edge + narrow.shape[2])
+    return pl.pallas_call(
+        body,
+        grid_spec=pltpu.PrefetchScalarGridSpec(
+            num_scalar_prefetch=1,
+            grid=(steps,),
+            in_specs=[
+                whole(normed.shape),
+                pl.BlockSpec((count, tile), lambda h, places_ref: (0, h)),
+                whole(turned.shape),
+                pl.BlockSpec((count, quarter), lambda h, places_ref: (0, h)),
+                whole(latent_back.shape),
+                whole(normed_two.shape),
+                whole(logit_grads.shape),
+                whole(wide.shape),
+                whole(narrow.shape),
+            ],
+            out_specs=whole(shape),
+            scratch_shapes=[
+                pltpu.VMEM((count, blocks * block), jnp.bfloat16),
+                pltpu.VMEM((blocks * share, count), jnp.bfloat16),
+                pltpu.VMEM((count, blocks * block), jnp.bfloat16),
+            ],
+        ),
+        out_shape=jax.ShapeDtypeStruct(shape, jnp.bfloat16),
+        compiler_params=kernel_params(40),
+        cost_estimate=short_cost(),
+    )(
+        places,
+        normed,
+        query_back,
+        turned,
+        expanded,
+        latent_back,
+        normed_two,
+        logit_grads,
+        wide,
+        narrow,
+    )
 
 
 def narrow_grads(places, normed, latent_back, normed_two, logit_grads, core):
@@ -721,7 +824,7 @@
             out_specs=pl.BlockSpec((1, block, sum(widths)), lambda i, places_ref: (i, 0, 0)),
         ),
         out_shape=jax.ShapeDtypeStruct((2 * PLANES, block, sum(widths)), jnp.bfloat16),
-        compiler_params=kernel_params(),
+        compiler_params=kernel_params(24),
         cost_estimate=short_cost(),
     )(places, normed, normed_two, latent_back, logit_grads)
 
@@ -757,7 +860,7 @@
             pltpu.SemaphoreType.DMA((count,)),
             pltpu.SemaphoreType.DMA((count,)),
         ],
-        compiler_params=kernel_params(),
+        compiler_params=kernel_params(24),
         cost_estimate=short_cost(),
     )(places, *blocks)
 
@@ -797,7 +900,7 @@
         out_specs=[result] * 3,
         out_shape=[jax.ShapeDtypeStruct((experts, units, width), jnp.float32)] * 3,
         input_output_aliases={5 * planes + i: i for i in range(len(earlier))},
-        compiler_params=kernel_params(),
+        compiler_params=kernel_params(52),
         cost_estimate=short_cost(),
     )(*rows, *grads, *gate_backs, *up_backs, *hiddens, *earlier)
 
@@ -921,7 +1024,7 @@
             jax.ShapeDtypeStruct((count, width), jnp.bfloat16),
         ],
         scratch_shapes=[pltpu.VMEM((count, width), jnp.float32)],
-        compiler_params=kernel_params(),
+        compiler_params=kernel_params(44),
         cost_estimate=short_cost(),
     )(normed, latent_normed, *ropes, *turns, *segments, flat, quarters, flat)
 
@@ -1038,7 +1141,7 @@
             jax.ShapeDtypeStruct((count, width), jnp.bfloat16),
         ],
         scratch_shapes=[pltpu.VMEM((count, width), jnp.float32)],
-        compiler_params=kernel_params(),
+        compiler_params=kernel_params(52),
         cost_estimate=short_cost(),
     )(upstream, query, keys, *ropes, *turns, *segments, flat, quarters, flat)
 
@@ -1124,12 +1227,13 @@
         jnp.concatenate([out_grad_other, out_grad], axis=1),
     )
     grad_rows = Spread(sent_rows(upstream_bf16, first))
-    blocks[12], blocks[10], blocks[5], blocks[7], got = together(
+    blocks[12], blocks[10], blocks[5], blocks[7], got, shared_packed = together(
         turn_planes(blocks[8]),
         swap_rows(blocks[8], 2),
         swap_rows(blocks[4], 1),
         swap_rows(blocks[6], 1),
         swap_cols(grad_rows.sent((0, 0))[0]),
+        shared_packed,
     )
     grad_rows.got(got, [0], (0, 0))
     source = jnp.where(
@@ -1163,7 +1267,7 @@
         blocks[9],
         blocks[11],
         passed,
-        shared_packed,
+        shared_here,
         normed_one,
         cosine,
         sine,
@@ -1174,7 +1278,7 @@
         swap_rows(blocks[8], 1),
         swap_rows(blocks[10], 1),
         swap_rows(passed, 1),
-        shared_packed,
+        lax.all_to_all(shared_packed, "row", split_axis=0, concat_axis=0, tiled=True),
         normed_one,
         cosine,
         sine,
@@ -1261,14 +1365,10 @@
     )
     (
         attended_other,
-        shared_here,
         grad_rows.held[2, 1],
         passed,
     ) = together(
         swap_cols(partner_part),
-        lax.all_to_all(
-            after(shared_packed, attended_part), "row", split_axis=0, concat_axis=0, tiled=True
-        ),
         grad_rows.cross(2),
         swap_rows(passed, 1),
     )
@@ -1596,12 +1696,6 @@
     unique_mine = back[COMMON:] + unique_rest[0] + unique_crossed
     shared_grads = lax.all_to_all(shared_grads, "row", split_axis=0, concat_axis=0, tiled=True)
     unique_other = swap_cols(unique_mine)
-    shared_grads = shared_grads.transpose(1, 0, 2, 3).reshape(3, row_devices * shared_share, -1)
-    shared_grads = shared_grads.astype(f32)
-    shared_gate_grad = shared_grads[0].T
-    shared_up_grad = shared_grads[1].T
-    shared_down_grad = shared_grads[2]
-
     upstream = upstream_bf16.astype(f32)
     normed_two_back = router_back + jnp.concatenate(
         [
@@ -1624,14 +1718,14 @@
     query_back, expanded_back, key_rope_back, latent_normed_back, input_part = attend_back(
         attended_back, query, keys, ropes, turns, segments, dense, RANK
     )
-    query_back, last_unique, output_got, sum_crossed = together(
+    query_back, shared_grads, last_unique, output_got, sum_crossed = together(
         query_back,
+        shared_grads,
         unique_out(sum_mine_0),
         swap_rows(output_sibling, 1),
-        across_out(sum_mine_3, sum_unique),
+        across_out(after(sum_mine_3, unique_other), sum_unique),
     )
     result = result + own_sum(sum_mine_3, sum_unique, sum_crossed)
-
     latent_gain_part = jnp.sum(latent_normed_back * latent_unit, axis=0)
     latent_weighted = latent_normed_back * latent_gain
     compressed_back = latent_scale * (
@@ -1643,70 +1737,69 @@
     latent_part = jnp.concatenate([compressed_back, rope_back], axis=1).astype(bf16)
     latent_turned = latent_normed.T
     wide_sibling = block_grads(
-        arrival, normed_one, query_back, 384, 1, latent_turned, expanded_back
-    )
-    wide_sibling, latent_part = together(wide_sibling, latent_part)
+        arrival, normed_one, after(query_back, latent_part), 384, 1, latent_turned, expanded_back
+    )
+    latent_other, wide_sibling = together(swap_cols(latent_part), wide_sibling)
+    latent_back = (latent_part.astype(f32) + latent_other.astype(f32)).astype(bf16)
+    narrow_sibling = narrow_grads(arrival, normed_one, latent_back, normed_two, logit_grads, 1)
+    weighted_part = jnp.sum(
+        after(input_part, wide_sibling).astype(f32) * gain_one * unit_one, axis=1
+    )
+    wide_got, narrow_sibling, weighted_part = together(
+        swap_rows(wide_sibling, 1), narrow_sibling, weighted_part
+    )
     output_total = by_plane(
         block_grads(
-            arrival, after(attended_back, wide_sibling), mixed, 256, 0, received=output_got
+            arrival, after(attended_back, narrow_sibling), mixed, 256, 0, received=output_got
         )
     )
-    weighted_part = jnp.sum(
-        after(input_part, wide_sibling).astype(f32) * gain_one * unit_one, axis=1
-    )
-    wide_got, latent_other, output_total, weighted_part, result = together(
-        swap_rows(wide_sibling, 1),
-        swap_cols(latent_part),
+    input_sent = other_columns(input_part, first)
+    small_part = jnp.concatenate([weighted_part, latent_gain_part]).reshape(-1, 128)
+    narrow_got = swap_rows(narrow_sibling, 1)
+    small_other, narrow_got, output_total, sum_crossed, result = together(
+        swap_cols(small_part),
+        narrow_got,
         output_total,
-        weighted_part,
+        across_out(sum_mine_0, last_unique),
         turn_planes(result),
     )
-    latent_back = (latent_part.astype(f32) + latent_other.astype(f32)).astype(bf16)
-    wide_total = by_plane(
-        block_grads(
-            arrival, normed_one, query_back, 384, 0, latent_turned, expanded_back, wide_got
+    sum_sent = result + own_sum(sum_mine_0, last_unique, sum_crossed)
+    joined_total = by_plane(
+        joined_grads(
+            arrival,
+            normed_one,
+            query_back,
+            latent_turned,
+            expanded_back,
+            latent_back,
+            normed_two,
+            logit_grads,
+            wide_got,
+            narrow_got,
         )
     )
-    narrow_sibling = narrow_grads(
-        arrival, normed_one, after(latent_back, wide_total), normed_two, logit_grads, 1
-    )
-    input_sent = other_columns(input_part, first)
-    half_rows = rows_count // 2
-    small_part = jnp.concatenate([weighted_part, latent_gain_part]).reshape(-1, 128)
-    wide_total, narrow_sibling, sum_crossed, crossed_output, input_low, small_other = together(
-        wide_total,
-        narrow_sibling,
-        across_out(sum_mine_0, last_unique),
-        [swap_rows(output_total[p, 1], 2) for p in (1, 2)],
-        swap_cols(input_sent[:half_rows]),
-        swap_cols(small_part),
-    )
-    sum_sent = result + own_sum(sum_mine_0, last_unique, sum_crossed)
-    output_sums = [output_total[p, 0] + crossed_output[p - 1] for p in (1, 2)]
-    narrow_mine = narrow_grads(
-        arrival, normed_one, latent_back, after(normed_two, wide_total), logit_grads, 0
-    )
-    crossed, crossed_output, moved_output, narrow_got, narrow_mine, input_high = together(
-        swap_rows(wide_total[1, 1], 2),
-        swap_rows(output_total[3, 1], 2),
+    joined_total, crossed_output, input_other = together(
+        joined_total,
+        swap_rows(output_total[1:, 1], 2),
+        swap_cols(after(input_sent, small_other)),
+    )
+    output_sums = [output_total[p, 0] + crossed_output[p - 1] for p in (1, 2, 3)]
+
+    crossed, crossed_output, moved_output, combined_other = together(
+        swap_rows(joined_total[1, 1], 2),
+        swap_rows(output_total[0, 1], 2),
         turn_planes(output_sums[0]),
-        swap_rows(narrow_sibling, 1),
-        narrow_mine,
-        swap_cols(input_sent[half_rows:]),
-    )
-    output_sums.append(output_total[3, 0] + crossed_output)
-    moving = [wide_total[1, 0] + crossed]
+        swap_cols(other_columns(sum_sent, first)),
+    )
+    moving = joined_total[1, 0] + crossed
     moving_output = output_sums[1] + moved_output
-    narrow_total = by_plane(narrow_mine + narrow_got)
-    crossed, moved, moved_output, crossed_narrow, combined_other = together(
-        swap_rows(wide_total[2, 1], 2),
-        turn_planes(moving[0]),
-        turn_planes(moving_output),
-        swap_rows(narrow_total[1, 1], 2),
-        swap_cols(other_columns(sum_sent, first)),
-    )
-    moving = [wide_total[2, 0] + crossed + moved, narrow_total[1, 0] + crossed_narrow]
-    moving_output = output_sums[2] + moved_output
+    last_output = output_total[0, 0] + crossed_output
+
+    shared_grads = after(shared_grads, joined_total).transpose(1, 0, 2, 3).reshape(3, row_devices * shared_share, -1)
+    shared_grads = shared_grads.astype(f32)
+    shared_gate_grad = shared_grads[0].T
+    shared_up_grad = shared_grads[1].T
+    shared_down_grad = shared_grads[2]
 
     latent_input = jnp.einsum("tc,dc->td", latent_back, latent_full, preferred_element_type=f32)
     small_sum = (small_part + small_other).reshape(-1)
@@ -1714,7 +1807,7 @@
     weighted_sum = weighted_sum + jnp.sum(latent_input * gain_one * unit_one, axis=1)
     normed_one_back = (
         own_columns(input_part, first).astype(f32)
-        + jnp.concatenate([input_low, input_high], axis=0).astype(f32)
+        + input_other.astype(f32)
         + own_columns(latent_input, first)
     )
     own_unit = own_columns(unit_one, first)
@@ -1725,45 +1818,37 @@
     gain_grads = jnp.concatenate(
         [norm_gain_part, own_columns(ffn_gain_part, first), small_sum[rows_count:]]
     ).reshape(-1, 128)
-    crossed, crossed_narrow, moved, crossed_output, gain_grads = together(
-        swap_rows(wide_total[3, 1], 2),
-        swap_rows(narrow_total[2, 1], 2),
-        [turn_planes(part) for part in moving],
-        swap_rows(output_total[0, 1], 2),
-        gain_grads,
-    )
-    moving = [
-        wide_total[3, 0] + crossed + moved[0],
-        narrow_total[2, 0] + crossed_narrow + moved[1],
-    ]
-    crossed, crossed_narrow, moved, moved_output = together(
-        swap_rows(wide_total[0, 1], 2),
-        swap_rows(narrow_total[3, 1], 2),
-        [turn_planes(part) for part in moving],
+    crossed, moved, moved_output, gains_other = together(
+        swap_rows(joined_total[2, 1], 2),
+        turn_planes(moving),
         turn_planes(moving_output),
-    )
-    moving_output = output_total[0, 0] + crossed_output + moved_output
-    moving = [
-        wide_total[0, 0] + crossed + moved[0],
-        narrow_total[3, 0] + crossed_narrow + moved[1],
-    ]
-    crossed_narrow, moved, others = together(
-        swap_rows(narrow_total[0, 1], 2),
-        turn_planes(moving[1]),
-        [swap_rows(gain_grads, bits) for bits in (1, 2, 3)],
-    )
-    moving[1] = narrow_total[0, 0] + crossed_narrow + moved
-    gain_grads = (gain_grads + others[0]) + (others[1] + others[2])
-    others = [swap_rows(gain_grads, bits) for bits in (4, 8, 12)]
-    gain_grads = (gain_grads + others[0]) + (others[1] + others[2])
-    gain_grads = gain_grads.reshape(-1)
+        swap_rows(gain_grads, 1),
+    )
+    moving = joined_total[2, 0] + crossed + moved
+    moving_output = output_sums[2] + moved_output
+    gain_grads = gain_grads + gains_other
+    crossed, moved, moved_output, gains_other = together(
+        swap_rows(joined_total[3, 1], 2),
+        turn_planes(moving),
+        turn_planes(moving_output),
+        swap_rows(gain_grads, 2),
+    )
+    moving = joined_total[3, 0] + crossed + moved
+    moving_output = last_output + moved_output
+    gain_grads = gain_grads + gains_other
+    crossed, moved, others = together(
+        swap_rows(joined_total[0, 1], 2),
+        turn_planes(moving),
+        [swap_rows(gain_grads, bits) for bits in (4, 8, 12)],
+    )
+    moving = joined_total[0, 0] + crossed + moved
+    gain_grads = ((gain_grads + others[0]) + (others[1] + others[2])).reshape(-1)
     output_grad, query_grad, expand_grad, latent_grad, router_grad = unpack_grads(
-        moving_output, *moving, (query_width, quarter, latent_width)
+        moving_output, moving, (query_width, quarter, latent_width)
     )
 
     combined = merge_rows(own_columns(sum_sent, first), combined_other, first)
     output = (own_columns(middle, first) + combined).astype(bf16)
-
     width_share = norm_gain.shape[0]
     norm_gain_grad = gain_grads[:width_share]
     ffn_gain_grad = gain_grads[width_share : 2 * width_share]

time: 1210 us -> 1170 us (0.967)
  Pallas kernels: 503 us -> 437 us
  local copies, waits for them, and re-layouts: 100 us -> 145 us
  waiting for transfers between devices: 311 us -> 283 us
    unnamed x231 -> x475, local copies, waits for them, and re-layouts: 20 us -> 77.8 us
    pallas_call x16, Pallas kernels: 94.3 us -> 70.1 us  [sum_tokens(): pl.pallas_call(body, grid=(2,), in_specs=in_specs, out_specs=out_specs, o...]
    pallas_call x4 -> x3, Pallas kernels: 33.1 us -> 16.1 us  [block_grads(): pl.pallas_call(body, grid_spec=pltpu.PrefetchScalarGridSpec(num_scalar_pr...]
    ppermute x24 -> x21, waiting for transfers between devices: 80.3 us -> 64.3 us  [turn_planes(): return lax.ppermute(values, 'row', [(i, (i + 4) % 16) for i in range(16)])]
    ppermute x73 -> x66, waiting for transfers between devices: 82.3 us -> 66.5 us  [swap_rows(): return lax.ppermute(values, 'row', [(i, i ^ bit) for i in range(16)])]
    ppermute x29 -> x28, starting transfers between devices: 33.5 us -> 29.4 us  [swap_cols(): return lax.ppermute(values, 'col', [(0, 1), (1, 0)])]
    ppermute x29 -> x28, waiting for transfers between devices: 148 us -> 152 us  [swap_cols(): return lax.ppermute(values, 'col', [(0, 1), (1, 0)])]
    ppermute x73 -> x66, starting transfers between devices: 41.4 us -> 45.2 us  [swap_rows(): return lax.ppermute(values, 'row', [(i, i ^ bit) for i in range(16)])]
  transfers between devices with their start and end apart: 129 -> 118, of which waited for: 43 -> 37; matrix products, arithmetic and copies ran while one was open for 18% -> 19% of each run, Pallas kernels for 40% -> 36%
where the time goes in v3:
time: 1170 us; the launch traced here: 1160 us
  Pallas kernels  437 us (37%)
  waiting for transfers between devices  283 us (24%)
  other arithmetic  168 us (14%)
  local copies, waits for them, and re-layouts  145 us (12%)
  starting transfers between devices  110 us (9%)
  matrix products  16.2 us (1%)
    ppermute x28, waiting for transfers between devices, swap_cols(): return lax.ppermute(values, 'col', [(0, 1), (1, 0)])  152 us
    pallas_call x4, Pallas kernels, run_experts(): pl.pallas_call(body, grid=(count,), in_specs=[wide, wide, narrow, matrix,...  111 us
    pallas_call x4, Pallas kernels, pick_rows(): pl.pallas_call(body, grid=(FAMILIES,), in_specs=[pl.BlockSpec(memory_spac...  82.4 us
    unnamed x475, local copies, waits for them, and re-layouts  77.8 us
    pallas_call x16, Pallas kernels, sum_tokens(): pl.pallas_call(body, grid=(2,), in_specs=in_specs, out_specs=out_specs, o...  70.1 us
    ppermute x66, waiting for transfers between devices, swap_rows(): return lax.ppermute(values, 'row', [(i, i ^ bit) for i in range(16)])  66.5 us
    ppermute x21, waiting for transfers between devices, turn_planes(): return lax.ppermute(values, 'row', [(i, (i + 4) % 16) for i in range(16)])  64.3 us
    pallas_call x2, Pallas kernels, expert_weight_grads(): pl.pallas_call(body, grid=(count, width // tile), in_specs=[wide] * (2 *...  53.9 us
  transfers between devices with their start and end apart: 118, of which 37 were waited for; matrix products, arithmetic and copies ran while one was open for 19% of the time, Pallas kernels for 36%

profile of v3, /device:TPU:0, one launch (start us, length us, event | category | flops | bytes accessed | tf_op | source)
XLA Modules:
  0.0 1163.2 jit_solution(16855326909964668331)
XLA Ops:
  13.5 13.7 %collective-permute-done.3 = f32[2,1024]{1,0:T(2,128)S(1)} collective-permute-done((f32[2,1024]{1,0:T(2,128)S(1)}, f32[2,1024]{1,0:T(2,128)S(1)}, u32[]{:S(2)}, u32[]{:S(2)}) %collective-permute-start.3) | collective-permute-done | bytes 8224 | tf_op jit(solution)/shard_map/ppermute | solution.py:94
  27.2 7.6 collective-permute-done.refs_4_
  38.4 23.1 %collective-permute-done.4.refs_8_ = bf16[128,3840]{1,0:T(8,128)(2,1)} collective-permute-done((bf16[128,3840]{1,0:T(8,128)(2,1)S(1)}, bf16[128,3840]{1,0:T(8,128)(2,1)}, u32[]{:S(2)}, u32[]{:S(2)}) %collective-permute-start.4) | collective-permute-done | bytes 983072 | tf_op jit(solution)/shard_map/ppermute | solution.py:102
  73.5 12.1 %collective-permute-done.13.refs_1_.refs_9_ = bf16[160,2048]{1,0:T(8,128)(2,1)S(1)} collective-permute-done((bf16[160,2048]{1,0:T(8,128)(2,1)}, bf16[160,2048]{1,0:T(8,128)(2,1)S(1)}, u32[]{:S(2)}, u32[]{:S(2)}) %collective-permute-start.13) | collective-permute-done | bytes 655392 | tf_op jit(solution)/shard_map/ppermute | solution.py:94
  109.0 23.7 %collective-permute-done.14.refs_14_ = bf16[128,3840]{1,0:T(8,128)(2,1)} collective-permute-done((bf16[128,3840]{1,0:T(8,128)(2,1)}, bf16[128,3840]{1,0:T(8,128)(2,1)}, u32[]{:S(2)}, u32[]{:S(2)}) %collective-permute-start.14) | collective-permute-done | bytes 983072 | tf_op jit(solution)/shard_map/ppermute | solution.py:98
  145.9 11.1 shard_map.298
  189.0 18.4 %shard_map.299 = (bf16[512,1536]{1,0:T(8,128)(2,1)S(1)}, bf16[512,2048]{1,0:T(8,128)(2,1)S(1)}, bf16[512,1024]{1,0:T(8,128)(2,1)S(1)}, bf16[512,2048]{1,0:T(8,128)(2,1)S(1)}) custom-call(bf16[512,2048]{1,0:T(8,128)(2,1)} %copy-done.5, bf16[512,512]{1,0:T(8,128)(2,1)S(1)} %fusion.20.latent_ref, bf16[512,128]{1,0:T(8,128)(2,1)S(1)} %get-tuple-element.871.rope0_ref, ...), custom_call_target="tpu_custom_call" | custom-call | flops 1000000000 | bytes 1000000 | tf_op jit(solution)/shard_map/pallas_call | solution.py:998
  210.0 7.6 collective-permute-done.24.refs_5_.refs_1_.refs_9_.refs_13_
  229.5 27.3 %collective-permute-done.26 = bf16[352,2048]{1,0:T(8,128)(2,1)S(1)} collective-permute-done((bf16[352,2048]{1,0:T(8,128)(2,1)S(1)}, bf16[352,2048]{1,0:T(8,128)(2,1)S(1)}, u32[]{:S(2)}, u32[]{:S(2)}) %collective-permute-start.26) | collective-permute-done | bytes 1441824 | tf_op jit(solution)/shard_map/ppermute | solution.py:94
  265.7 27.8 %collective-permute-done.31.refs_5_.refs_13_.refs_1_ = bf16[320,2048]{1,0:T(8,128)(2,1)S(1)} collective-permute-done((bf16[320,2048]{1,0:T(8,128)(2,1)S(1)}, bf16[320,2048]{1,0:T(8,128)(2,1)S(1)}, u32[]{:S(2)}, u32[]{:S(2)}) %collective-permute-start.31) | collective-permute-done | bytes 1310752 | tf_op jit(solution)/shard_map/ppermute | solution.py:94
  321.3 7.4 shard_map.301
  328.7 7.9 collective-permute-done.34.refs_1_.refs_5_
  347.7 30.4 %collective-permute-done.39.refs_5_.refs_1_ = bf16[320,2048]{1,0:T(8,128)(2,1)S(1)} collective-permute-done((bf16[320,2048]{1,0:T(8,128)(2,1)S(1)}, bf16[320,2048]{1,0:T(8,128)(2,1)S(1)}, u32[]{:S(2)}, u32[]{:S(2)}) %collective-permute-start.39) | collective-permute-done | bytes 1310752 | tf_op jit(solution)/shard_map/ppermute | solution.py:94
  398.4 20.4 %shard_map.302 = (bf16[4,256,2048]{2,1,0:T(8,128)(2,1)}, f32[4,256,128]{2,1,0:T(8,128)S(1)}, bf16[4,512,128]{2,1,0:T(8,128)(2,1)S(1)}, bf16[4,512,256]{2,1,0:T(8,128)(2,1)S(1)}, f32[384,2048]{1,0:T(8,128)}) custom-call(bf16[352,2048]{1,0:T(8,128)(2,1)} %collective-permute-done.29.refs_0_, bf16[320,2048]{1,0:T(8,128)(2,1)} %collective-permute-done.34.refs_1_.refs_5_, ...), custom_call_target="tpu_custom_call" | custom-call | flops 1000000000 | bytes 1000000 | tf_op jit(solution)/shard_map/pallas_call | solution.py:400
  432.7 27.5 %shard_map.303 = (bf16[4,256,2048]{2,1,0:T(8,128)(2,1)}, bf16[4,256,2048]{2,1,0:T(8,128)(2,1)}, bf16[4,256,704]{2,1,0:T(8,128)(2,1)}, bf16[4,256,704]{2,1,0:T(8,...) custom-call(bf16[4,256,2048]{2,1,0:T(8,128)(2,1)} %get-tuple-element.429.rows_ref.refs_1_, ...), custom_call_target="tpu_custom_call" | custom-call | flops 1000000000 | bytes 1000000 | tf_op jit(solution)/shard_map/pallas_call | solution.py:479
  490.3 7.3 shard_map.305
  501.9 20.3 %shard_map.306 = (bf16[4,256,2048]{2,1,0:T(8,128)(2,1)}, f32[4,256,128]{2,1,0:T(8,128)S(1)}, bf16[4,512,128]{2,1,0:T(8,128)(2,1)S(1)}, bf16[4,512,256]{2,1,0:T(8,128)(2,1)S(1)}, f32[384,2048]{1,0:T(8,128)}) custom-call(bf16[352,2048]{1,0:T(8,128)(2,1)} %collective-permute-done.32.refs_0_, bf16[320,2048]{1,0:T(8,128)(2,1)S(1)} %copy-done.53, ...), custom_call_target="tpu_custom_call" | custom-call | flops 1000000000 | bytes 1000000 | tf_op jit(solution)/shard_map/pallas_call | solution.py:400
  536.4 27.5 %shard_map.307 = (bf16[4,256,2048]{2,1,0:T(8,128)(2,1)}, bf16[4,256,2048]{2,1,0:T(8,128)(2,1)}, bf16[4,256,704]{2,1,0:T(8,128)(2,1)}, bf16[4,256,704]{2,1,0:T(8,...) custom-call(bf16[4,256,2048]{2,1,0:T(8,128)(2,1)} %get-tuple-element.459.rows_ref.refs_2_, ...), custom_call_target="tpu_custom_call" | custom-call | flops 1000000000 | bytes 1000000 | tf_op jit(solution)/shard_map/pallas_call | solution.py:479
  595.0 21.0 %shard_map.312 = (bf16[4,256,2048]{2,1,0:T(8,128)(2,1)}, f32[4,256,128]{2,1,0:T(8,128)S(1)}, bf16[4,512,128]{2,1,0:T(8,128)(2,1)S(1)}, bf16[4,512,256]{2,1,0:T(8,128)(2,1)S(1)}, f32[384,2048]{1,0:T(8,128)}) custom-call(bf16[352,2048]{1,0:T(8,128)(2,1)} %collective-permute-done.37.refs_0_, bf16[320,2048]{1,0:T(8,128)(2,1)} %collective-permute-done.44.refs_5_.refs_1_, ...), custom_call_target="tpu_custom_call" | custom-call | flops 1000000000 | bytes 1000000 | tf_op jit(solution)/shard_map/pallas_call | solution.py:400
  640.0 27.7 %shard_map.316 = (bf16[4,256,2048]{2,1,0:T(8,128)(2,1)}, bf16[4,256,2048]{2,1,0:T(8,128)(2,1)}, bf16[4,256,704]{2,1,0:T(8,128)(2,1)}, bf16[4,256,704]{2,1,0:T(8,...) custom-call(bf16[4,256,2048]{2,1,0:T(8,128)(2,1)} %get-tuple-element.509.rows_ref.refs_3_, ...), custom_call_target="tpu_custom_call" | custom-call | flops 1000000000 | bytes 1000000 | tf_op jit(solution)/shard_map/pallas_call | solution.py:479
  711.9 20.7 %shard_map.319 = (bf16[4,256,2048]{2,1,0:T(8,128)(2,1)}, f32[4,256,128]{2,1,0:T(8,128)S(1)}, bf16[4,512,128]{2,1,0:T(8,128)(2,1)S(1)}, bf16[4,512,256]{2,1,0:T(8,128)(2,1)S(1)}, f32[384,2048]{1,0:T(8,128)}) custom-call(bf16[352,2048]{1,0:T(8,128)(2,1)} %copy-done.170, bf16[320,2048]{1,0:T(8,128)(2,1)} %copy-done.21, ...), custom_call_target="tpu_custom_call" | custom-call | flops 1000000000 | bytes 1000000 | tf_op jit(solution)/shard_map/pallas_call | solution.py:400
  752.0 27.9 %shard_map.320 = (bf16[4,256,2048]{2,1,0:T(8,128)(2,1)}, bf16[4,256,2048]{2,1,0:T(8,128)(2,1)}, bf16[4,256,704]{2,1,0:T(8,128)(2,1)}, bf16[4,256,704]{2,1,0:T(8,...) custom-call(bf16[4,256,2048]{2,1,0:T(8,128)(2,1)} %get-tuple-element.544.rows_ref.refs_0_, ...), custom_call_target="tpu_custom_call" | custom-call | flops 1000000000 | bytes 1000000 | tf_op jit(solution)/shard_map/pallas_call | solution.py:479
  810.1 26.8 %shard_map.324 = (f32[4,704,2048]{2,1,0:T(8,128)}, f32[4,704,2048]{2,1,0:T(8,128)}, f32[4,704,2048]{2,1,0:T(8,128)}) custom-call(bf16[4,256,2048]{2,1,0:T(8,128)(2,1)} %get-tuple-element.544.rows_ref.refs_0_, bf16[4,256,2048]{2,1,0:T(8,128)(2,1)} %get-tuple-element.429.rows_ref.refs_1_, bf16[4,256,2048]{2,1,0:T(8,128)(2,1)} %get-tuple-element.459.rows_ref.refs_2_, ...), custom_call_target="tpu_custom_call" | custom-call | flops 1000000000 | bytes 1000000 | tf_op jit(solution)/shard_map/pallas_call | solution.py:894
  870.0 27.1 %shard_map.328 = (f32[4,704,2048]{2,1,0:T(8,128)}, f32[4,704,2048]{2,1,0:T(8,128)}, f32[4,704,2048]{2,1,0:T(8,128)}) custom-call(bf16[4,256,2048]{2,1,0:T(8,128)(2,1)} %get-tuple-element.544.rows_ref.refs_0_, bf16[4,256,2048]{2,1,0:T(8,128)(2,1)} %get-tuple-element.429.rows_ref.refs_1_, ...), custom_call_target="tpu_custom_call", output_to_operand_aliasing={{0}: (20, {}), {1}: (21, {}), {2}: (22, {})} | custom-call | flops 1000000000 | bytes 1000000 | tf_op jit(solution)/shard_map/pallas_call | solution.py:894
  927.1 9.5 collective-permute-done.86
  953.7 28.7 %shard_map.330 = (bf16[512,1536]{1,0:T(8,128)(2,1)}, bf16[512,2048]{1,0:T(8,128)(2,1)}, f32[512,128]{1,0:T(8,128)S(1)}, f32[512,512]{1,0:T(8,128)}, bf16[512,2048]{1,0:T(8,128)(2,1)}) custom-call(bf16[512,2048]{1,0:T(8,128)(2,1)} %copy-done.18, bf16[512,1536]{1,0:T(8,128)(2,1)} %copy-done.128, bf16[512,2048]{1,0:T(8,128)(2,1)} %copy-done.111, ...), custom_call_target="tpu_custom_call" | custom-call | flops 1000000000 | bytes 1000000 | tf_op jit(solution)/shard_map/pallas_call | solution.py:1112
  993.0 7.2 shard_map.332
  1038.5 7.6 collective-permute-done.95
  1058.2 10.7 shard_map.335
  1090.7 8.1 collective-permute-done.98
  1128.2 11.6 collective-permute-done.109
  1148.5 9.0 collective-permute-done.112
  (930 shorter events, 594.8 us)
Async XLA Ops:
  90.9 42.8 %collective-permute-start.17 = (bf16[512,2048]{1,0:T(8,128)(2,1)}, bf16[512,2048]{1,0:T(8,128)(2,1)}, u32[]{:S(2)}, u32[]{:S(2)}) collective-permute-start(bf16[512,2048]{1,0:T(8,128)(2,1)} %pad_maximum_fusion.8), channel_id=1, source_target_pairs={{0,2},{2,0},{4,6},{6,4},{8,10},{10,8},{12,14},{14,12},{16,18},{18,... | collective-permute-start | bytes 6291464 | tf_op jit(solution)/shard_map/ppermute | solution.py:98
  92.0 41.7 %all-to-all-start = ((bf16[16,3,88,128]{3,2,1,0:T(8,128)(2,1)}), bf16[16,3,88,128]{3,2,1,0:T(8,128)(2,1)}, u32[]{:S(2)}, u32[]{:S(2)}) async-start(bf16[16,3,88,128]{3,2,1,0:T(8,128)(2,1)} %copy.173), calls=%async_computation | async-start | bytes 2162688 | tf_op jit(solution)/shard_map/all_to_all | solution.py:1281
  138.4 42.2 %collective-permute-start.20 = (bf16[352,2048]{1,0:T(8,128)(2,1)}, bf16[352,2048]{1,0:T(8,128)(2,1)S(1)}, u32[]{:S(2)}, u32[]{:S(2)}) collective-permute-start(bf16[352,2048]{1,0:T(8,128)(2,1)} %pad_maximum_fusion.12.refs_0_.refs_8_), channel_id=1, source_target_pairs={{0,4},{2,6},{4,0},{6,2},{8,12},{10,14},{12,8},{14,10},{16,20},{18,... | collective-permute-start | bytes 4325384 | tf_op jit(solution)/shard_map/ppermute | solution.py:98
  140.4 40.2 %collective-permute-start.21 = (bf16[352,2048]{1,0:T(8,128)(2,1)}, bf16[352,2048]{1,0:T(8,128)(2,1)}, u32[]{:S(2)}, u32[]{:S(2)}) collective-permute-start(bf16[352,2048]{1,0:T(8,128)(2,1)} %pad_maximum_fusion.12.refs_0_.refs_8_), channel_id=1, source_target_pairs={{0,8},{2,10},{4,12},{6,14},{8,16},{10,18},{12,20},{14,22},{16,24},... | collective-permute-start | bytes 4325384 | tf_op jit(solution)/shard_map/ppermute | solution.py:102
  343.3 38.5 %collective-permute-start.40 = (bf16[864,2048]{1,0:T(8,128)(2,1)S(1)}, bf16[864,2048]{1,0:T(8,128)(2,1)S(1)}, u32[]{:S(2)}, u32[]{:S(2)}) collective-permute-start(bf16[864,2048]{1,0:T(8,128)(2,1)S(1)} %pad_maximum_fusion.1), channel_id=1, source_target_pairs={{0,2},{2,0},{4,6},{6,4},{8,10},{10,8},{12,14},{14,12},{16,18},{18,... | collective-permute-start | bytes 10616840 | tf_op jit(solution)/shard_map/ppermute | solution.py:98
  395.5 73.8 %collective-permute-start.50 = (bf16[704,2048]{1,0:T(8,128)(2,1)}, bf16[704,2048]{1,0:T(8,128)(2,1)S(1)}, u32[]{:S(2)}, u32[]{:S(2)}) collective-permute-start(bf16[704,2048]{1,0:T(8,128)(2,1)} %pad_maximum_fusion.6), channel_id=1, source_target_pairs={{0,2},{2,0},{4,6},{6,4},{8,10},{10,8},{12,14},{14,12},{16,18},{18,... | collective-permute-start | bytes 8650760 | tf_op jit(solution)/shard_map/ppermute | solution.py:98
  426.9 49.2 %collective-permute-start.49 = (bf16[704,2048]{1,0:T(8,128)(2,1)}, bf16[704,2048]{1,0:T(8,128)(2,1)}, u32[]{:S(2)}, u32[]{:S(2)}) collective-permute-start(bf16[704,2048]{1,0:T(8,128)(2,1)} %pad_maximum_fusion.5), channel_id=1, source_target_pairs={{0,2},{2,0},{4,6},{6,4},{8,10},{10,8},{12,14},{14,12},{16,18},{18,... | collective-permute-start | bytes 8650760 | tf_op jit(solution)/shard_map/ppermute | solution.py:98
  430.7 45.4 %collective-permute-start.47 = (bf16[480,2048]{1,0:T(8,128)(2,1)}, bf16[480,2048]{1,0:T(8,128)(2,1)S(1)}, u32[]{:S(2)}, u32[]{:S(2)}) collective-permute-start(bf16[480,2048]{1,0:T(8,128)(2,1)} %pad_maximum_fusion.9), channel_id=1, source_target_pairs={{0,1},{1,0},{2,3},{3,2},{4,5},{5,4},{6,7},{7,6},{8,9},{9,8},{10,11... | collective-permute-start | bytes 5898248 | tf_op jit(solution)/shard_map/ppermute | solution.py:94
  431.3 39.6 %collective-permute-start.46 = (bf16[352,2048]{1,0:T(8,128)(2,1)S(1)}, bf16[352,2048]{1,0:T(8,128)(2,1)}, u32[]{:S(2)}, u32[]{:S(2)}) collective-permute-start(bf16[352,2048]{1,0:T(8,128)(2,1)S(1)} %copy-done.32), channel_id=1, source_target_pairs={{0,4},{2,6},{4,0},{6,2},{8,12},{10,14},{12,8},{14,10},{16,20},{18,... | collective-permute-start | bytes 4325384 | tf_op jit(solution)/shard_map/ppermute | solution.py:98
  432.5 38.3 %collective-permute-start.48 = (bf16[320,2048]{1,0:T(8,128)(2,1)}, bf16[320,2048]{1,0:T(8,128)(2,1)}, u32[]{:S(2)}, u32[]{:S(2)}) collective-permute-start(bf16[320,2048]{1,0:T(8,128)(2,1)} %collective-permute-done.44.refs_5_.refs_1_), channel_id=1, source_target_pairs={{0,2},{2,0},{4,6},{6,4},{8,10},{10,8},{12,14},{14,12},{16,18},{18,... | collective-permute-start | bytes 3932168 | tf_op jit(solution)/shard_map/ppermute | solution.py:98
  476.1 47.9 %collective-permute-start.52 = (bf16[2,512,2048]{2,1,0:T(8,128)(2,1)}, bf16[2,512,2048]{2,1,0:T(8,128)(2,1)}, u32[]{:S(2)}, u32[]{:S(2)}) collective-permute-start(bf16[2,512,2048]{2,1,0:T(8,128)(2,1)} %get-tuple-element.457), channel_id=1, source_target_pairs={{0,2},{2,0},{4,6},{6,4},{8,10},{10,8},{12,14},{14,12},{16,18},{18,... | collective-permute-start | bytes 12582920 | tf_op jit(solution)/shard_map/ppermute | solution.py:98
  479.8 44.2 %collective-permute-start.54 = (bf16[864,2048]{1,0:T(8,128)(2,1)}, bf16[864,2048]{1,0:T(8,128)(2,1)S(1)}, u32[]{:S(2)}, u32[]{:S(2)}) collective-permute-start(bf16[864,2048]{1,0:T(8,128)(2,1)} %pad_maximum_fusion.3), channel_id=1, source_target_pairs={{0,2},{2,0},{4,6},{6,4},{8,10},{10,8},{12,14},{14,12},{16,18},{18,... | collective-permute-start | bytes 10616840 | tf_op jit(solution)/shard_map/ppermute | solution.py:98
  484.0 40.0 %collective-permute-start.53 = (bf16[320,2048]{1,0:T(8,128)(2,1)}, bf16[320,2048]{1,0:T(8,128)(2,1)S(1)}, u32[]{:S(2)}, u32[]{:S(2)}) collective-permute-start(bf16[320,2048]{1,0:T(8,128)(2,1)} %pad_maximum_fusion.25), channel_id=1, source_target_pairs={{0,1},{1,0},{2,3},{3,2},{4,5},{5,4},{6,7},{7,6},{8,9},{9,8},{10,11... | collective-permute-start | bytes 3932168 | tf_op jit(solution)/shard_map/ppermute | solution.py:94
  571.7 44.4 %collective-permute-start.58 = (bf16[2,512,2048]{2,1,0:T(8,128)(2,1)}, bf16[2,512,2048]{2,1,0:T(8,128)(2,1)}, u32[]{:S(2)}, u32[]{:S(2)}) collective-permute-start(bf16[2,512,2048]{2,1,0:T(8,128)(2,1)} %get-tuple-element.493), channel_id=1, source_target_pairs={{0,2},{2,0},{4,6},{6,4},{8,10},{10,8},{12,14},{14,12},{16,18},{18,... | collective-permute-start | bytes 12582920 | tf_op jit(solution)/shard_map/ppermute | solution.py:98
  576.5 39.5 %collective-permute-start.59 = (bf16[352,2048]{1,0:T(8,128)(2,1)}, bf16[352,2048]{1,0:T(8,128)(2,1)}, u32[]{:S(2)}, u32[]{:S(2)}) collective-permute-start(bf16[352,2048]{1,0:T(8,128)(2,1)} %pad_maximum_fusion.13), channel_id=1, source_target_pairs={{0,4},{2,6},{4,0},{6,2},{8,12},{10,14},{12,8},{14,10},{16,20},{18,... | collective-permute-start | bytes 4325384 | tf_op jit(solution)/shard_map/ppermute | solution.py:98
  632.5 43.5 %collective-permute-start.64 = (bf16[2,512,2048]{2,1,0:T(8,128)(2,1)}, bf16[2,512,2048]{2,1,0:T(8,128)(2,1)}, u32[]{:S(2)}, u32[]{:S(2)}) collective-permute-start(bf16[2,512,2048]{2,1,0:T(8,128)(2,1)} %shard_map.315), channel_id=1, source_target_pairs={{0,2},{2,0},{4,6},{6,4},{8,10},{10,8},{12,14},{14,12},{16,18},{18,... | collective-permute-start | bytes 12582920 | tf_op jit(solution)/shard_map/ppermute | solution.py:98
  637.1 38.9 %collective-permute-start.65 = (bf16[352,2048]{1,0:T(8,128)(2,1)}, bf16[352,2048]{1,0:T(8,128)(2,1)}, u32[]{:S(2)}, u32[]{:S(2)}) collective-permute-start(bf16[352,2048]{1,0:T(8,128)(2,1)} %pad_maximum_fusion.14), channel_id=1, source_target_pairs={{0,4},{2,6},{4,0},{6,2},{8,12},{10,14},{12,8},{14,10},{16,20},{18,... | collective-permute-start | bytes 4325384 | tf_op jit(solution)/shard_map/ppermute | solution.py:98
  639.7 72.1 %collective-permute-start.66 = (bf16[160,2048]{1,0:T(8,128)(2,1)}, bf16[160,2048]{1,0:T(8,128)(2,1)}, u32[]{:S(2)}, u32[]{:S(2)}) collective-permute-start(bf16[160,2048]{1,0:T(8,128)(2,1)} %get-tuple-element.858), channel_id=1, source_target_pairs={{0,2},{2,0},{4,6},{6,4},{8,10},{10,8},{12,14},{14,12},{16,18},{18,... | collective-permute-start | bytes 1966088 | tf_op jit(solution)/shard_map/ppermute | solution.py:98
  681.2 52.6 %collective-permute-start.67 = (bf16[2,512,2048]{2,1,0:T(8,128)(2,1)}, bf16[2,512,2048]{2,1,0:T(8,128)(2,1)}, u32[]{:S(2)}, u32[]{:S(2)}) collective-permute-start(bf16[2,512,2048]{2,1,0:T(8,128)(2,1)} %get-tuple-element.540), channel_id=1, source_target_pairs={{0,2},{2,0},{4,6},{6,4},{8,10},{10,8},{12,14},{14,12},{16,18},{18,... | collective-permute-start | bytes 12582920 | tf_op jit(solution)/shard_map/ppermute | solution.py:98
  685.4 48.4 %collective-permute-start.69 = (bf16[2,160,2048]{2,1,0:T(8,128)(2,1)}, bf16[2,160,2048]{2,1,0:T(8,128)(2,1)}, u32[]{:S(2)}, u32[]{:S(2)}) collective-permute-start(bf16[2,160,2048]{2,1,0:T(8,128)(2,1)} %get-tuple-element.530), channel_id=1, source_target_pairs={{0,1},{1,0},{2,3},{3,2},{4,5},{5,4},{6,7},{7,6},{8,9},{9,8},{10,11... | collective-permute-start | bytes 3932168 | tf_op jit(solution)/shard_map/ppermute | solution.py:94
  690.1 43.6 %collective-permute-start.68 = (bf16[352,2048]{1,0:T(8,128)(2,1)}, bf16[352,2048]{1,0:T(8,128)(2,1)}, u32[]{:S(2)}, u32[]{:S(2)}) collective-permute-start(bf16[352,2048]{1,0:T(8,128)(2,1)} %pad_maximum_fusion.15), channel_id=1, source_target_pairs={{0,4},{2,6},{4,0},{6,2},{8,12},{10,14},{12,8},{14,10},{16,20},{18,... | collective-permute-start | bytes 4325384 | tf_op jit(solution)/shard_map/ppermute | solution.py:98
  691.3 42.4 %collective-permute-start.70 = (bf16[352,2048]{1,0:T(8,128)(2,1)}, bf16[352,2048]{1,0:T(8,128)(2,1)}, u32[]{:S(2)}, u32[]{:S(2)}) collective-permute-start(bf16[352,2048]{1,0:T(8,128)(2,1)} %maximum_add_fusion.4), channel_id=1, source_target_pairs={{0,8},{2,10},{4,12},{6,14},{8,16},{10,18},{12,20},{14,22},{16,24},... | collective-permute-start | bytes 4325384 | tf_op jit(solution)/shard_map/ppermute | solution.py:102
  744.0 43.3 %collective-permute-start.73 = (bf16[2,512,2048]{2,1,0:T(8,128)(2,1)S(1)}, bf16[2,512,2048]{2,1,0:T(8,128)(2,1)}, u32[]{:S(2)}, u32[]{:S(2)}) collective-permute-start(bf16[2,512,2048]{2,1,0:T(8,128)(2,1)S(1)} %copy-done.69), channel_id=1, source_target_pairs={{0,2},{2,0},{4,6},{6,4},{8,10},{10,8},{12,14},{14,12},{16,18},{18,... | collective-permute-start | bytes 12582920 | tf_op jit(solution)/shard_map/ppermute | solution.py:98
  748.5 38.8 %collective-permute-start.74 = (bf16[352,2048]{1,0:T(8,128)(2,1)}, bf16[352,2048]{1,0:T(8,128)(2,1)}, u32[]{:S(2)}, u32[]{:S(2)}) collective-permute-start(bf16[352,2048]{1,0:T(8,128)(2,1)} %pad_maximum_fusion.16), channel_id=1, source_target_pairs={{0,4},{2,6},{4,0},{6,2},{8,12},{10,14},{12,8},{14,10},{16,20},{18,... | collective-permute-start | bytes 4325384 | tf_op jit(solution)/shard_map/ppermute | solution.py:98
  787.3 49.9 %collective-permute-start.75 = (bf16[2,512,2048]{2,1,0:T(8,128)(2,1)}, bf16[2,512,2048]{2,1,0:T(8,128)(2,1)}, u32[]{:S(2)}, u32[]{:S(2)}) collective-permute-start(bf16[2,512,2048]{2,1,0:T(8,128)(2,1)} %get-tuple-element.586), channel_id=1, source_target_pairs={{0,2},{2,0},{4,6},{6,4},{8,10},{10,8},{12,14},{14,12},{16,18},{18,... | collective-permute-start | bytes 12582920 | tf_op jit(solution)/shard_map/ppermute | solution.py:98
  798.0 38.9 %collective-permute-start.78 = (bf16[352,2048]{1,0:T(8,128)(2,1)}, bf16[352,2048]{1,0:T(8,128)(2,1)}, u32[]{:S(2)}, u32[]{:S(2)}) collective-permute-start(bf16[352,2048]{1,0:T(8,128)(2,1)} %fusion.9), channel_id=1, source_target_pairs={{0,8},{2,10},{4,12},{6,14},{8,16},{10,18},{12,20},{14,22},{16,24},... | collective-permute-start | bytes 4325384 | tf_op jit(solution)/shard_map/ppermute | solution.py:102
  847.0 50.4 %collective-permute-start.81 = (bf16[2,512,2048]{2,1,0:T(8,128)(2,1)}, bf16[2,512,2048]{2,1,0:T(8,128)(2,1)}, u32[]{:S(2)}, u32[]{:S(2)}) collective-permute-start(bf16[2,512,2048]{2,1,0:T(8,128)(2,1)} %shard_map.327), channel_id=1, source_target_pairs={{0,2},{2,0},{4,6},{6,4},{8,10},{10,8},{12,14},{14,12},{16,18},{18,... | collective-permute-start | bytes 12582920 | tf_op jit(solution)/shard_map/ppermute | solution.py:98
  853.7 43.6 %collective-permute-start.79 = (bf16[352,2048]{1,0:T(8,128)(2,1)}, bf16[352,2048]{1,0:T(8,128)(2,1)}, u32[]{:S(2)}, u32[]{:S(2)}) collective-permute-start(bf16[352,2048]{1,0:T(8,128)(2,1)} %fusion.10), channel_id=1, source_target_pairs={{0,8},{2,10},{4,12},{6,14},{8,16},{10,18},{12,20},{14,22},{16,24},... | collective-permute-start | bytes 4325384 | tf_op jit(solution)/shard_map/ppermute | solution.py:102
  857.7 39.6 %collective-permute-start.82 = (bf16[192,2048]{1,0:T(8,128)(2,1)}, bf16[192,2048]{1,0:T(8,128)(2,1)}, u32[]{:S(2)}, u32[]{:S(2)}) collective-permute-start(bf16[192,2048]{1,0:T(8,128)(2,1)} %slice_bitcast_fusion.5), channel_id=1, source_target_pairs={{0,4},{2,6},{4,0},{6,2},{8,12},{10,14},{12,8},{14,10},{16,20},{18,... | collective-permute-start | bytes 2359304 | tf_op jit(solution)/shard_map/ppermute | solution.py:98
  920.4 69.5 %collective-permute-start.88 = (bf16[2,160,2048]{2,1,0:T(8,128)(2,1)}, bf16[2,160,2048]{2,1,0:T(8,128)(2,1)}, u32[]{:S(2)}, u32[]{:S(2)}) collective-permute-start(bf16[2,160,2048]{2,1,0:T(8,128)(2,1)} %get-tuple-element.643), channel_id=1, source_target_pairs={{0,1},{1,0},{2,3},{3,2},{4,5},{5,4},{6,7},{7,6},{8,9},{9,8},{10,11... | collective-permute-start | bytes 3932168 | tf_op jit(solution)/shard_map/ppermute | solution.py:94
  922.3 67.7 %all-to-all-start.2 = ((bf16[16,3,88,128]{3,2,1,0:T(8,128)(2,1)}), bf16[16,3,88,128]{3,2,1,0:T(8,128)(2,1)}, u32[]{:S(2)}, u32[]{:S(2)}) async-start(bf16[16,3,88,128]{3,2,1,0:T(8,128)(2,1)} %copy.188), calls=%async_computation.2 | async-start | bytes 2162688 | tf_op jit(solution)/shard_map/all_to_all | solution.py:1697
  1089.2 38.9 %collective-permute-start.106 = (bf16[128,2688]{1,0:T(8,128)(2,1)}, bf16[128,2688]{1,0:T(8,128)(2,1)S(1)}, u32[]{:S(2)}, u32[]{:S(2)}) collective-permute-start(bf16[128,2688]{1,0:T(8,128)(2,1)} %get-tuple-element.812), channel_id=1, source_target_pairs={{0,4},{2,6},{4,0},{6,2},{8,12},{10,14},{12,8},{14,10},{16,20},{18,... | collective-permute-start | bytes 2064392 | tf_op jit(solution)/shard_map/ppermute | solution.py:98
  (321 other events, 4312.6 us)

commit v4 on v3

--- a/solution.py
+++ b/solution.py
@@ -1302,23 +1302,8 @@
     latent_normed = (latent_unit * latent_gain).astype(bf16)
     key_rope = rotate(latent[:, RANK:].astype(f32), cosine, sine).astype(bf16)
     ropes = head_ropes(key_rope)
-    routes_all = flat_dense[
-        :, QUERY_COLUMNS + 1536 + latent_width + expert_count :
-    ][:, : rows_count * TOPK // block]
-    routes_all = routes_all.reshape(row_devices, rows_count, TOPK).transpose(0, 2, 1)[arrival]
-    routes_all = routes_all.astype(jnp.int32)
-
-    routes_all = local_tokens(routes_all, 2, first)
-    held_experts = row_place * EXP_DEV + jnp.arange(EXP_DEV, dtype=jnp.int32)
-    hits = jnp.any(routes_all[:, :, None, :] == held_experts[None, None, :, None], axis=1)
-    upper = (places[:, None] <= places[None, :]).astype(bf16)
-    ranks = jnp.einsum("sjt,tu->sju", hits.astype(bf16), upper, preferred_element_type=f32)
-    codes = jnp.where(hits, ranks.astype(jnp.int32) - 1, -1)
-    codes = jnp.pad(codes, ((0, 0), (0, 8 - EXP_DEV), (0, 0)), constant_values=-1)
-    plane_codes = [codes[p * FAMILIES : (p + 1) * FAMILIES] for p in range(PLANES)]
-
-    latent_normed, plane_codes, grad_rows.held[0, 1], grad_rows.held[1, 0] = together(
-        latent_normed, plane_codes, grad_rows.cross(0), grad_turned
+    latent_normed, grad_rows.held[0, 1], grad_rows.held[1, 0] = together(
+        latent_normed, grad_rows.cross(0), grad_turned
     )
 
     query, keys, mixed, attended_part = attend(
@@ -1379,14 +1364,29 @@
     normed_sent = (middle_sent * scale_sent * gain_two).astype(bf16)
     rows = Spread(normed_sent)
 
+    routes_all = after(flat_dense, normed_sent)[
+        :, QUERY_COLUMNS + 1536 + latent_width + expert_count :
+    ][:, : rows_count * TOPK // block]
+    routes_all = routes_all.reshape(row_devices, rows_count, TOPK).transpose(0, 2, 1)[arrival]
+    routes_all = routes_all.astype(jnp.int32)
+
+    routes_all = local_tokens(routes_all, 2, first)
+    held_experts = row_place * EXP_DEV + jnp.arange(EXP_DEV, dtype=jnp.int32)
+    hits = jnp.any(routes_all[:, :, None, :] == held_experts[None, None, :, None], axis=1)
+    upper = (places[:, None] <= places[None, :]).astype(bf16)
+    ranks = jnp.einsum("sjt,tu->sju", hits.astype(bf16), upper, preferred_element_type=f32)
+    codes = jnp.where(hits, ranks.astype(jnp.int32) - 1, -1)
+    codes = jnp.pad(codes, ((0, 0), (0, 8 - EXP_DEV), (0, 0)), constant_values=-1)
+    plane_codes = [codes[p * FAMILIES : (p + 1) * FAMILIES] for p in range(PLANES)]
+
     shared_here = shared_here.transpose(1, 2, 0, 3).reshape(3, shared_share, D)
     shared_here = jnp.pad(shared_here, ((0, 0), (0, SHARED_PAD - shared_share), (0, 0)))
     shared_pair = shared_here[:2].reshape(2 * SHARED_PAD, D)
     shared_last = shared_here[2]
 
     sent, starts = batch(rows.sent((0, 0)) + grad_rows.sent((1, 1)))
-    rows.held[1, 0], rows.held[0, 1], got, shared_pair, shared_last = together(
-        rows.turn(1), rows.cross(0), swap_cols(sent), shared_pair, shared_last
+    rows.held[1, 0], rows.held[0, 1], got, shared_pair, shared_last, plane_codes = together(
+        rows.turn(1), rows.cross(0), swap_cols(sent), shared_pair, shared_last, plane_codes
     )
     rows.got(got, starts, (0, 0))
     grad_rows.got(got, starts[1:], (1, 1))

time: 1170 us -> 1180 us (level)
    ppermute x28, waiting for transfers between devices: 152 us -> 138 us  [swap_cols(): return lax.ppermute(values, 'col', [(0, 1), (1, 0)])]
    unnamed x475 -> x451, local copies, waits for them, and re-layouts: 77.8 us -> 73.4 us
  transfers between devices with their start and end apart: 118 -> 118, of which waited for: 37 -> 39; matrix products, arithmetic and copies ran while one was open for 19% -> 19% of each run, Pallas kernels for 36% -> 36%
where the time goes in v4:
time: 1180 us; the launch traced here: 1160 us
  Pallas kernels  437 us (37%)
  waiting for transfers between devices  287 us (24%)
  other arithmetic  176 us (15%)
  local copies, waits for them, and re-layouts  144 us (12%)
  starting transfers between devices  99.8 us (8%)
  matrix products  16.3 us (1%)
    ppermute x28, waiting for transfers between devices, swap_cols(): return lax.ppermute(values, 'col', [(0, 1), (1, 0)])  138 us
    pallas_call x4, Pallas kernels, run_experts(): pl.pallas_call(body, grid=(count,), in_specs=[wide, wide, narrow, matrix,...  111 us
    pallas_call x4, Pallas kernels, pick_rows(): pl.pallas_call(body, grid=(FAMILIES,), in_specs=[pl.BlockSpec(memory_spac...  82.5 us
    ppermute x66, waiting for transfers between devices, swap_rows(): return lax.ppermute(values, 'row', [(i, i ^ bit) for i in range(16)])  78.2 us
    unnamed x451, local copies, waits for them, and re-layouts  73.4 us
    ppermute x21, waiting for transfers between devices, turn_planes(): return lax.ppermute(values, 'row', [(i, (i + 4) % 16) for i in range(16)])  71 us
    pallas_call x16, Pallas kernels, sum_tokens(): pl.pallas_call(body, grid=(2,), in_specs=in_specs, out_specs=out_specs, o...  70.1 us
    pallas_call x2, Pallas kernels, expert_weight_grads(): pl.pallas_call(body, grid=(count, width // tile), in_specs=[wide] * (2 *...  53.9 us
  transfers between devices with their start and end apart: 118, of which 39 were waited for; matrix products, arithmetic and copies ran while one was open for 19% of the time, Pallas kernels for 36%

profile of v4, /device:TPU:0, one launch (start us, length us, event | category | flops | bytes accessed | tf_op | source)
XLA Modules:
  0.0 1164.6 jit_solution(2432453354799477474)
XLA Ops:
  13.5 13.7 %collective-permute-done.3 = f32[2,1024]{1,0:T(2,128)S(1)} collective-permute-done((f32[2,1024]{1,0:T(2,128)S(1)}, f32[2,1024]{1,0:T(2,128)S(1)}, u32[]{:S(2)}, u32[]{:S(2)}) %collective-permute-start.3) | collective-permute-done | bytes 8224 | tf_op jit(solution)/shard_map/ppermute | solution.py:94
  27.2 7.6 collective-permute-done.refs_4_
  38.4 23.1 %collective-permute-done.4.refs_8_ = bf16[128,3840]{1,0:T(8,128)(2,1)} collective-permute-done((bf16[128,3840]{1,0:T(8,128)(2,1)S(1)}, bf16[128,3840]{1,0:T(8,128)(2,1)}, u32[]{:S(2)}, u32[]{:S(2)}) %collective-permute-start.4) | collective-permute-done | bytes 983072 | tf_op jit(solution)/shard_map/ppermute | solution.py:102
  73.4 12.1 %collective-permute-done.13.refs_1_.refs_9_ = bf16[160,2048]{1,0:T(8,128)(2,1)S(1)} collective-permute-done((bf16[160,2048]{1,0:T(8,128)(2,1)}, bf16[160,2048]{1,0:T(8,128)(2,1)S(1)}, u32[]{:S(2)}, u32[]{:S(2)}) %collective-permute-start.13) | collective-permute-done | bytes 655392 | tf_op jit(solution)/shard_map/ppermute | solution.py:94
  109.0 23.6 %collective-permute-done.14.refs_14_ = bf16[128,3840]{1,0:T(8,128)(2,1)} collective-permute-done((bf16[128,3840]{1,0:T(8,128)(2,1)}, bf16[128,3840]{1,0:T(8,128)(2,1)}, u32[]{:S(2)}, u32[]{:S(2)}) %collective-permute-start.14) | collective-permute-done | bytes 983072 | tf_op jit(solution)/shard_map/ppermute | solution.py:98
  146.8 11.0 shard_map.298
  161.9 9.8 collective-permute-done.20.refs_4_.refs_12_
  181.6 18.4 %shard_map.299 = (bf16[512,1536]{1,0:T(8,128)(2,1)S(1)}, bf16[512,2048]{1,0:T(8,128)(2,1)S(1)}, bf16[512,1024]{1,0:T(8,128)(2,1)S(1)}, bf16[512,2048]{1,0:T(8,128)(2,1)S(1)}) custom-call(bf16[512,2048]{1,0:T(8,128)(2,1)} %copy-done.2, bf16[512,512]{1,0:T(8,128)(2,1)S(1)} %fusion.20.latent_ref, bf16[512,128]{1,0:T(8,128)(2,1)S(1)} %get-tuple-element.877.rope0_ref, ...), custom_call_target="tpu_custom_call" | custom-call | flops 1000000000 | bytes 1000000 | tf_op jit(solution)/shard_map/pallas_call | solution.py:998
  202.6 7.6 collective-permute-done.24.refs_5_.refs_1_.refs_9_.refs_13_
  230.8 26.1 %collective-permute-done.26 = bf16[352,2048]{1,0:T(8,128)(2,1)S(1)} collective-permute-done((bf16[352,2048]{1,0:T(8,128)(2,1)S(1)}, bf16[352,2048]{1,0:T(8,128)(2,1)S(1)}, u32[]{:S(2)}, u32[]{:S(2)}) %collective-permute-start.26) | collective-permute-done | bytes 1441824 | tf_op jit(solution)/shard_map/ppermute | solution.py:94
  282.8 13.9 %collective-permute-done.31.refs_5_.refs_13_.refs_1_ = bf16[320,2048]{1,0:T(8,128)(2,1)} collective-permute-done((bf16[320,2048]{1,0:T(8,128)(2,1)}, bf16[320,2048]{1,0:T(8,128)(2,1)}, u32[]{:S(2)}, u32[]{:S(2)}) %collective-permute-start.31) | collective-permute-done | bytes 1310752 | tf_op jit(solution)/shard_map/ppermute | solution.py:94
  330.4 9.1 collective-permute-done.34.refs_1_.refs_5_
  350.6 30.4 %collective-permute-done.39.refs_5_.refs_1_ = bf16[320,2048]{1,0:T(8,128)(2,1)S(1)} collective-permute-done((bf16[320,2048]{1,0:T(8,128)(2,1)S(1)}, bf16[320,2048]{1,0:T(8,128)(2,1)S(1)}, u32[]{:S(2)}, u32[]{:S(2)}) %collective-permute-start.39) | collective-permute-done | bytes 1310752 | tf_op jit(solution)/shard_map/ppermute | solution.py:94
  401.6 20.5 %shard_map.302 = (bf16[4,256,2048]{2,1,0:T(8,128)(2,1)}, f32[4,256,128]{2,1,0:T(8,128)S(1)}, bf16[4,512,128]{2,1,0:T(8,128)(2,1)S(1)}, bf16[4,512,256]{2,1,0:T(8,128)(2,1)S(1)}, f32[384,2048]{1,0:T(8,128)}) custom-call(bf16[352,2048]{1,0:T(8,128)(2,1)} %collective-permute-done.29.refs_0_, bf16[320,2048]{1,0:T(8,128)(2,1)} %collective-permute-done.34.refs_1_.refs_5_, ...), custom_call_target="tpu_custom_call" | custom-call | flops 1000000000 | bytes 1000000 | tf_op jit(solution)/shard_map/pallas_call | solution.py:400
  436.7 27.5 %shard_map.303 = (bf16[4,256,2048]{2,1,0:T(8,128)(2,1)}, bf16[4,256,2048]{2,1,0:T(8,128)(2,1)}, bf16[4,256,704]{2,1,0:T(8,128)(2,1)}, bf16[4,256,704]{2,1,0:T(8,...) custom-call(bf16[4,256,2048]{2,1,0:T(8,128)(2,1)} %get-tuple-element.431.rows_ref.refs_1_, ...), custom_call_target="tpu_custom_call" | custom-call | flops 1000000000 | bytes 1000000 | tf_op jit(solution)/shard_map/pallas_call | solution.py:479
  495.1 7.3 shard_map.305
  504.5 20.4 %shard_map.306 = (bf16[4,256,2048]{2,1,0:T(8,128)(2,1)}, f32[4,256,128]{2,1,0:T(8,128)S(1)}, bf16[4,512,128]{2,1,0:T(8,128)(2,1)S(1)}, bf16[4,512,256]{2,1,0:T(8,128)(2,1)S(1)}, f32[384,2048]{1,0:T(8,128)}) custom-call(bf16[352,2048]{1,0:T(8,128)(2,1)} %collective-permute-done.32.refs_0_, bf16[320,2048]{1,0:T(8,128)(2,1)S(1)} %copy-done.43, ...), custom_call_target="tpu_custom_call" | custom-call | flops 1000000000 | bytes 1000000 | tf_op jit(solution)/shard_map/pallas_call | solution.py:400
  536.9 27.5 %shard_map.307 = (bf16[4,256,2048]{2,1,0:T(8,128)(2,1)}, bf16[4,256,2048]{2,1,0:T(8,128)(2,1)}, bf16[4,256,704]{2,1,0:T(8,128)(2,1)}, bf16[4,256,704]{2,1,0:T(8,...) custom-call(bf16[4,256,2048]{2,1,0:T(8,128)(2,1)} %get-tuple-element.461.rows_ref.refs_2_, ...), custom_call_target="tpu_custom_call" | custom-call | flops 1000000000 | bytes 1000000 | tf_op jit(solution)/shard_map/pallas_call | solution.py:479
  593.4 21.0 %shard_map.312 = (bf16[4,256,2048]{2,1,0:T(8,128)(2,1)}, f32[4,256,128]{2,1,0:T(8,128)S(1)}, bf16[4,512,128]{2,1,0:T(8,128)(2,1)S(1)}, bf16[4,512,256]{2,1,0:T(8,128)(2,1)S(1)}, f32[384,2048]{1,0:T(8,128)}) custom-call(bf16[352,2048]{1,0:T(8,128)(2,1)} %collective-permute-done.37.refs_0_, bf16[320,2048]{1,0:T(8,128)(2,1)} %collective-permute-done.44.refs_5_.refs_1_, ...), custom_call_target="tpu_custom_call" | custom-call | flops 1000000000 | bytes 1000000 | tf_op jit(solution)/shard_map/pallas_call | solution.py:400
  639.6 27.7 %shard_map.316 = (bf16[4,256,2048]{2,1,0:T(8,128)(2,1)}, bf16[4,256,2048]{2,1,0:T(8,128)(2,1)}, bf16[4,256,704]{2,1,0:T(8,128)(2,1)}, bf16[4,256,704]{2,1,0:T(8,...) custom-call(bf16[4,256,2048]{2,1,0:T(8,128)(2,1)} %get-tuple-element.511.rows_ref.refs_3_, ...), custom_call_target="tpu_custom_call" | custom-call | flops 1000000000 | bytes 1000000 | tf_op jit(solution)/shard_map/pallas_call | solution.py:479
  710.1 20.7 %shard_map.319 = (bf16[4,256,2048]{2,1,0:T(8,128)(2,1)}, f32[4,256,128]{2,1,0:T(8,128)S(1)}, bf16[4,512,128]{2,1,0:T(8,128)(2,1)S(1)}, bf16[4,512,256]{2,1,0:T(8,128)(2,1)S(1)}, f32[384,2048]{1,0:T(8,128)}) custom-call(bf16[352,2048]{1,0:T(8,128)(2,1)} %multiply_convert_fusion.2.refs_0_, bf16[320,2048]{1,0:T(8,128)(2,1)} %collective-permute-done.31.refs_5_.refs_13_.refs_1_, ...), custom_call_target="tpu_custom_call" | custom-call | flops 1000000000 | bytes 1000000 | tf_op jit(solution)/shard_map/pallas_call | solution.py:400
  752.6 27.9 %shard_map.320 = (bf16[4,256,2048]{2,1,0:T(8,128)(2,1)}, bf16[4,256,2048]{2,1,0:T(8,128)(2,1)}, bf16[4,256,704]{2,1,0:T(8,128)(2,1)}, bf16[4,256,704]{2,1,0:T(8,...) custom-call(bf16[4,256,2048]{2,1,0:T(8,128)(2,1)} %get-tuple-element.546.rows_ref.refs_0_, ...), custom_call_target="tpu_custom_call" | custom-call | flops 1000000000 | bytes 1000000 | tf_op jit(solution)/shard_map/pallas_call | solution.py:479
  809.0 26.8 %shard_map.324 = (f32[4,704,2048]{2,1,0:T(8,128)}, f32[4,704,2048]{2,1,0:T(8,128)}, f32[4,704,2048]{2,1,0:T(8,128)}) custom-call(bf16[4,256,2048]{2,1,0:T(8,128)(2,1)} %get-tuple-element.546.rows_ref.refs_0_, bf16[4,256,2048]{2,1,0:T(8,128)(2,1)} %get-tuple-element.431.rows_ref.refs_1_, bf16[4,256,2048]{2,1,0:T(8,128)(2,1)} %get-tuple-element.461.rows_ref.refs_2_, ...), custom_call_target="tpu_custom_call" | custom-call | flops 1000000000 | bytes 1000000 | tf_op jit(solution)/shard_map/pallas_call | solution.py:894
  870.3 27.1 %shard_map.328 = (f32[4,704,2048]{2,1,0:T(8,128)}, f32[4,704,2048]{2,1,0:T(8,128)}, f32[4,704,2048]{2,1,0:T(8,128)}) custom-call(bf16[4,256,2048]{2,1,0:T(8,128)(2,1)} %get-tuple-element.546.rows_ref.refs_0_, bf16[4,256,2048]{2,1,0:T(8,128)(2,1)} %get-tuple-element.431.rows_ref.refs_1_, ...), custom_call_target="tpu_custom_call", output_to_operand_aliasing={{0}: (20, {}), {1}: (21, {}), {2}: (22, {})} | custom-call | flops 1000000000 | bytes 1000000 | tf_op jit(solution)/shard_map/pallas_call | solution.py:894
  928.7 8.3 collective-permute-done.86
  954.4 28.7 %shard_map.330 = (bf16[512,1536]{1,0:T(8,128)(2,1)}, bf16[512,2048]{1,0:T(8,128)(2,1)}, f32[512,128]{1,0:T(8,128)S(1)}, f32[512,512]{1,0:T(8,128)}, bf16[512,2048]{1,0:T(8,128)(2,1)}) custom-call(bf16[512,2048]{1,0:T(8,128)(2,1)} %copy-done.15, bf16[512,1536]{1,0:T(8,128)(2,1)} %copy-done.118, bf16[512,2048]{1,0:T(8,128)(2,1)} %copy-done.101, ...), custom_call_target="tpu_custom_call" | custom-call | flops 1000000000 | bytes 1000000 | tf_op jit(solution)/shard_map/pallas_call | solution.py:1112
  993.0 7.2 shard_map.332
  1038.4 8.3 collective-permute-done.95
  1059.6 10.7 shard_map.335
  1091.9 8.3 collective-permute-done.98
  1129.6 11.6 collective-permute-done.109
  1150.0 8.9 collective-permute-done.112
  (905 shorter events, 607.8 us)
Async XLA Ops:
  90.9 42.6 %collective-permute-start.17 = (bf16[512,2048]{1,0:T(8,128)(2,1)}, bf16[512,2048]{1,0:T(8,128)(2,1)}, u32[]{:S(2)}, u32[]{:S(2)}) collective-permute-start(bf16[512,2048]{1,0:T(8,128)(2,1)} %pad_maximum_fusion.8), channel_id=1, source_target_pairs={{0,2},{2,0},{4,6},{6,4},{8,10},{10,8},{12,14},{14,12},{16,18},{18,... | collective-permute-start | bytes 6291464 | tf_op jit(solution)/shard_map/ppermute | solution.py:98
  92.0 41.5 %all-to-all-start = ((bf16[16,3,88,128]{3,2,1,0:T(8,128)(2,1)}), bf16[16,3,88,128]{3,2,1,0:T(8,128)(2,1)}, u32[]{:S(2)}, u32[]{:S(2)}) async-start(bf16[16,3,88,128]{3,2,1,0:T(8,128)(2,1)} %copy.173), calls=%async_computation | async-start | bytes 2162688 | tf_op jit(solution)/shard_map/all_to_all | solution.py:1281
  218.9 39.5 %collective-permute-start.28 = (bf16[672,2048]{1,0:T(8,128)(2,1)}, bf16[672,2048]{1,0:T(8,128)(2,1)}, u32[]{:S(2)}, u32[]{:S(2)}) collective-permute-start(bf16[672,2048]{1,0:T(8,128)(2,1)} %pad_maximum_fusion.7), channel_id=1, source_target_pairs={{0,2},{2,0},{4,6},{6,4},{8,10},{10,8},{12,14},{14,12},{16,18},{18,... | collective-permute-start | bytes 8257544 | tf_op jit(solution)/shard_map/ppermute | solution.py:98
  304.4 38.5 %collective-permute-start.35 = (bf16[864,2048]{1,0:T(8,128)(2,1)}, bf16[864,2048]{1,0:T(8,128)(2,1)}, u32[]{:S(2)}, u32[]{:S(2)}) collective-permute-start(bf16[864,2048]{1,0:T(8,128)(2,1)} %pad_maximum_fusion), channel_id=1, source_target_pairs={{0,2},{2,0},{4,6},{6,4},{8,10},{10,8},{12,14},{14,12},{16,18},{18,... | collective-permute-start | bytes 10616840 | tf_op jit(solution)/shard_map/ppermute | solution.py:98
  347.1 38.5 %collective-permute-start.40 = (bf16[864,2048]{1,0:T(8,128)(2,1)S(1)}, bf16[864,2048]{1,0:T(8,128)(2,1)S(1)}, u32[]{:S(2)}, u32[]{:S(2)}) collective-permute-start(bf16[864,2048]{1,0:T(8,128)(2,1)S(1)} %pad_maximum_fusion.1), channel_id=1, source_target_pairs={{0,2},{2,0},{4,6},{6,4},{8,10},{10,8},{12,14},{14,12},{16,18},{18,... | collective-permute-start | bytes 10616840 | tf_op jit(solution)/shard_map/ppermute | solution.py:98
  398.7 74.7 %collective-permute-start.50 = (bf16[704,2048]{1,0:T(8,128)(2,1)}, bf16[704,2048]{1,0:T(8,128)(2,1)S(1)}, u32[]{:S(2)}, u32[]{:S(2)}) collective-permute-start(bf16[704,2048]{1,0:T(8,128)(2,1)} %pad_maximum_fusion.6), channel_id=1, source_target_pairs={{0,2},{2,0},{4,6},{6,4},{8,10},{10,8},{12,14},{14,12},{16,18},{18,... | collective-permute-start | bytes 8650760 | tf_op jit(solution)/shard_map/ppermute | solution.py:98
  430.7 50.3 %collective-permute-start.49 = (bf16[704,2048]{1,0:T(8,128)(2,1)}, bf16[704,2048]{1,0:T(8,128)(2,1)}, u32[]{:S(2)}, u32[]{:S(2)}) collective-permute-start(bf16[704,2048]{1,0:T(8,128)(2,1)} %pad_maximum_fusion.5), channel_id=1, source_target_pairs={{0,2},{2,0},{4,6},{6,4},{8,10},{10,8},{12,14},{14,12},{16,18},{18,... | collective-permute-start | bytes 8650760 | tf_op jit(solution)/shard_map/ppermute | solution.py:98
  435.6 45.4 %collective-permute-start.47 = (bf16[480,2048]{1,0:T(8,128)(2,1)}, bf16[480,2048]{1,0:T(8,128)(2,1)S(1)}, u32[]{:S(2)}, u32[]{:S(2)}) collective-permute-start(bf16[480,2048]{1,0:T(8,128)(2,1)} %pad_maximum_fusion.9), channel_id=1, source_target_pairs={{0,1},{1,0},{2,3},{3,2},{4,5},{5,4},{6,7},{7,6},{8,9},{9,8},{10,11... | collective-permute-start | bytes 5898248 | tf_op jit(solution)/shard_map/ppermute | solution.py:94
  436.2 38.8 %collective-permute-start.46 = (bf16[352,2048]{1,0:T(8,128)(2,1)S(1)}, bf16[352,2048]{1,0:T(8,128)(2,1)}, u32[]{:S(2)}, u32[]{:S(2)}) collective-permute-start(bf16[352,2048]{1,0:T(8,128)(2,1)S(1)} %copy-done.25), channel_id=1, source_target_pairs={{0,4},{2,6},{4,0},{6,2},{8,12},{10,14},{12,8},{14,10},{16,20},{18,... | collective-permute-start | bytes 4325384 | tf_op jit(solution)/shard_map/ppermute | solution.py:98
  436.5 38.5 %collective-permute-start.48 = (bf16[320,2048]{1,0:T(8,128)(2,1)}, bf16[320,2048]{1,0:T(8,128)(2,1)}, u32[]{:S(2)}, u32[]{:S(2)}) collective-permute-start(bf16[320,2048]{1,0:T(8,128)(2,1)} %collective-permute-done.44.refs_5_.refs_1_), channel_id=1, source_target_pairs={{0,2},{2,0},{4,6},{6,4},{8,10},{10,8},{12,14},{14,12},{16,18},{18,... | collective-permute-start | bytes 3932168 | tf_op jit(solution)/shard_map/ppermute | solution.py:98
  481.0 44.0 %collective-permute-start.52 = (bf16[2,512,2048]{2,1,0:T(8,128)(2,1)}, bf16[2,512,2048]{2,1,0:T(8,128)(2,1)}, u32[]{:S(2)}, u32[]{:S(2)}) collective-permute-start(bf16[2,512,2048]{2,1,0:T(8,128)(2,1)} %get-tuple-element.459), channel_id=1, source_target_pairs={{0,2},{2,0},{4,6},{6,4},{8,10},{10,8},{12,14},{14,12},{16,18},{18,... | collective-permute-start | bytes 12582920 | tf_op jit(solution)/shard_map/ppermute | solution.py:98
  484.7 40.3 %collective-permute-start.54 = (bf16[864,2048]{1,0:T(8,128)(2,1)}, bf16[864,2048]{1,0:T(8,128)(2,1)S(1)}, u32[]{:S(2)}, u32[]{:S(2)}) collective-permute-start(bf16[864,2048]{1,0:T(8,128)(2,1)} %pad_maximum_fusion.3), channel_id=1, source_target_pairs={{0,2},{2,0},{4,6},{6,4},{8,10},{10,8},{12,14},{14,12},{16,18},{18,... | collective-permute-start | bytes 10616840 | tf_op jit(solution)/shard_map/ppermute | solution.py:98
  572.1 42.3 %collective-permute-start.58 = (bf16[2,512,2048]{2,1,0:T(8,128)(2,1)}, bf16[2,512,2048]{2,1,0:T(8,128)(2,1)}, u32[]{:S(2)}, u32[]{:S(2)}) collective-permute-start(bf16[2,512,2048]{2,1,0:T(8,128)(2,1)} %get-tuple-element.495), channel_id=1, source_target_pairs={{0,2},{2,0},{4,6},{6,4},{8,10},{10,8},{12,14},{14,12},{16,18},{18,... | collective-permute-start | bytes 12582920 | tf_op jit(solution)/shard_map/ppermute | solution.py:98
  630.7 44.9 %collective-permute-start.64 = (bf16[2,512,2048]{2,1,0:T(8,128)(2,1)}, bf16[2,512,2048]{2,1,0:T(8,128)(2,1)}, u32[]{:S(2)}, u32[]{:S(2)}) collective-permute-start(bf16[2,512,2048]{2,1,0:T(8,128)(2,1)} %shard_map.315), channel_id=1, source_target_pairs={{0,2},{2,0},{4,6},{6,4},{8,10},{10,8},{12,14},{14,12},{16,18},{18,... | collective-permute-start | bytes 12582920 | tf_op jit(solution)/shard_map/ppermute | solution.py:98
  635.3 40.3 %collective-permute-start.65 = (bf16[352,2048]{1,0:T(8,128)(2,1)}, bf16[352,2048]{1,0:T(8,128)(2,1)}, u32[]{:S(2)}, u32[]{:S(2)}) collective-permute-start(bf16[352,2048]{1,0:T(8,128)(2,1)} %pad_maximum_fusion.14), channel_id=1, source_target_pairs={{0,4},{2,6},{4,0},{6,2},{8,12},{10,14},{12,8},{14,10},{16,20},{18,... | collective-permute-start | bytes 4325384 | tf_op jit(solution)/shard_map/ppermute | solution.py:98
  637.0 38.6 %collective-permute-start.62 = (bf16[352,2048]{1,0:T(8,128)(2,1)}, bf16[352,2048]{1,0:T(8,128)(2,1)}, u32[]{:S(2)}, u32[]{:S(2)}) collective-permute-start(bf16[352,2048]{1,0:T(8,128)(2,1)} %maximum_add_fusion.3), channel_id=1, source_target_pairs={{0,8},{2,10},{4,12},{6,14},{8,16},{10,18},{12,20},{14,22},{16,24},... | collective-permute-start | bytes 4325384 | tf_op jit(solution)/shard_map/ppermute | solution.py:102
  637.0 38.6 %collective-permute-start.63 = (bf16[2,160,2048]{2,1,0:T(8,128)(2,1)}, bf16[2,160,2048]{2,1,0:T(8,128)(2,1)}, u32[]{:S(2)}, u32[]{:S(2)}) collective-permute-start(bf16[2,160,2048]{2,1,0:T(8,128)(2,1)} %get-tuple-element.523), channel_id=1, source_target_pairs={{0,1},{1,0},{2,3},{3,2},{4,5},{5,4},{6,7},{7,6},{8,9},{9,8},{10,11... | collective-permute-start | bytes 3932168 | tf_op jit(solution)/shard_map/ppermute | solution.py:94
  639.6 70.5 %collective-permute-start.66 = (bf16[160,2048]{1,0:T(8,128)(2,1)}, bf16[160,2048]{1,0:T(8,128)(2,1)}, u32[]{:S(2)}, u32[]{:S(2)}) collective-permute-start(bf16[160,2048]{1,0:T(8,128)(2,1)} %get-tuple-element.860), channel_id=1, source_target_pairs={{0,2},{2,0},{4,6},{6,4},{8,10},{10,8},{12,14},{14,12},{16,18},{18,... | collective-permute-start | bytes 1966088 | tf_op jit(solution)/shard_map/ppermute | solution.py:98
  680.8 51.9 %collective-permute-start.67 = (bf16[2,512,2048]{2,1,0:T(8,128)(2,1)}, bf16[2,512,2048]{2,1,0:T(8,128)(2,1)}, u32[]{:S(2)}, u32[]{:S(2)}) collective-permute-start(bf16[2,512,2048]{2,1,0:T(8,128)(2,1)} %get-tuple-element.542), channel_id=1, source_target_pairs={{0,2},{2,0},{4,6},{6,4},{8,10},{10,8},{12,14},{14,12},{16,18},{18,... | collective-permute-start | bytes 12582920 | tf_op jit(solution)/shard_map/ppermute | solution.py:98
  685.0 47.7 %collective-permute-start.69 = (bf16[2,160,2048]{2,1,0:T(8,128)(2,1)}, bf16[2,160,2048]{2,1,0:T(8,128)(2,1)}, u32[]{:S(2)}, u32[]{:S(2)}) collective-permute-start(bf16[2,160,2048]{2,1,0:T(8,128)(2,1)} %get-tuple-element.532), channel_id=1, source_target_pairs={{0,1},{1,0},{2,3},{3,2},{4,5},{5,4},{6,7},{7,6},{8,9},{9,8},{10,11... | collective-permute-start | bytes 3932168 | tf_op jit(solution)/shard_map/ppermute | solution.py:94
  689.2 43.4 %collective-permute-start.68 = (bf16[352,2048]{1,0:T(8,128)(2,1)}, bf16[352,2048]{1,0:T(8,128)(2,1)}, u32[]{:S(2)}, u32[]{:S(2)}) collective-permute-start(bf16[352,2048]{1,0:T(8,128)(2,1)} %pad_maximum_fusion.15), channel_id=1, source_target_pairs={{0,4},{2,6},{4,0},{6,2},{8,12},{10,14},{12,8},{14,10},{16,20},{18,... | collective-permute-start | bytes 4325384 | tf_op jit(solution)/shard_map/ppermute | solution.py:98
  690.0 42.6 %collective-permute-start.70 = (bf16[352,2048]{1,0:T(8,128)(2,1)}, bf16[352,2048]{1,0:T(8,128)(2,1)}, u32[]{:S(2)}, u32[]{:S(2)}) collective-permute-start(bf16[352,2048]{1,0:T(8,128)(2,1)} %maximum_add_fusion.4), channel_id=1, source_target_pairs={{0,8},{2,10},{4,12},{6,14},{8,16},{10,18},{12,20},{14,22},{16,24},... | collective-permute-start | bytes 4325384 | tf_op jit(solution)/shard_map/ppermute | solution.py:102
  742.8 45.0 %collective-permute-start.73 = (bf16[2,512,2048]{2,1,0:T(8,128)(2,1)S(1)}, bf16[2,512,2048]{2,1,0:T(8,128)(2,1)}, u32[]{:S(2)}, u32[]{:S(2)}) collective-permute-start(bf16[2,512,2048]{2,1,0:T(8,128)(2,1)S(1)} %copy-done.59), channel_id=1, source_target_pairs={{0,2},{2,0},{4,6},{6,4},{8,10},{10,8},{12,14},{14,12},{16,18},{18,... | collective-permute-start | bytes 12582920 | tf_op jit(solution)/shard_map/ppermute | solution.py:98
  747.4 40.4 %collective-permute-start.74 = (bf16[352,2048]{1,0:T(8,128)(2,1)}, bf16[352,2048]{1,0:T(8,128)(2,1)}, u32[]{:S(2)}, u32[]{:S(2)}) collective-permute-start(bf16[352,2048]{1,0:T(8,128)(2,1)} %pad_maximum_fusion.16), channel_id=1, source_target_pairs={{0,4},{2,6},{4,0},{6,2},{8,12},{10,14},{12,8},{14,10},{16,20},{18,... | collective-permute-start | bytes 4325384 | tf_op jit(solution)/shard_map/ppermute | solution.py:98
  749.1 38.7 %collective-permute-start.71 = (bf16[352,2048]{1,0:T(8,128)(2,1)}, bf16[352,2048]{1,0:T(8,128)(2,1)}, u32[]{:S(2)}, u32[]{:S(2)}) collective-permute-start(bf16[352,2048]{1,0:T(8,128)(2,1)} %fusion.8), channel_id=1, source_target_pairs={{0,8},{2,10},{4,12},{6,14},{8,16},{10,18},{12,20},{14,22},{16,24},... | collective-permute-start | bytes 4325384 | tf_op jit(solution)/shard_map/ppermute | solution.py:102
  787.8 49.9 %collective-permute-start.75 = (bf16[2,512,2048]{2,1,0:T(8,128)(2,1)}, bf16[2,512,2048]{2,1,0:T(8,128)(2,1)}, u32[]{:S(2)}, u32[]{:S(2)}) collective-permute-start(bf16[2,512,2048]{2,1,0:T(8,128)(2,1)} %get-tuple-element.588), channel_id=1, source_target_pairs={{0,2},{2,0},{4,6},{6,4},{8,10},{10,8},{12,14},{14,12},{16,18},{18,... | collective-permute-start | bytes 12582920 | tf_op jit(solution)/shard_map/ppermute | solution.py:98
  848.0 49.6 %collective-permute-start.81 = (bf16[2,512,2048]{2,1,0:T(8,128)(2,1)}, bf16[2,512,2048]{2,1,0:T(8,128)(2,1)}, u32[]{:S(2)}, u32[]{:S(2)}) collective-permute-start(bf16[2,512,2048]{2,1,0:T(8,128)(2,1)} %shard_map.327), channel_id=1, source_target_pairs={{0,2},{2,0},{4,6},{6,4},{8,10},{10,8},{12,14},{14,12},{16,18},{18,... | collective-permute-start | bytes 12582920 | tf_op jit(solution)/shard_map/ppermute | solution.py:98
  853.9 43.7 %collective-permute-start.79 = (bf16[352,2048]{1,0:T(8,128)(2,1)}, bf16[352,2048]{1,0:T(8,128)(2,1)}, u32[]{:S(2)}, u32[]{:S(2)}) collective-permute-start(bf16[352,2048]{1,0:T(8,128)(2,1)} %fusion.10), channel_id=1, source_target_pairs={{0,8},{2,10},{4,12},{6,14},{8,16},{10,18},{12,20},{14,22},{16,24},... | collective-permute-start | bytes 4325384 | tf_op jit(solution)/shard_map/ppermute | solution.py:102
  857.9 39.6 %collective-permute-start.82 = (bf16[192,2048]{1,0:T(8,128)(2,1)}, bf16[192,2048]{1,0:T(8,128)(2,1)}, u32[]{:S(2)}, u32[]{:S(2)}) collective-permute-start(bf16[192,2048]{1,0:T(8,128)(2,1)} %slice_bitcast_fusion.5), channel_id=1, source_target_pairs={{0,4},{2,6},{4,0},{6,2},{8,12},{10,14},{12,8},{14,10},{16,20},{18,... | collective-permute-start | bytes 2359304 | tf_op jit(solution)/shard_map/ppermute | solution.py:98
  920.0 70.0 %collective-permute-start.88 = (bf16[2,160,2048]{2,1,0:T(8,128)(2,1)}, bf16[2,160,2048]{2,1,0:T(8,128)(2,1)}, u32[]{:S(2)}, u32[]{:S(2)}) collective-permute-start(bf16[2,160,2048]{2,1,0:T(8,128)(2,1)} %get-tuple-element.645), channel_id=1, source_target_pairs={{0,1},{1,0},{2,3},{3,2},{4,5},{5,4},{6,7},{7,6},{8,9},{9,8},{10,11... | collective-permute-start | bytes 3932168 | tf_op jit(solution)/shard_map/ppermute | solution.py:94
  922.6 67.4 %all-to-all-start.2 = ((bf16[16,3,88,128]{3,2,1,0:T(8,128)(2,1)}), bf16[16,3,88,128]{3,2,1,0:T(8,128)(2,1)}, u32[]{:S(2)}, u32[]{:S(2)}) async-start(bf16[16,3,88,128]{3,2,1,0:T(8,128)(2,1)} %copy.188), calls=%async_computation.2 | async-start | bytes 2162688 | tf_op jit(solution)/shard_map/all_to_all | solution.py:1697
  1090.5 39.2 %collective-permute-start.106 = (bf16[128,2688]{1,0:T(8,128)(2,1)}, bf16[128,2688]{1,0:T(8,128)(2,1)S(1)}, u32[]{:S(2)}, u32[]{:S(2)}) collective-permute-start(bf16[128,2688]{1,0:T(8,128)(2,1)} %get-tuple-element.814), channel_id=1, source_target_pairs={{0,4},{2,6},{4,0},{6,2},{8,12},{10,14},{12,8},{14,10},{16,20},{18,... | collective-permute-start | bytes 2064392 | tf_op jit(solution)/shard_map/ppermute | solution.py:98
  (308 other events, 4278.0 us)

commit v5 on v4

--- a/solution.py
+++ b/solution.py
@@ -550,7 +550,7 @@
         in_specs=in_specs,
         out_specs=out_specs,
         out_shape=out_shape,
-        compiler_params=kernel_params(24),
+        compiler_params=kernel_params(60),
         cost_estimate=short_cost(),
     )(*operands)
 

time: 1180 us -> 1180 us (level)
  Pallas kernels: 437 us -> 460 us
  local copies, waits for them, and re-layouts: 144 us -> 127 us
    pallas_call x16, Pallas kernels: 70.1 us -> 94.1 us  [sum_tokens(): pl.pallas_call(body, grid=(2,), in_specs=in_specs, out_specs=out_specs, o...]
    unnamed x451 -> x371, local copies, waits for them, and re-layouts: 73.4 us -> 56.9 us
  transfers between devices with their start and end apart: 118 -> 118, of which waited for: 39 -> 41; matrix products, arithmetic and copies ran while one was open for 19% -> 19% of each run, Pallas kernels for 36% -> 38%
where the time goes in v5:
time: 1180 us; the launch traced here: 1170 us
  Pallas kernels  460 us (39%)
  waiting for transfers between devices  292 us (25%)
  other arithmetic  169 us (14%)
  local copies, waits for them, and re-layouts  127 us (11%)
  starting transfers between devices  101 us (9%)
  matrix products  16 us (1%)
    ppermute x28, waiting for transfers between devices, swap_cols(): return lax.ppermute(values, 'col', [(0, 1), (1, 0)])  141 us
    pallas_call x4, Pallas kernels, run_experts(): pl.pallas_call(body, grid=(count,), in_specs=[wide, wide, narrow, matrix,...  111 us
    pallas_call x16, Pallas kernels, sum_tokens(): pl.pallas_call(body, grid=(2,), in_specs=in_specs, out_specs=out_specs, o...  94.1 us
    pallas_call x4, Pallas kernels, pick_rows(): pl.pallas_call(body, grid=(FAMILIES,), in_specs=[pl.BlockSpec(memory_spac...  81.7 us
    ppermute x66, waiting for transfers between devices, swap_rows(): return lax.ppermute(values, 'row', [(i, i ^ bit) for i in range(16)])  77.5 us
    ppermute x21, waiting for transfers between devices, turn_planes(): return lax.ppermute(values, 'row', [(i, (i + 4) % 16) for i in range(16)])  72.9 us
    unnamed x371, local copies, waits for them, and re-layouts  56.9 us
    pallas_call x2, Pallas kernels, expert_weight_grads(): pl.pallas_call(body, grid=(count, width // tile), in_specs=[wide] * (2 *...  53.7 us
  transfers between devices with their start and end apart: 118, of which 41 were waited for; matrix products, arithmetic and copies ran while one was open for 19% of the time, Pallas kernels for 38%

profile of v5, /device:TPU:0, one launch (start us, length us, event | category | flops | bytes accessed | tf_op | source)
XLA Modules:
  0.0 1168.2 jit_solution(9341409195255508740)
XLA Ops:
  13.5 13.7 %collective-permute-done.3 = f32[2,1024]{1,0:T(2,128)S(1)} collective-permute-done((f32[2,1024]{1,0:T(2,128)S(1)}, f32[2,1024]{1,0:T(2,128)S(1)}, u32[]{:S(2)}, u32[]{:S(2)}) %collective-permute-start.3) | collective-permute-done | bytes 8224 | tf_op jit(solution)/shard_map/ppermute | solution.py:94
  27.2 7.6 collective-permute-done.refs_4_
  38.4 23.1 %collective-permute-done.4.refs_8_ = bf16[128,3840]{1,0:T(8,128)(2,1)} collective-permute-done((bf16[128,3840]{1,0:T(8,128)(2,1)S(1)}, bf16[128,3840]{1,0:T(8,128)(2,1)}, u32[]{:S(2)}, u32[]{:S(2)}) %collective-permute-start.4) | collective-permute-done | bytes 983072 | tf_op jit(solution)/shard_map/ppermute | solution.py:102
  73.4 12.1 %collective-permute-done.13.refs_1_.refs_9_ = bf16[160,2048]{1,0:T(8,128)(2,1)S(1)} collective-permute-done((bf16[160,2048]{1,0:T(8,128)(2,1)}, bf16[160,2048]{1,0:T(8,128)(2,1)S(1)}, u32[]{:S(2)}, u32[]{:S(2)}) %collective-permute-start.13) | collective-permute-done | bytes 655392 | tf_op jit(solution)/shard_map/ppermute | solution.py:94
  108.9 23.6 %collective-permute-done.14.refs_14_ = bf16[128,3840]{1,0:T(8,128)(2,1)} collective-permute-done((bf16[128,3840]{1,0:T(8,128)(2,1)}, bf16[128,3840]{1,0:T(8,128)(2,1)}, u32[]{:S(2)}, u32[]{:S(2)}) %collective-permute-start.14) | collective-permute-done | bytes 983072 | tf_op jit(solution)/shard_map/ppermute | solution.py:98
  146.8 11.1 shard_map.298
  161.9 9.7 collective-permute-done.20.refs_4_.refs_12_
  181.6 18.4 %shard_map.299 = (bf16[512,1536]{1,0:T(8,128)(2,1)S(1)}, bf16[512,2048]{1,0:T(8,128)(2,1)S(1)}, bf16[512,1024]{1,0:T(8,128)(2,1)S(1)}, bf16[512,2048]{1,0:T(8,128)(2,1)S(1)}) custom-call(bf16[512,2048]{1,0:T(8,128)(2,1)} %copy-done.8, bf16[512,512]{1,0:T(8,128)(2,1)S(1)} %fusion.20.latent_ref, bf16[512,128]{1,0:T(8,128)(2,1)S(1)} %get-tuple-element.877.rope0_ref, ...), custom_call_target="tpu_custom_call" | custom-call | flops 1000000000 | bytes 1000000 | tf_op jit(solution)/shard_map/pallas_call | solution.py:998
  227.5 28.1 %collective-permute-done.26 = bf16[352,2048]{1,0:T(8,128)(2,1)S(1)} collective-permute-done((bf16[352,2048]{1,0:T(8,128)(2,1)S(1)}, bf16[352,2048]{1,0:T(8,128)(2,1)S(1)}, u32[]{:S(2)}, u32[]{:S(2)}) %collective-permute-start.26) | collective-permute-done | bytes 1441824 | tf_op jit(solution)/shard_map/ppermute | solution.py:94
  280.5 13.7 %collective-permute-done.31.refs_5_.refs_13_.refs_1_ = bf16[320,2048]{1,0:T(8,128)(2,1)} collective-permute-done((bf16[320,2048]{1,0:T(8,128)(2,1)}, bf16[320,2048]{1,0:T(8,128)(2,1)}, u32[]{:S(2)}, u32[]{:S(2)}) %collective-permute-start.31) | collective-permute-done | bytes 1310752 | tf_op jit(solution)/shard_map/ppermute | solution.py:94
  320.9 7.4 shard_map.301
  328.3 9.7 collective-permute-done.34.refs_1_.refs_5_
  349.2 30.4 %collective-permute-done.39.refs_5_.refs_1_ = bf16[320,2048]{1,0:T(8,128)(2,1)S(1)} collective-permute-done((bf16[320,2048]{1,0:T(8,128)(2,1)S(1)}, bf16[320,2048]{1,0:T(8,128)(2,1)S(1)}, u32[]{:S(2)}, u32[]{:S(2)}) %collective-permute-start.39) | collective-permute-done | bytes 1310752 | tf_op jit(solution)/shard_map/ppermute | solution.py:94
  398.9 20.5 %shard_map.302 = (bf16[4,256,2048]{2,1,0:T(8,128)(2,1)}, f32[4,256,128]{2,1,0:T(8,128)S(1)}, bf16[4,512,128]{2,1,0:T(8,128)(2,1)S(1)}, bf16[4,512,256]{2,1,0:T(8,128)(2,1)S(1)}, f32[384,2048]{1,0:T(8,128)}) custom-call(bf16[352,2048]{1,0:T(8,128)(2,1)} %collective-permute-done.29.refs_0_, bf16[320,2048]{1,0:T(8,128)(2,1)} %collective-permute-done.34.refs_1_.refs_5_, ...), custom_call_target="tpu_custom_call" | custom-call | flops 1000000000 | bytes 1000000 | tf_op jit(solution)/shard_map/pallas_call | solution.py:400
  434.0 27.5 %shard_map.303 = (bf16[4,256,2048]{2,1,0:T(8,128)(2,1)}, bf16[4,256,2048]{2,1,0:T(8,128)(2,1)}, bf16[4,256,704]{2,1,0:T(8,128)(2,1)}, bf16[4,256,704]{2,1,0:T(8,...) custom-call(bf16[4,256,2048]{2,1,0:T(8,128)(2,1)} %get-tuple-element.431.rows_ref.refs_1_, ...), custom_call_target="tpu_custom_call" | custom-call | flops 1000000000 | bytes 1000000 | tf_op jit(solution)/shard_map/pallas_call | solution.py:479
  467.5 11.1 collective-permute-done.47.refs_1_.refs_5_.refs_9_.refs_13_
  507.9 20.1 %shard_map.306 = (bf16[4,256,2048]{2,1,0:T(8,128)(2,1)}, f32[4,256,128]{2,1,0:T(8,128)S(1)}, bf16[4,512,128]{2,1,0:T(8,128)(2,1)S(1)}, bf16[4,512,256]{2,1,0:T(8,128)(2,1)S(1)}, f32[384,2048]{1,0:T(8,128)}) custom-call(bf16[352,2048]{1,0:T(8,128)(2,1)} %collective-permute-done.32.refs_0_, bf16[320,2048]{1,0:T(8,128)(2,1)S(1)} %copy-done.32, ...), custom_call_target="tpu_custom_call" | custom-call | flops 1000000000 | bytes 1000000 | tf_op jit(solution)/shard_map/pallas_call | solution.py:400
  537.8 27.5 %shard_map.307 = (bf16[4,256,2048]{2,1,0:T(8,128)(2,1)}, bf16[4,256,2048]{2,1,0:T(8,128)(2,1)}, bf16[4,256,704]{2,1,0:T(8,128)(2,1)}, bf16[4,256,704]{2,1,0:T(8,...) custom-call(bf16[4,256,2048]{2,1,0:T(8,128)(2,1)} %get-tuple-element.461.rows_ref.refs_2_, ...), custom_call_target="tpu_custom_call" | custom-call | flops 1000000000 | bytes 1000000 | tf_op jit(solution)/shard_map/pallas_call | solution.py:479
  589.4 7.4 shard_map.311
  598.7 20.7 %shard_map.312 = (bf16[4,256,2048]{2,1,0:T(8,128)(2,1)}, f32[4,256,128]{2,1,0:T(8,128)S(1)}, bf16[4,512,128]{2,1,0:T(8,128)(2,1)S(1)}, bf16[4,512,256]{2,1,0:T(8,128)(2,1)S(1)}, f32[384,2048]{1,0:T(8,128)}) custom-call(bf16[352,2048]{1,0:T(8,128)(2,1)} %collective-permute-done.37.refs_0_, bf16[320,2048]{1,0:T(8,128)(2,1)} %collective-permute-done.44.refs_5_.refs_1_, ...), custom_call_target="tpu_custom_call" | custom-call | flops 1000000000 | bytes 1000000 | tf_op jit(solution)/shard_map/pallas_call | solution.py:400
  645.9 27.7 %shard_map.316 = (bf16[4,256,2048]{2,1,0:T(8,128)(2,1)}, bf16[4,256,2048]{2,1,0:T(8,128)(2,1)}, bf16[4,256,704]{2,1,0:T(8,128)(2,1)}, bf16[4,256,704]{2,1,0:T(8,...) custom-call(bf16[4,256,2048]{2,1,0:T(8,128)(2,1)} %get-tuple-element.511.rows_ref.refs_3_, ...), custom_call_target="tpu_custom_call" | custom-call | flops 1000000000 | bytes 1000000 | tf_op jit(solution)/shard_map/pallas_call | solution.py:479
  715.9 20.4 %shard_map.319 = (bf16[4,256,2048]{2,1,0:T(8,128)(2,1)}, f32[4,256,128]{2,1,0:T(8,128)S(1)}, bf16[4,512,128]{2,1,0:T(8,128)(2,1)S(1)}, bf16[4,512,256]{2,1,0:T(8,128)(2,1)S(1)}, f32[384,2048]{1,0:T(8,128)}) custom-call(bf16[352,2048]{1,0:T(8,128)(2,1)} %multiply_convert_fusion.2.refs_0_, bf16[320,2048]{1,0:T(8,128)(2,1)} %collective-permute-done.31.refs_5_.refs_13_.refs_1_, ...), custom_call_target="tpu_custom_call" | custom-call | flops 1000000000 | bytes 1000000 | tf_op jit(solution)/shard_map/pallas_call | solution.py:400
  755.8 28.0 %shard_map.320 = (bf16[4,256,2048]{2,1,0:T(8,128)(2,1)}, bf16[4,256,2048]{2,1,0:T(8,128)(2,1)}, bf16[4,256,704]{2,1,0:T(8,128)(2,1)}, bf16[4,256,704]{2,1,0:T(8,...) custom-call(bf16[4,256,2048]{2,1,0:T(8,128)(2,1)} %get-tuple-element.546.rows_ref.refs_0_, ...), custom_call_target="tpu_custom_call" | custom-call | flops 1000000000 | bytes 1000000 | tf_op jit(solution)/shard_map/pallas_call | solution.py:479
  812.8 26.6 %shard_map.324 = (f32[4,704,2048]{2,1,0:T(8,128)}, f32[4,704,2048]{2,1,0:T(8,128)}, f32[4,704,2048]{2,1,0:T(8,128)}) custom-call(bf16[4,256,2048]{2,1,0:T(8,128)(2,1)} %get-tuple-element.546.rows_ref.refs_0_, bf16[4,256,2048]{2,1,0:T(8,128)(2,1)} %get-tuple-element.431.rows_ref.refs_1_, bf16[4,256,2048]{2,1,0:T(8,128)(2,1)} %get-tuple-element.461.rows_ref.refs_2_, ...), custom_call_target="tpu_custom_call" | custom-call | flops 1000000000 | bytes 1000000 | tf_op jit(solution)/shard_map/pallas_call | solution.py:894
  873.2 27.1 %shard_map.328 = (f32[4,704,2048]{2,1,0:T(8,128)}, f32[4,704,2048]{2,1,0:T(8,128)}, f32[4,704,2048]{2,1,0:T(8,128)}) custom-call(bf16[4,256,2048]{2,1,0:T(8,128)(2,1)} %get-tuple-element.546.rows_ref.refs_0_, bf16[4,256,2048]{2,1,0:T(8,128)(2,1)} %get-tuple-element.431.rows_ref.refs_1_, ...), custom_call_target="tpu_custom_call", output_to_operand_aliasing={{0}: (20, {}), {1}: (21, {}), {2}: (22, {})} | custom-call | flops 1000000000 | bytes 1000000 | tf_op jit(solution)/shard_map/pallas_call | solution.py:894
  932.6 8.5 collective-permute-done.86
  959.0 28.7 %shard_map.330 = (bf16[512,1536]{1,0:T(8,128)(2,1)}, bf16[512,2048]{1,0:T(8,128)(2,1)}, f32[512,128]{1,0:T(8,128)S(1)}, f32[512,512]{1,0:T(8,128)}, bf16[512,2048]{1,0:T(8,128)(2,1)}) custom-call(bf16[512,2048]{1,0:T(8,128)(2,1)} %copy-done.19, bf16[512,1536]{1,0:T(8,128)(2,1)} %copy-done.74, bf16[512,2048]{1,0:T(8,128)(2,1)} %copy-done.68, ...), custom_call_target="tpu_custom_call" | custom-call | flops 1000000000 | bytes 1000000 | tf_op jit(solution)/shard_map/pallas_call | solution.py:1112
  1043.1 8.0 collective-permute-done.95
  1063.2 10.8 shard_map.335
  1095.7 8.0 collective-permute-done.98
  1133.1 11.6 collective-permute-done.109
  1153.5 9.0 collective-permute-done.112
  (827 shorter events, 606.8 us)
Async XLA Ops:
  90.9 42.6 %collective-permute-start.17 = (bf16[512,2048]{1,0:T(8,128)(2,1)}, bf16[512,2048]{1,0:T(8,128)(2,1)}, u32[]{:S(2)}, u32[]{:S(2)}) collective-permute-start(bf16[512,2048]{1,0:T(8,128)(2,1)} %pad_maximum_fusion.8), channel_id=1, source_target_pairs={{0,2},{2,0},{4,6},{6,4},{8,10},{10,8},{12,14},{14,12},{16,18},{18,... | collective-permute-start | bytes 6291464 | tf_op jit(solution)/shard_map/ppermute | solution.py:98
  92.0 41.6 %all-to-all-start = ((bf16[16,3,88,128]{3,2,1,0:T(8,128)(2,1)}), bf16[16,3,88,128]{3,2,1,0:T(8,128)(2,1)}, u32[]{:S(2)}, u32[]{:S(2)}) async-start(bf16[16,3,88,128]{3,2,1,0:T(8,128)(2,1)} %copy.173), calls=%async_computation | async-start | bytes 2162688 | tf_op jit(solution)/shard_map/all_to_all | solution.py:1281
  217.6 39.4 %collective-permute-start.28 = (bf16[672,2048]{1,0:T(8,128)(2,1)}, bf16[672,2048]{1,0:T(8,128)(2,1)}, u32[]{:S(2)}, u32[]{:S(2)}) collective-permute-start(bf16[672,2048]{1,0:T(8,128)(2,1)} %pad_maximum_fusion.7), channel_id=1, source_target_pairs={{0,2},{2,0},{4,6},{6,4},{8,10},{10,8},{12,14},{14,12},{16,18},{18,... | collective-permute-start | bytes 8257544 | tf_op jit(solution)/shard_map/ppermute | solution.py:98
  303.0 38.5 %collective-permute-start.35 = (bf16[864,2048]{1,0:T(8,128)(2,1)}, bf16[864,2048]{1,0:T(8,128)(2,1)}, u32[]{:S(2)}, u32[]{:S(2)}) collective-permute-start(bf16[864,2048]{1,0:T(8,128)(2,1)} %pad_maximum_fusion), channel_id=1, source_target_pairs={{0,2},{2,0},{4,6},{6,4},{8,10},{10,8},{12,14},{14,12},{16,18},{18,... | collective-permute-start | bytes 10616840 | tf_op jit(solution)/shard_map/ppermute | solution.py:98
  345.7 38.5 %collective-permute-start.40 = (bf16[864,2048]{1,0:T(8,128)(2,1)S(1)}, bf16[864,2048]{1,0:T(8,128)(2,1)S(1)}, u32[]{:S(2)}, u32[]{:S(2)}) collective-permute-start(bf16[864,2048]{1,0:T(8,128)(2,1)S(1)} %pad_maximum_fusion.1), channel_id=1, source_target_pairs={{0,2},{2,0},{4,6},{6,4},{8,10},{10,8},{12,14},{14,12},{16,18},{18,... | collective-permute-start | bytes 10616840 | tf_op jit(solution)/shard_map/ppermute | solution.py:98
  396.4 70.8 %collective-permute-start.50 = (bf16[704,2048]{1,0:T(8,128)(2,1)}, bf16[704,2048]{1,0:T(8,128)(2,1)}, u32[]{:S(2)}, u32[]{:S(2)}) collective-permute-start(bf16[704,2048]{1,0:T(8,128)(2,1)} %pad_maximum_fusion.6), channel_id=1, source_target_pairs={{0,2},{2,0},{4,6},{6,4},{8,10},{10,8},{12,14},{14,12},{16,18},{18,... | collective-permute-start | bytes 8650760 | tf_op jit(solution)/shard_map/ppermute | solution.py:98
  429.2 49.3 %collective-permute-start.49 = (bf16[704,2048]{1,0:T(8,128)(2,1)}, bf16[704,2048]{1,0:T(8,128)(2,1)}, u32[]{:S(2)}, u32[]{:S(2)}) collective-permute-start(bf16[704,2048]{1,0:T(8,128)(2,1)} %pad_maximum_fusion.5), channel_id=1, source_target_pairs={{0,2},{2,0},{4,6},{6,4},{8,10},{10,8},{12,14},{14,12},{16,18},{18,... | collective-permute-start | bytes 8650760 | tf_op jit(solution)/shard_map/ppermute | solution.py:98
  433.2 45.4 %collective-permute-start.47 = (bf16[480,2048]{1,0:T(8,128)(2,1)}, bf16[480,2048]{1,0:T(8,128)(2,1)S(1)}, u32[]{:S(2)}, u32[]{:S(2)}) collective-permute-start(bf16[480,2048]{1,0:T(8,128)(2,1)} %pad_maximum_fusion.9), channel_id=1, source_target_pairs={{0,1},{1,0},{2,3},{3,2},{4,5},{5,4},{6,7},{7,6},{8,9},{9,8},{10,11... | collective-permute-start | bytes 5898248 | tf_op jit(solution)/shard_map/ppermute | solution.py:94
  478.6 52.0 %collective-permute-start.52 = (bf16[2,512,2048]{2,1,0:T(8,128)(2,1)}, bf16[2,512,2048]{2,1,0:T(8,128)(2,1)}, u32[]{:S(2)}, u32[]{:S(2)}) collective-permute-start(bf16[2,512,2048]{2,1,0:T(8,128)(2,1)} %get-tuple-element.459), channel_id=1, source_target_pairs={{0,2},{2,0},{4,6},{6,4},{8,10},{10,8},{12,14},{14,12},{16,18},{18,... | collective-permute-start | bytes 12582920 | tf_op jit(solution)/shard_map/ppermute | solution.py:98
  482.4 48.3 %collective-permute-start.54 = (bf16[864,2048]{1,0:T(8,128)(2,1)}, bf16[864,2048]{1,0:T(8,128)(2,1)}, u32[]{:S(2)}, u32[]{:S(2)}) collective-permute-start(bf16[864,2048]{1,0:T(8,128)(2,1)} %pad_maximum_fusion.3), channel_id=1, source_target_pairs={{0,2},{2,0},{4,6},{6,4},{8,10},{10,8},{12,14},{14,12},{16,18},{18,... | collective-permute-start | bytes 10616840 | tf_op jit(solution)/shard_map/ppermute | solution.py:98
  486.4 44.2 %collective-permute-start.53 = (bf16[320,2048]{1,0:T(8,128)(2,1)}, bf16[320,2048]{1,0:T(8,128)(2,1)}, u32[]{:S(2)}, u32[]{:S(2)}) collective-permute-start(bf16[320,2048]{1,0:T(8,128)(2,1)} %pad_maximum_fusion.25), channel_id=1, source_target_pairs={{0,1},{1,0},{2,3},{3,2},{4,5},{5,4},{6,7},{7,6},{8,9},{9,8},{10,11... | collective-permute-start | bytes 3932168 | tf_op jit(solution)/shard_map/ppermute | solution.py:94
  572.5 49.6 %collective-permute-start.58 = (bf16[2,512,2048]{2,1,0:T(8,128)(2,1)}, bf16[2,512,2048]{2,1,0:T(8,128)(2,1)}, u32[]{:S(2)}, u32[]{:S(2)}) collective-permute-start(bf16[2,512,2048]{2,1,0:T(8,128)(2,1)} %get-tuple-element.495), channel_id=1, source_target_pairs={{0,2},{2,0},{4,6},{6,4},{8,10},{10,8},{12,14},{14,12},{16,18},{18,... | collective-permute-start | bytes 12582920 | tf_op jit(solution)/shard_map/ppermute | solution.py:98
  579.0 43.1 %collective-permute-start.59 = (bf16[352,2048]{1,0:T(8,128)(2,1)}, bf16[352,2048]{1,0:T(8,128)(2,1)}, u32[]{:S(2)}, u32[]{:S(2)}) collective-permute-start(bf16[352,2048]{1,0:T(8,128)(2,1)} %pad_maximum_fusion.13), channel_id=1, source_target_pairs={{0,4},{2,6},{4,0},{6,2},{8,12},{10,14},{12,8},{14,10},{16,20},{18,... | collective-permute-start | bytes 4325384 | tf_op jit(solution)/shard_map/ppermute | solution.py:98
  637.9 43.7 %collective-permute-start.64 = (bf16[2,512,2048]{2,1,0:T(8,128)(2,1)}, bf16[2,512,2048]{2,1,0:T(8,128)(2,1)}, u32[]{:S(2)}, u32[]{:S(2)}) collective-permute-start(bf16[2,512,2048]{2,1,0:T(8,128)(2,1)} %shard_map.315), channel_id=1, source_target_pairs={{0,2},{2,0},{4,6},{6,4},{8,10},{10,8},{12,14},{14,12},{16,18},{18,... | collective-permute-start | bytes 12582920 | tf_op jit(solution)/shard_map/ppermute | solution.py:98
  643.2 38.4 %collective-permute-start.65 = (bf16[352,2048]{1,0:T(8,128)(2,1)}, bf16[352,2048]{1,0:T(8,128)(2,1)}, u32[]{:S(2)}, u32[]{:S(2)}) collective-permute-start(bf16[352,2048]{1,0:T(8,128)(2,1)} %pad_maximum_fusion.14), channel_id=1, source_target_pairs={{0,4},{2,6},{4,0},{6,2},{8,12},{10,14},{12,8},{14,10},{16,20},{18,... | collective-permute-start | bytes 4325384 | tf_op jit(solution)/shard_map/ppermute | solution.py:98
  645.8 70.0 %collective-permute-start.66 = (bf16[160,2048]{1,0:T(8,128)(2,1)}, bf16[160,2048]{1,0:T(8,128)(2,1)S(1)}, u32[]{:S(2)}, u32[]{:S(2)}) collective-permute-start(bf16[160,2048]{1,0:T(8,128)(2,1)} %get-tuple-element.860), channel_id=1, source_target_pairs={{0,2},{2,0},{4,6},{6,4},{8,10},{10,8},{12,14},{14,12},{16,18},{18,... | collective-permute-start | bytes 1966088 | tf_op jit(solution)/shard_map/ppermute | solution.py:98
  687.5 51.5 %collective-permute-start.67 = (bf16[2,512,2048]{2,1,0:T(8,128)(2,1)}, bf16[2,512,2048]{2,1,0:T(8,128)(2,1)}, u32[]{:S(2)}, u32[]{:S(2)}) collective-permute-start(bf16[2,512,2048]{2,1,0:T(8,128)(2,1)} %get-tuple-element.542), channel_id=1, source_target_pairs={{0,2},{2,0},{4,6},{6,4},{8,10},{10,8},{12,14},{14,12},{16,18},{18,... | collective-permute-start | bytes 12582920 | tf_op jit(solution)/shard_map/ppermute | solution.py:98
  691.5 47.6 %collective-permute-start.69 = (bf16[2,160,2048]{2,1,0:T(8,128)(2,1)}, bf16[2,160,2048]{2,1,0:T(8,128)(2,1)}, u32[]{:S(2)}, u32[]{:S(2)}) collective-permute-start(bf16[2,160,2048]{2,1,0:T(8,128)(2,1)} %get-tuple-element.532), channel_id=1, source_target_pairs={{0,1},{1,0},{2,3},{3,2},{4,5},{5,4},{6,7},{7,6},{8,9},{9,8},{10,11... | collective-permute-start | bytes 3932168 | tf_op jit(solution)/shard_map/ppermute | solution.py:94
  696.7 42.4 %collective-permute-start.68 = (bf16[352,2048]{1,0:T(8,128)(2,1)}, bf16[352,2048]{1,0:T(8,128)(2,1)}, u32[]{:S(2)}, u32[]{:S(2)}) collective-permute-start(bf16[352,2048]{1,0:T(8,128)(2,1)} %pad_maximum_fusion.15), channel_id=1, source_target_pairs={{0,4},{2,6},{4,0},{6,2},{8,12},{10,14},{12,8},{14,10},{16,20},{18,... | collective-permute-start | bytes 4325384 | tf_op jit(solution)/shard_map/ppermute | solution.py:98
  697.1 42.0 %collective-permute-start.70 = (bf16[352,2048]{1,0:T(8,128)(2,1)}, bf16[352,2048]{1,0:T(8,128)(2,1)}, u32[]{:S(2)}, u32[]{:S(2)}) collective-permute-start(bf16[352,2048]{1,0:T(8,128)(2,1)} %maximum_add_fusion.4), channel_id=1, source_target_pairs={{0,8},{2,10},{4,12},{6,14},{8,16},{10,18},{12,20},{14,22},{16,24},... | collective-permute-start | bytes 4325384 | tf_op jit(solution)/shard_map/ppermute | solution.py:102
  749.5 40.0 %collective-permute-start.73 = (bf16[2,512,2048]{2,1,0:T(8,128)(2,1)}, bf16[2,512,2048]{2,1,0:T(8,128)(2,1)}, u32[]{:S(2)}, u32[]{:S(2)}) collective-permute-start(bf16[2,512,2048]{2,1,0:T(8,128)(2,1)} %shard_map.323), channel_id=1, source_target_pairs={{0,2},{2,0},{4,6},{6,4},{8,10},{10,8},{12,14},{14,12},{16,18},{18,... | collective-permute-start | bytes 12582920 | tf_op jit(solution)/shard_map/ppermute | solution.py:98
  751.1 38.3 %collective-permute-start.74 = (bf16[352,2048]{1,0:T(8,128)(2,1)S(1)}, bf16[352,2048]{1,0:T(8,128)(2,1)}, u32[]{:S(2)}, u32[]{:S(2)}) collective-permute-start(bf16[352,2048]{1,0:T(8,128)(2,1)S(1)} %pad_maximum_fusion.16), channel_id=1, source_target_pairs={{0,4},{2,6},{4,0},{6,2},{8,12},{10,14},{12,8},{14,10},{16,20},{18,... | collective-permute-start | bytes 4325384 | tf_op jit(solution)/shard_map/ppermute | solution.py:98
  789.4 50.3 %collective-permute-start.75 = (bf16[2,512,2048]{2,1,0:T(8,128)(2,1)}, bf16[2,512,2048]{2,1,0:T(8,128)(2,1)}, u32[]{:S(2)}, u32[]{:S(2)}) collective-permute-start(bf16[2,512,2048]{2,1,0:T(8,128)(2,1)} %get-tuple-element.588), channel_id=1, source_target_pairs={{0,2},{2,0},{4,6},{6,4},{8,10},{10,8},{12,14},{14,12},{16,18},{18,... | collective-permute-start | bytes 12582920 | tf_op jit(solution)/shard_map/ppermute | solution.py:98
  800.7 38.7 %collective-permute-start.78 = (bf16[352,2048]{1,0:T(8,128)(2,1)}, bf16[352,2048]{1,0:T(8,128)(2,1)}, u32[]{:S(2)}, u32[]{:S(2)}) collective-permute-start(bf16[352,2048]{1,0:T(8,128)(2,1)} %fusion.9), channel_id=1, source_target_pairs={{0,8},{2,10},{4,12},{6,14},{8,16},{10,18},{12,20},{14,22},{16,24},... | collective-permute-start | bytes 4325384 | tf_op jit(solution)/shard_map/ppermute | solution.py:102
  849.9 50.7 %collective-permute-start.81 = (bf16[2,512,2048]{2,1,0:T(8,128)(2,1)}, bf16[2,512,2048]{2,1,0:T(8,128)(2,1)}, u32[]{:S(2)}, u32[]{:S(2)}) collective-permute-start(bf16[2,512,2048]{2,1,0:T(8,128)(2,1)} %shard_map.327), channel_id=1, source_target_pairs={{0,2},{2,0},{4,6},{6,4},{8,10},{10,8},{12,14},{14,12},{16,18},{18,... | collective-permute-start | bytes 12582920 | tf_op jit(solution)/shard_map/ppermute | solution.py:98
  856.8 43.8 %collective-permute-start.79 = (bf16[352,2048]{1,0:T(8,128)(2,1)}, bf16[352,2048]{1,0:T(8,128)(2,1)}, u32[]{:S(2)}, u32[]{:S(2)}) collective-permute-start(bf16[352,2048]{1,0:T(8,128)(2,1)} %fusion.10), channel_id=1, source_target_pairs={{0,8},{2,10},{4,12},{6,14},{8,16},{10,18},{12,20},{14,22},{16,24},... | collective-permute-start | bytes 4325384 | tf_op jit(solution)/shard_map/ppermute | solution.py:102
  860.8 39.7 %collective-permute-start.82 = (bf16[192,2048]{1,0:T(8,128)(2,1)}, bf16[192,2048]{1,0:T(8,128)(2,1)}, u32[]{:S(2)}, u32[]{:S(2)}) collective-permute-start(bf16[192,2048]{1,0:T(8,128)(2,1)} %slice_bitcast_fusion.5), channel_id=1, source_target_pairs={{0,4},{2,6},{4,0},{6,2},{8,12},{10,14},{12,8},{14,10},{16,20},{18,... | collective-permute-start | bytes 2359304 | tf_op jit(solution)/shard_map/ppermute | solution.py:98
  862.2 38.3 %collective-permute-start.80 = (bf16[2,160,2048]{2,1,0:T(8,128)(2,1)}, bf16[2,160,2048]{2,1,0:T(8,128)(2,1)}, u32[]{:S(2)}, u32[]{:S(2)}) collective-permute-start(bf16[2,160,2048]{2,1,0:T(8,128)(2,1)} %get-tuple-element.615), channel_id=1, source_target_pairs={{0,1},{1,0},{2,3},{3,2},{4,5},{5,4},{6,7},{7,6},{8,9},{9,8},{10,11... | collective-permute-start | bytes 3932168 | tf_op jit(solution)/shard_map/ppermute | solution.py:94
  924.4 70.3 %collective-permute-start.88 = (bf16[2,160,2048]{2,1,0:T(8,128)(2,1)}, bf16[2,160,2048]{2,1,0:T(8,128)(2,1)}, u32[]{:S(2)}, u32[]{:S(2)}) collective-permute-start(bf16[2,160,2048]{2,1,0:T(8,128)(2,1)} %get-tuple-element.645), channel_id=1, source_target_pairs={{0,1},{1,0},{2,3},{3,2},{4,5},{5,4},{6,7},{7,6},{8,9},{9,8},{10,11... | collective-permute-start | bytes 3932168 | tf_op jit(solution)/shard_map/ppermute | solution.py:94
  926.4 68.3 %all-to-all-start.2 = ((bf16[16,3,88,128]{3,2,1,0:T(8,128)(2,1)}), bf16[16,3,88,128]{3,2,1,0:T(8,128)(2,1)}, u32[]{:S(2)}, u32[]{:S(2)}) async-start(bf16[16,3,88,128]{3,2,1,0:T(8,128)(2,1)} %copy.188), calls=%async_computation.2 | async-start | bytes 2162688 | tf_op jit(solution)/shard_map/all_to_all | solution.py:1697
  1094.2 38.9 %collective-permute-start.106 = (bf16[128,2688]{1,0:T(8,128)(2,1)}, bf16[128,2688]{1,0:T(8,128)(2,1)S(1)}, u32[]{:S(2)}, u32[]{:S(2)}) collective-permute-start(bf16[128,2688]{1,0:T(8,128)(2,1)} %get-tuple-element.814), channel_id=1, source_target_pairs={{0,4},{2,6},{4,0},{6,2},{8,12},{10,14},{12,8},{14,10},{16,20},{18,... | collective-permute-start | bytes 2064392 | tf_op jit(solution)/shard_map/ppermute | solution.py:98
  1115.3 38.1 %collective-permute-start.110 = (bf16[128,2688]{1,0:T(8,128)(2,1)S(1)}, bf16[128,2688]{1,0:T(8,128)(2,1)S(1)}, u32[]{:S(2)}, u32[]{:S(2)}) collective-permute-start(bf16[128,2688]{1,0:T(8,128)(2,1)S(1)} %copy-done.151), channel_id=1, source_target_pairs={{0,4},{2,6},{4,0},{6,2},{8,12},{10,14},{12,8},{14,10},{16,20},{18,... | collective-permute-start | bytes 2064392 | tf_op jit(solution)/shard_map/ppermute | solution.py:98
  (270 other events, 4060.4 us)
